TPU v7x, 32 devices: a whole 2x2x4 slice. The times are simulated.
32 devices in a mesh: gx: 4 (over z), gy: 8 (over y, x, core).
Axes of the slice: x: 2, y: 2, z: 4, core: 2. Of those that a mesh axis runs over, the one named last changes fastest.
Arguments:
- velocity: float32 [3, 32, 64, 128], P(None, 'gx', 'gy'), may hold values from -1 to 1
- wall_cells: int32 [32, 64, 128], P('gx', 'gy'), may hold values 0 or 1
- tile_counts: int32 [4, 8, 8], P('gx', 'gy'), may hold values from 32 to 256, as said below
- helper_tile: int32 [4, 8], P('gx'), may hold values from 0 to 63, as said below
- base_fields: float32 [4, 8, 8, 3, 32, 1024], P('gx', 'gy'), may hold values from -2.5 to 2.5
- extra_fields: float32 [4, 8, 3, 224, 1024], P('gx', 'gy'), may hold values from -6.1 to 6.1
- base_noise: bfloat16 [4, 8, 8, 2, 3, 32, 1024], P('gx', 'gy'), may hold values from -2.5 to 2.5
- extra_noise: bfloat16 [4, 8, 2, 3, 224, 1024], P('gx', 'gy'), may hold values from -2.5 to 2.5
Outputs:
- new_base_fields: float32 [4, 8, 8, 3, 32, 1024], P('gx', 'gy')
- new_extra_fields: float32 [4, 8, 3, 224, 1024], P('gx', 'gy')
- polymer_stress: float32 [4, 8, 8, 6, 1024], P('gx', 'gy')
Inputs may be any that keep to these rules, and one draw needn't show every extreme that they name: `tile_counts`: each entry is 32 or 256. In each row of tiles exactly 8 tiles have 256, these are the tiles that helper_tile names, one column of tiles holds at most 4 of them and in every row some column holds exactly 4. `helper_tile`: entry [i, h] = o * 8 + t names tile t of column o in row i; the entries of a row are distinct and name exactly the row's tiles with 256 fields.
All inputs are finite; a program needn't handle non-finite values. No bound on the sum of `wall_cells` on one device may be relied on, other than what follows from the above.
Results may differ from a plain program's by a relative error of at most 0.0003.
Values sent between devices are 32-bit elements; how exact they have to be, the bound alone decides.
No kernel may reach another device: no remote copies, remote signals or barrier semaphores. Data moves between devices by JAX's collectives and lax.ppermute only.
A program may use at most 128 MiB of HBM per device.

v0:
```python
import functools

import jax
import jax.numpy as jnp
from jax import lax
from jax.experimental import pallas as pl
from jax.experimental.pallas import tpu as pltpu
from jax.sharding import PartitionSpec as P

ALL_FIELDS = 256
HEAVY_MOST = 4
LANES = 128
SUB = 8
LARGE = 16 << 20

time_step = 0.05
weissenberg = 0.25
max_extension = 50.0
noise_scale = (time_step / weissenberg) ** 0.5
component_pairs = ((0, 0), (1, 1), (2, 2), (0, 1), (0, 2), (1, 2))
moment_of = {(0, 0): 0, (1, 1): 1, (2, 2): 2, (0, 1): 3, (1, 0): 3, (0, 2): 4, (2, 0): 4, (1, 2): 5, (2, 1): 5}
f32 = jnp.float32

smem = pl.BlockSpec(memory_space=pltpu.SMEM)
vmem = pl.BlockSpec(memory_space=pltpu.VMEM)
hbm = pl.BlockSpec(memory_space=pltpu.HBM)


def far_memory(*arrays):
    return [pltpu.with_memory_space_constraint(array, pltpu.HBM) for array in arrays]


def column_sum(value):
    return jnp.sum(value, axis=0, keepdims=True)


def wide(row):
    return jnp.broadcast_to(row, (SUB, LANES))


def turned(value, cell_z):
    sub = lax.broadcasted_iota(jnp.int32, value.shape, 0)
    group = lax.broadcasted_iota(jnp.int32, value.shape, 1) // cell_z
    skewed = pltpu.roll(value, cell_z, 1, stride=cell_z, stride_axis=0)
    mixed = jnp.take_along_axis(skewed, (group + sub) & (SUB - 1), axis=0, mode="promise_in_bounds")
    return pltpu.roll(mixed, 0, 1, stride=cell_z, stride_axis=0)


def relax_of(total, inverse):
    factor = 1.0 / (1.0 - total * inverse / max_extension)
    return 1.0 - (time_step * 0.5 / weissenberg) * factor


def stepped(vectors, noise, matrix):
    return [
        matrix[3 * a] * vectors[0]
        + matrix[3 * a + 1] * vectors[1]
        + matrix[3 * a + 2] * vectors[2]
        + noise_scale * noise[a]
        for a in range(3)
    ]


def with_diagonal(grad, relax):
    return [g + relax if i % 4 == 0 else g for i, g in enumerate(grad)]


def noise_rows(ref, start):
    both = [ref(a, pl.ds(start, 2 * SUB)).astype(f32) for a in range(3)]
    return [[w[:SUB] for w in both], [w[SUB:] for w in both]]


def add_moments(sums, q):
    return [s + q[a] * q[b] for s, (a, b) in zip(sums, component_pairs)]


def owned_slots(tiles, me, helper):
    rank = jnp.int32(0)
    found = []
    for h in range(helper.shape[1]):
        tile = helper[0, h] - me * tiles
        owned = (tile >= 0) & (tile < tiles)
        found.append((h, owned, tile, rank))
        rank = rank + owned.astype(jnp.int32)
    return found


def small(flops, traffic):
    return pl.CostEstimate(flops=flops, bytes_accessed=traffic, transcendentals=0)


def edges(velocity, x_last, x_first, y_last, y_first):
    depth, width = velocity.shape[1:3]
    for a in range(3):
        x_last[a] = velocity[a, depth - 1]
        x_first[a] = velocity[a, 0]
        for x in range(depth):
            y_last[a, pl.ds(x, 1), :] = velocity[a, x, pl.ds(width - 1, 1), :]
            y_first[a, pl.ds(x, 1), :] = velocity[a, x, pl.ds(0, 1), :]


def call_edges(velocity):
    _, depth, width, length = velocity.shape
    along_x = jax.ShapeDtypeStruct((3, width, length), f32)
    along_y = jax.ShapeDtypeStruct((3, depth, length), f32)
    return pl.pallas_call(
        edges,
        out_shape=(along_x, along_x, along_y, along_y),
        in_specs=[vmem],
        out_specs=(vmem,) * 4,
        compiler_params=pltpu.CompilerParams(vmem_limit_bytes=4 << 20),
        cost_estimate=small(1 << 10, 1 << 17),
        name="edges",
    )(velocity)


def heavy_moments(helper, base, noise, out, fields, shocks, sems):
    tiles = base.shape[2]
    me = lax.axis_index("gy")
    groups = fields.shape[2] // (2 * SUB)

    def copies(tile, rank):
        return (
            pltpu.make_async_copy(base.at[0, 0, tile], fields.at[rank], sems.at[0, rank]),
            pltpu.make_async_copy(noise.at[0, 0, tile, 0], shocks.at[rank, 0], sems.at[1, rank]),
        )

    def later(tile, rank):
        return pltpu.make_async_copy(noise.at[0, 0, tile, 1], shocks.at[rank, 1], sems.at[2, rank])

    found = owned_slots(tiles, me, helper)
    for _, owned, tile, rank in found:

        @pl.when(owned)
        def _(tile=tile, rank=rank):
            for copy in copies(tile, rank):
                copy.start()
            later(tile, rank).start()

    for h, owned, tile, rank in found:

        @pl.when(owned)
        def _(h=h, tile=tile, rank=rank):
            for copy in copies(tile, rank):
                copy.wait()

            @pl.loop(0, fields.shape[3] // LANES)
            def _(x):
                lanes = pl.ds(pl.multiple_of(x * LANES, LANES), LANES)
                sums = [jnp.zeros((SUB, LANES), f32)] * 16
                for group in range(groups):
                    pair = noise_rows(lambda a, rows: shocks[rank, 0, a, rows, lanes], group * 2 * SUB)
                    for half in range(2):
                        rows = pl.ds((2 * group + half) * SUB, SUB)
                        q = [fields[rank, a, rows, lanes] for a in range(3)]
                        w = pair[half]
                        terms = [q[a] * q[b] for a, b in component_pairs]
                        terms += [q[a] * w[b] for a in range(3) for b in range(3)]
                        terms += [w[0] * w[0] + w[1] * w[1] + w[2] * w[2]]
                        sums = [s + t for s, t in zip(sums, terms)]
                for i, s in enumerate(sums):
                    out[h, i, pl.ds(x, 1), :] = column_sum(s)

    for _, owned, tile, rank in found:

        @pl.when(owned)
        def _(tile=tile, rank=rank):
            later(tile, rank).wait()


def call_heavy_moments(helper_tile, base_fields, base_noise):
    slots = helper_tile.shape[1]
    _, _, _, _, count, cells = base_fields.shape
    steps = base_noise.shape[3]
    return pl.pallas_call(
        heavy_moments,
        out_shape=(
            jax.ShapeDtypeStruct((slots, 16, cells // LANES, LANES), f32),
            jax.ShapeDtypeStruct((HEAVY_MOST, 3, count, cells), f32),
            jax.ShapeDtypeStruct((HEAVY_MOST, steps, 3, count, cells), jnp.bfloat16),
        ),
        in_specs=[smem, hbm, hbm],
        out_specs=(vmem, vmem, vmem),
        scratch_shapes=[pltpu.SemaphoreType.DMA((3, HEAVY_MOST))],
        compiler_params=pltpu.CompilerParams(vmem_limit_bytes=LARGE),
        cost_estimate=small(8 << 20, 3 << 20),
        name="heavy_moments",
    )(helper_tile, *far_memory(base_fields, base_noise))


def gradients(tiles, helper, velocity, x_low, x_high, y_low, y_high, wall, moments, grad, keep, send):
    me = lax.axis_index("gy")
    depth = velocity.shape[1]
    cell_z = velocity.shape[3] // tiles
    sub = lax.broadcasted_iota(jnp.int32, (SUB, LANES), 0)
    lane = lax.broadcasted_iota(jnp.int32, (SUB, LANES), 1)
    z = lane % cell_z
    scales = [turned(jnp.where(wall[x] == 0, 0.5 * time_step, 0.0).astype(f32), cell_z) for x in range(depth)]
    for a in range(3):
        rows = [x_low[a]] + [velocity[a, x] for x in range(depth)] + [x_high[a]]
        rows = [turned(row, cell_z) for row in rows]
        low, high = turned(y_low[a], cell_z), turned(y_high[a], cell_z)
        for x in range(depth):
            here = rows[x + 1]
            above = high if x == depth - 1 else pltpu.roll(high, LANES - cell_z * (x + 1), 1)
            below = low if x == 0 else pltpu.roll(low, LANES - cell_z * x, 1)
            y_up = jnp.where(lane < LANES - cell_z, pltpu.roll(here, LANES - cell_z, 1), above)
            y_down = jnp.where(lane >= cell_z, pltpu.roll(here, cell_z, 1), below)
            next_tile = pltpu.roll(pltpu.roll(here, cell_z - 1, 1), 1, 0)
            last_tile = pltpu.roll(pltpu.roll(here, LANES - cell_z + 1, 1), SUB - 1, 0)
            next_tile = jnp.where(sub == 0, 0.0, next_tile)
            last_tile = jnp.where(sub == SUB - 1, 0.0, last_tile)
            z_up = jnp.where(z == cell_z - 1, next_tile, pltpu.roll(here, LANES - 1, 1))
            z_down = jnp.where(z == 0, last_tile, pltpu.roll(here, 1, 1))
            for b, difference in enumerate((rows[x + 2] - rows[x], y_up - y_down, z_up - z_down)):
                grad[pl.ds(((3 * a + b) * depth + x) * SUB, SUB), :] = difference * scales[x]
    for h, owned, tile, _ in owned_slots(tiles, me, helper):

        @pl.when(owned)
        def _(h=h, tile=tile):
            g = [grad[pl.ds(i * depth * SUB + SUB - 1 - tile, depth, stride=SUB), :] for i in range(9)]
            m = [moments[h, i] for i in range(16)]
            cross = lambda a, b: m[6 + 3 * a + b]
            square = lambda a, b: m[moment_of[a, b]]
            once, twice, kick = 0.0, 0.0, 0.0
            for a in range(3):
                for b in range(3):
                    once += g[3 * a + b] * square(a, b)
                    kick += g[3 * a + b] * cross(b, a)
                    inner = 0.0
                    for c in range(3):
                        inner += g[3 * a + c] * square(b, c)
                    twice += g[3 * a + b] * inner
            rows = g + [
                twice + (2 * noise_scale) * kick + noise_scale**2 * m[15],
                2.0 * once + (2 * noise_scale) * (cross(0, 0) + cross(1, 1) + cross(2, 2)),
                m[0] + m[1] + m[2],
            ]
            stays = (me & 1) == (h & 1)

            @pl.when(stays)
            def _():
                for i, row in enumerate(rows):
                    keep[h >> 1, i] = row

            @pl.when(jnp.logical_not(stays))
            def _():
                for i, row in enumerate(rows):
                    send[h >> 1, i] = row


def call_gradients(tiles, helper_tile, velocity, halos, wall_cells, moments):
    slots = helper_tile.shape[1]
    depth = velocity.shape[1]
    half = jax.ShapeDtypeStruct((slots // 2, 12, depth, LANES), f32)
    return pl.pallas_call(
        functools.partial(gradients, tiles),
        out_shape=(jax.ShapeDtypeStruct((9 * depth * SUB, LANES), f32), half, half),
        in_specs=[smem] + [vmem] * 7,
        out_specs=(vmem,) * 3,
        compiler_params=pltpu.CompilerParams(vmem_limit_bytes=8 << 20),
        cost_estimate=small(4 << 20, 1 << 20),
        name="gradients",
    )(helper_tile, velocity, *halos, wall_cells, moments)


def swapped(block, bit):
    size = lax.axis_size("gy")
    return lax.ppermute(block, "gy", [(i, i ^ (1 << bit)) for i in range(size)])


def arrived(tiles, me, helper, slot, bit):
    owner = helper[0, slot] // tiles
    return (((owner ^ me) >> bit) & 1) == 1


def merge(tiles, bit, helper, kept, received, keep, send):
    me = lax.axis_index("gy")
    below = me & ((2 << bit) - 1)
    mine = (me >> (bit + 1)) & 1
    for j in range(kept.shape[0]):
        pick = arrived(tiles, me, helper, (j << (bit + 1)) | below, bit)
        stays = mine == (j & 1)
        for source, chosen in ((received, pick), (kept, jnp.logical_not(pick))):
            for out, there in ((keep, stays), (send, jnp.logical_not(stays))):

                @pl.when(chosen & there)
                def _(j=j, source=source, out=out):
                    for i in range(kept.shape[1]):
                        out[j >> 1, i] = source[j, i]


def call_merge(tiles, bit, helper_tile, kept, received):
    half = jax.ShapeDtypeStruct((kept.shape[0] // 2,) + kept.shape[1:], f32)
    return pl.pallas_call(
        functools.partial(merge, tiles, bit),
        out_shape=(half, half),
        in_specs=[smem, vmem, vmem],
        out_specs=(vmem, vmem),
        compiler_params=pltpu.CompilerParams(vmem_limit_bytes=4 << 20),
        cost_estimate=small(1 << 10, 1 << 18),
        name="merge",
    )(helper_tile, kept, received)


def call_join(first, second):
    def join(first, second, out):
        out[: first.shape[0]] = first[...]
        out[first.shape[0] :] = second[...]

    return pl.pallas_call(
        join,
        out_shape=jax.ShapeDtypeStruct((2 * first.shape[0],) + first.shape[1:], f32),
        in_specs=[vmem, vmem],
        out_specs=vmem,
        compiler_params=pltpu.CompilerParams(vmem_limit_bytes=4 << 20),
        cost_estimate=small(1 << 10, 1 << 18),
        name="join",
    )(first, second)


def stress_rows(sums, inverse):
    second = [s * inverse for s in sums]
    stretch = 1.0 / (1.0 - (second[0] + second[1] + second[2]) / max_extension)
    return [(stretch * s - (1.0 if i < 3 else 0.0)) * (1.0 / weissenberg) for i, s in enumerate(second)]


def tile_grad(grad, depth, tile, x):
    return [wide(grad[pl.ds((i * depth + x + 1) * SUB - 1 - tile, 1), :]) for i in range(9)]


def ordinary(counts, base, noise, grad, new_base, stress, fields, shocks, totals, relaxes, sems):
    tiles, _, count, cells = fields.shape
    depth = cells // LANES
    groups = count // (2 * SUB)

    def loads(tile):
        return (
            pltpu.make_async_copy(base.at[0, 0, tile], fields.at[tile], sems.at[0, tile]),
            pltpu.make_async_copy(noise.at[0, 0, tile], shocks.at[tile], sems.at[1, tile]),
        )

    def store(tile):
        return pltpu.make_async_copy(fields.at[tile], new_base.at[0, 0, tile], sems.at[0, tile])

    for tile in range(tiles):

        @pl.when(counts[0, 0, tile] != ALL_FIELDS)
        def _(tile=tile):
            for copy in loads(tile):
                copy.start()

    @pl.loop(0, tiles)
    def _(tile):
        tile_count = counts[0, 0, tile]

        @pl.when(tile_count != ALL_FIELDS)
        def _():
            for copy in loads(tile):
                copy.wait()
            inverse = 1.0 / jnp.full((1, LANES), tile_count.astype(f32))
            for x in range(depth):
                lanes = pl.ds(x * LANES, LANES)
                total = jnp.zeros((SUB, LANES), f32)
                for group in range(2 * groups):
                    for a in range(3):
                        q = fields[tile, a, pl.ds(group * SUB, SUB), lanes]
                        total = total + q * q
                totals[pl.ds(x, 1), :] = column_sum(total)
            for step in range(2):
                relaxes[...] = relax_of(totals[...], inverse)
                for x in range(depth):
                    lanes = pl.ds(x * LANES, LANES)
                    matrix = with_diagonal(tile_grad(grad, depth, tile, x), wide(relaxes[pl.ds(x, 1), :]))
                    sums = [jnp.zeros((SUB, LANES), f32)] * (1 if step == 0 else 6)
                    for group in range(groups):
                        pair = noise_rows(lambda a, rows: shocks[tile, step, a, rows, lanes], group * 2 * SUB)
                        for half in range(2):
                            rows = pl.ds((2 * group + half) * SUB, SUB)
                            q = stepped([fields[tile, a, rows, lanes] for a in range(3)], pair[half], matrix)
                            for a in range(3):
                                fields[tile, a, rows, lanes] = q[a]
                            if step == 0:
                                sums[0] = sums[0] + (q[0] * q[0] + q[1] * q[1] + q[2] * q[2])
                            else:
                                sums = add_moments(sums, q)
                    if step == 0:
                        totals[pl.ds(x, 1), :] = column_sum(sums[0])
                    else:
                        for i, row in enumerate(stress_rows([column_sum(s) for s in sums], inverse)):
                            stress[x, i, pl.ds(tile, 1), :] = row
            store(tile).start()

    for tile in range(tiles):

        @pl.when(counts[0, 0, tile] != ALL_FIELDS)
        def _(tile=tile):
            store(tile).wait()


def call_ordinary(tile_counts, base_fields, base_noise, grad):
    _, _, tiles, _, count, cells = base_fields.shape
    steps = base_noise.shape[3]
    depth = cells // LANES
    return pl.pallas_call(
        ordinary,
        out_shape=(
            jax.ShapeDtypeStruct(base_fields.shape, f32),
            jax.ShapeDtypeStruct((depth, 6, tiles, LANES), f32),
        ),
        in_specs=[smem, hbm, hbm, vmem],
        out_specs=(hbm, vmem),
        scratch_shapes=[
            pltpu.VMEM((tiles, 3, count, cells), f32),
            pltpu.VMEM((tiles, steps, 3, count, cells), jnp.bfloat16),
            pltpu.VMEM((depth, LANES), f32),
            pltpu.VMEM((depth, LANES), f32),
            pltpu.SemaphoreType.DMA((2, tiles)),
        ],
        compiler_params=pltpu.CompilerParams(vmem_limit_bytes=LARGE),
        cost_estimate=small(32 << 20, 10 << 20),
        name="ordinary_tiles",
    )(tile_counts, *far_memory(base_fields, base_noise), grad)


def extra(tiles, bit, rows_each, helper, base, noise, kept, received, new_fields, reply, fields, shocks, message, sems):
    me = lax.axis_index("gy")
    steps, _, count, cells = shocks.shape
    depth = cells // LANES
    pieces = count // rows_each
    groups = count // (2 * SUB)
    inverse = 1.0 / float(ALL_FIELDS)

    def field_load(r):
        rows = pl.ds(r * rows_each, rows_each)
        return pltpu.make_async_copy(base.at[0, 0, :, rows], fields.at[:, rows], sems.at[r])

    def noise_load(step):
        return pltpu.make_async_copy(noise.at[0, 0, step], shocks.at[step], sems.at[pieces + step])

    def store(x):
        lanes = pl.ds(x * LANES, LANES)
        return pltpu.make_async_copy(
            fields.at[:, :, lanes], new_fields.at[0, 0, :, :, lanes], sems.at[pieces + steps + x]
        )

    for r in range(pieces):
        field_load(r).start()
    for step in range(steps):
        noise_load(step).start()
    pick = arrived(tiles, me, helper, me, bit)
    for i in range(message.shape[0]):
        message[i] = jnp.where(pick, received[0, i], kept[0, i])

    def squares(r, totals):
        field_load(r).wait()
        totals = list(totals)
        for x in range(depth):
            for group in range(rows_each // SUB):
                rows = pl.ds(pl.multiple_of(r * rows_each + group * SUB, SUB), SUB)
                for a in range(3):
                    q = fields[a, rows, pl.ds(x * LANES, LANES)]
                    totals[x] = totals[x] + q * q
        return totals

    zero = jnp.zeros((SUB, LANES), f32)
    totals = lax.fori_loop(0, pieces, squares, [zero] * depth)
    for x in range(depth):
        reply[0, pl.ds(x, 1), :] = column_sum(totals[x])
    first = relax_of(reply[0] + message[11], inverse)
    reply[0] = first

    for step in range(2):
        noise_load(step).wait()

        @pl.loop(0, depth)
        def _(x):
            lanes = pl.ds(pl.multiple_of(x * LANES, LANES), LANES)
            grad = [wide(message[i, pl.ds(x, 1), :]) for i in range(9)]
            matrix = with_diagonal(grad, wide(reply[step, pl.ds(x, 1), :]))
            sums = [zero] * (1 if step == 0 else 6)
            for group in range(groups):
                pair = noise_rows(lambda a, rows: shocks[step, a, rows, lanes], group * 2 * SUB)
                for half in range(2):
                    rows = pl.ds((2 * group + half) * SUB, SUB)
                    q = stepped([fields[a, rows, lanes] for a in range(3)], pair[half], matrix)
                    for a in range(3):
                        fields[a, rows, lanes] = q[a]
                    if step == 0:
                        sums[0] = sums[0] + (q[0] * q[0] + q[1] * q[1] + q[2] * q[2])
                    else:
                        sums = add_moments(sums, q)
            if step == 0:
                reply[1, pl.ds(x, 1), :] = column_sum(sums[0])
            else:
                for i, s in enumerate(sums):
                    reply[2 + i, pl.ds(x, 1), :] = column_sum(s)
                store(x).start()

        if step == 0:
            total = reply[1] + (message[9] + first * message[10] + first * first * message[11])
            reply[1] = relax_of(total, inverse)

    for x in range(depth):
        store(x).wait()


def call_extra(tiles, bit, helper_tile, extra_fields, extra_noise, kept, received):
    _, _, _, count, cells = extra_fields.shape
    steps = extra_noise.shape[2]
    depth = cells // LANES
    rows_each = 32
    return pl.pallas_call(
        functools.partial(extra, tiles, bit, rows_each),
        out_shape=(
            jax.ShapeDtypeStruct(extra_fields.shape, f32),
            jax.ShapeDtypeStruct((8, depth, LANES), f32),
        ),
        in_specs=[smem, hbm, hbm, vmem, vmem],
        out_specs=(hbm, vmem),
        scratch_shapes=[
            pltpu.VMEM((3, count, cells), f32),
            pltpu.VMEM((steps, 3, count, cells), jnp.bfloat16),
            pltpu.VMEM(kept.shape[1:], f32),
            pltpu.SemaphoreType.DMA((count // rows_each + steps + depth,)),
        ],
        compiler_params=pltpu.CompilerParams(vmem_limit_bytes=LARGE),
        cost_estimate=small(32 << 20, 9 << 20),
        name="extra_fields",
    )(helper_tile, *far_memory(extra_fields, extra_noise), kept, received)


def heavy(bits, helper, base, noise, grad, near, far, old_base, old_stress, new_base, stress, fields, rows, answer, sems):
    slots = helper.shape[1]
    tiles = old_stress.shape[2]
    me = lax.axis_index("gy")
    _, _, count, cells = base.shape
    depth = cells // LANES
    groups = count // (2 * SUB)

    def store(tile, rank):
        return pltpu.make_async_copy(fields.at[rank], new_base.at[0, 0, tile], sems.at[rank])

    rows[...] = old_stress[...]
    found = owned_slots(tiles, me, helper)
    for h, owned, tile, rank in found:

        @pl.when(owned)
        def _(h=h, tile=tile, rank=rank):
            flips = me ^ h
            place = sum(((flips >> (bits - 1 - i)) & 1) << i for i in range(bits))
            is_far = place >= slots // 2
            place = place & (slots // 2 - 1)
            for i in range(near.shape[1]):
                answer[i] = jnp.where(is_far, far[place, i], near[place, i])

            @pl.loop(0, depth)
            def _(x):
                lanes = pl.ds(pl.multiple_of(x * LANES, LANES), LANES)
                g = tile_grad(grad, depth, tile, x)
                matrices = [with_diagonal(g, wide(answer[s, pl.ds(x, 1), :])) for s in range(2)]
                sums = [jnp.zeros((SUB, LANES), f32)] * 6
                for group in range(groups):
                    pairs = [
                        noise_rows(lambda a, r: noise[rank, s, a, r, lanes], group * 2 * SUB) for s in range(2)
                    ]
                    for half in range(2):
                        part = pl.ds((2 * group + half) * SUB, SUB)
                        q = [base[rank, a, part, lanes] for a in range(3)]
                        for s in range(2):
                            q = stepped(q, pairs[s][half], matrices[s])
                        for a in range(3):
                            fields[rank, a, part, lanes] = q[a]
                        sums = add_moments(sums, q)
                sums = [column_sum(s) + answer[2 + i, pl.ds(x, 1), :] for i, s in enumerate(sums)]
                for i, row in enumerate(stress_rows(sums, 1.0 / float(ALL_FIELDS))):
                    rows[x, i, pl.ds(tile, 1), :] = row

            store(tile, rank).start()

    def result(x):
        target = stress.at[0, 0, :, :, pl.ds(x * LANES, LANES)]
        return pltpu.make_async_copy(rows.at[x], target, sems.at[HEAVY_MOST + x])

    for x in range(depth):
        result(x).start()
    for _, owned, tile, rank in found:

        @pl.when(owned)
        def _(tile=tile, rank=rank):
            store(tile, rank).wait()

    for x in range(depth):
        result(x).wait()


def call_heavy(bits, helper_tile, held, held_noise, grad, near, far, new_base, stress):
    depth, _, tiles, _ = stress.shape
    return pl.pallas_call(
        functools.partial(heavy, bits),
        out_shape=(
            jax.ShapeDtypeStruct(new_base.shape, f32),
            jax.ShapeDtypeStruct((1, 1, 6, tiles, depth * LANES), f32),
        ),
        in_specs=[smem, vmem, vmem, vmem, vmem, vmem, hbm, vmem],
        out_specs=(hbm, hbm),
        input_output_aliases={6: 0},
        scratch_shapes=[
            pltpu.VMEM(held.shape, f32),
            pltpu.VMEM(stress.shape, f32),
            pltpu.VMEM(near.shape[1:], f32),
            pltpu.SemaphoreType.DMA((HEAVY_MOST + depth,)),
        ],
        compiler_params=pltpu.CompilerParams(vmem_limit_bytes=LARGE),
        cost_estimate=small(8 << 20, 4 << 20),
        name="heavy_tiles",
    )(helper_tile, held, held_noise, grad, near, far, new_base, stress)


def both_ways(last, first, axis):
    size = lax.axis_size(axis)
    up = [(i, i + 1) for i in range(size - 1)]
    down = [(i + 1, i) for i in range(size - 1)]
    return lax.ppermute(last, axis, up), lax.ppermute(first, axis, down)


def per_device(
    velocity, wall_cells, tile_counts, helper_tile, base_fields, extra_fields, base_noise, extra_noise
):
    tiles = tile_counts.shape[2]
    bits = lax.axis_size("gy").bit_length() - 1
    x_last, x_first, y_last, y_first = call_edges(velocity)
    halos = both_ways(x_last, x_first, "gx") + both_ways(y_last, y_first, "gy")
    moments, held, held_noise = call_heavy_moments(helper_tile, base_fields, base_noise)
    grad, keep, send = call_gradients(tiles, helper_tile, velocity, halos, wall_cells, moments)
    received = swapped(send, 0)
    for bit in range(bits - 1):
        keep, send = call_merge(tiles, bit, helper_tile, keep, received)
        received = swapped(send, bit + 1)
    new_base, stress = call_ordinary(tile_counts, base_fields, base_noise, grad)
    new_extra, reply = call_extra(tiles, bits - 1, helper_tile, extra_fields, extra_noise, keep, received)
    near = reply[None]
    for bit in range(bits - 1, 0, -1):
        near = call_join(near, swapped(near, bit))
    far = swapped(near, 0)
    new_base, stress = call_heavy(bits, helper_tile, held, held_noise, grad, near, far, new_base, stress)
    return new_base, new_extra, jnp.swapaxes(stress, 2, 3)


def solution(mesh):
    in_specs = (
        P(None, "gx", "gy", None),
        P("gx", "gy", None),
        P("gx", "gy", None),
        P("gx", None),
        P("gx", "gy", None, None, None, None),
        P("gx", "gy", None, None, None),
        P("gx", "gy", None, None, None, None, None),
        P("gx", "gy", None, None, None, None),
    )
    out_specs = (
        P("gx", "gy", None, None, None, None),
        P("gx", "gy", None, None, None),
        P("gx", "gy", None, None, None),
    )
    return jax.shard_map(
        per_device, mesh=mesh, in_specs=in_specs, out_specs=out_specs, check_vma=False
    )
```

profile of v0, /device:TPU:15, one launch (start us, length us, event | category | flops | bytes accessed | tf_op | source)
XLA Modules:
  0.0 52.8 jit_solution(12302633687987368213)
XLA Ops:
  0.6 0.0 copy-start
  0.6 0.9 %copy-done = f32[3,8,8,128]{3,2,1,0:T(8,128)S(1)} copy-done((f32[3,8,8,128]{3,2,1,0:T(8,128)S(1)}, f32[3,8,8,128]{3,2,1,0:T(8,128)}, u32[]{:S(2)}) %copy-start) | copy-done | bytes 98328
  1.5 3.2 %collective-permute-start = (f32[3,8,128]{2,1,0:T(8,128)S(1)}, f32[3,8,128]{2,1,0:T(8,128)S(1)}, u32[]{:S(2)}, u32[]{:S(2)}) collective-permute-start(f32[3,8,128]{2,1,0:T(8,128)S(1)} %get-tuple-element.25), channel_id=1, source_target_pairs={{0,8},{8,16},{16,24},{1,9},{9,17},{17,25},{2,10},{10,18},{18,26},{... | collective-permute-start | bytes 36872 | tf_op jit(solution)/shard_map/ppermute | solution.py:624
  4.8 2.1 %collective-permute-start.1 = (f32[3,8,128]{2,1,0:T(8,128)S(1)}, f32[3,8,128]{2,1,0:T(8,128)S(1)}, u32[]{:S(2)}, u32[]{:S(2)}) collective-permute-start(f32[3,8,128]{2,1,0:T(8,128)S(1)} %get-tuple-element.26), channel_id=1, source_target_pairs={{8,0},{16,8},{24,16},{9,1},{17,9},{25,17},{10,2},{18,10},{26,18},{... | collective-permute-start | bytes 36872 | tf_op jit(solution)/shard_map/ppermute | solution.py:624
  6.8 1.3 %collective-permute-start.2 = (f32[3,8,128]{2,1,0:T(8,128)S(1)}, f32[3,8,128]{2,1,0:T(8,128)S(1)}, u32[]{:S(2)}, u32[]{:S(2)}) collective-permute-start(f32[3,8,128]{2,1,0:T(8,128)S(1)} %get-tuple-element.27), channel_id=1, source_target_pairs={{0,1},{1,2},{2,3},{3,4},{4,5},{5,6},{6,7},{8,9},{9,10},{10,11},{11... | collective-permute-start | bytes 36872 | tf_op jit(solution)/shard_map/ppermute | solution.py:624
  8.1 0.0 copy-start.1
  8.2 0.0 copy-start.2
  8.2 3.9 %collective-permute-start.3 = (f32[3,8,128]{2,1,0:T(8,128)S(1)}, f32[3,8,128]{2,1,0:T(8,128)S(1)}, u32[]{:S(2)}, u32[]{:S(2)}) collective-permute-start(f32[3,8,128]{2,1,0:T(8,128)S(1)} %get-tuple-element.28), channel_id=1, source_target_pairs={{1,0},{2,1},{3,2},{4,3},{5,4},{6,5},{7,6},{9,8},{10,9},{11,10},{12... | collective-permute-start | bytes 36872 | tf_op jit(solution)/shard_map/ppermute | solution.py:624
  12.1 0.0 copy-start.3
  12.1 0.6 %copy-done.3 = s32[1,8]{1,0:T(1,128)S(1)} copy-done((s32[1,8]{1,0:T(1,128)S(1)}, s32[1,8]{1,0:T(1,128)}, u32[]{:S(2)}) %copy-start.3) | copy-done | bytes 56
  12.7 2.5 %heavy_moments.1 = (f32[8,16,8,128]{3,2,1,0:T(8,128)S(1)}, f32[4,3,32,1024]{3,2,1,0:T(8,128)S(1)}, bf16[4,2,3,32,1024]{4,3,2,1,0:T(8,128)(2,1)S(1)}) custom-call(s32[1,8]{1,0:T(1,128)S(1)} %copy-done.3, f32[1,1,8,3,32,1024]{5,4,3,2,1,0:T(8,128)} %base.5, bf16[1,1,8,2,3,32,1024]{6,5,4,3,2,1,0:T(8,128)(2,1)} %noise.5), custom_call_target="tpu_custom_call" | custom-call | flops 8388608 | bytes 3145728 | tf_op jit(solution)/shard_map/heavy_moments/pallas_call | solution.py:175
  15.2 0.0 collective-permute-done.x_low
  15.3 0.0 collective-permute-done.1.x_high
  15.3 0.0 collective-permute-done.2.y_low
  15.3 0.0 collective-permute-done.3.y_high
  15.3 1.2 %gradients.1 = (f32[576,128]{1,0:T(8,128)S(1)}, f32[4,12,8,128]{3,2,1,0:T(8,128)S(1)}, f32[4,12,8,128]{3,2,1,0:T(8,128)S(1)}) custom-call(s32[1,8]{1,0:T(1,128)S(1)} %copy-done.3, f32[3,8,8,128]{3,2,1,0:T(8,128)S(1)} %copy-done.1, f32[3,8,128]{2,1,0:T(8,128)S(1)} %collective-permute-done.x_low, f32[3,8,128]{2,1,0:T(8,128)S(1)} %collective-permute-done.1.x_high, ...), custom_call_target="tpu_custom_call" | custom-call | flops 4194304 | bytes 1048576 | tf_op jit(solution)/shard_map/gradients/pallas_call | solution.py:256
  16.5 2.6 %collective-permute-start.4 = (f32[4,12,8,128]{3,2,1,0:T(8,128)S(1)}, f32[4,12,8,128]{3,2,1,0:T(8,128)S(1)}, u32[]{:S(2)}, u32[]{:S(2)}) collective-permute-start(f32[4,12,8,128]{3,2,1,0:T(8,128)S(1)} %get-tuple-element.32), channel_id=1, source_target_pairs={{0,1},{1,0},{2,3},{3,2},{4,5},{5,4},{6,7},{7,6},{8,9},{9,8},{10,11... | collective-permute-start | bytes 589832 | tf_op jit(solution)/shard_map/ppermute | solution.py:269
  19.1 1.1 %collective-permute-done.4.received = f32[4,12,8,128]{3,2,1,0:T(8,128)S(1)} collective-permute-done((f32[4,12,8,128]{3,2,1,0:T(8,128)S(1)}, f32[4,12,8,128]{3,2,1,0:T(8,128)S(1)}, u32[]{:S(2)}, u32[]{:S(2)}) %collective-permute-start.4) | collective-permute-done | bytes 196640 | tf_op jit(solution)/shard_map/ppermute | solution.py:269
  20.2 0.7 %merge.2 = (f32[2,12,8,128]{3,2,1,0:T(8,128)S(1)}, f32[2,12,8,128]{3,2,1,0:T(8,128)S(1)}) custom-call(s32[1,8]{1,0:T(1,128)S(1)} %copy-done.3, f32[4,12,8,128]{3,2,1,0:T(8,128)S(1)} %get-tuple-element.31.kept, f32[4,12,8,128]{3,2,1,0:T(8,128)S(1)} %collective-permute-done.4.received), custom_call_target="tpu_custom_call" | custom-call | flops 1024 | bytes 262144 | tf_op jit(solution)/shard_map/merge/pallas_call | solution.py:295
  20.8 0.1 collective-permute-start.5
  20.9 4.0 %collective-permute-done.5.received = f32[2,12,8,128]{3,2,1,0:T(8,128)S(1)} collective-permute-done((f32[2,12,8,128]{3,2,1,0:T(8,128)S(1)}, f32[2,12,8,128]{3,2,1,0:T(8,128)S(1)}, u32[]{:S(2)}, u32[]{:S(2)}) %collective-permute-start.5) | collective-permute-done | bytes 98336 | tf_op jit(solution)/shard_map/ppermute | solution.py:269
  24.9 0.6 %merge.3 = (f32[1,12,8,128]{3,2,1,0:T(8,128)S(1)}, f32[1,12,8,128]{3,2,1,0:T(8,128)S(1)}) custom-call(s32[1,8]{1,0:T(1,128)S(1)} %copy-done.3, f32[2,12,8,128]{3,2,1,0:T(8,128)S(1)} %get-tuple-element.33.kept, f32[2,12,8,128]{3,2,1,0:T(8,128)S(1)} %collective-permute-done.5.received), custom_call_target="tpu_custom_call" | custom-call | flops 1024 | bytes 262144 | tf_op jit(solution)/shard_map/merge/pallas_call | solution.py:295
  25.5 0.2 collective-permute-start.6
  25.7 2.8 %collective-permute-done.6.received = f32[1,12,8,128]{3,2,1,0:T(8,128)S(1)} collective-permute-done((f32[1,12,8,128]{3,2,1,0:T(8,128)S(1)}, f32[1,12,8,128]{3,2,1,0:T(8,128)S(1)}, u32[]{:S(2)}, u32[]{:S(2)}) %collective-permute-start.6) | collective-permute-done | bytes 49184 | tf_op jit(solution)/shard_map/ppermute | solution.py:269
  28.5 5.8 %extra_fields.1 = (f32[1,1,3,224,1024]{4,3,2,1,0:T(8,128)}, f32[8,8,128]{2,1,0:T(8,128)S(1)}) custom-call(s32[1,8]{1,0:T(1,128)S(1)} %copy-done.3, f32[1,1,3,224,1024]{4,3,2,1,0:T(8,128)} %base.4, bf16[1,1,2,3,224,1024]{5,4,3,2,1,0:T(8,128)(2,1)} %noise.4, f32[1,12,8,128]{3,2,1,0:T(8,128)S(1)} %get-tuple-element.35.kept, ...), custom_call_target="tpu_custom_call" | custom-call | flops 33554432 | bytes 9437184 | tf_op jit(solution)/shard_map/extra_fields/pallas_call | solution.py:513
  34.3 0.2 collective-permute-start.7
  34.6 2.6 %collective-permute-done.7.second = f32[1,8,8,128]{3,2,1,0:T(8,128)S(1)} collective-permute-done((f32[1,8,8,128]{3,2,1,0:T(8,128)S(1)}, f32[1,8,8,128]{3,2,1,0:T(8,128)S(1)}, u32[]{:S(2)}, u32[]{:S(2)}) %collective-permute-start.7) | collective-permute-done | bytes 32800 | tf_op jit(solution)/shard_map/ppermute | solution.py:269
  37.2 0.3 collective-permute-start.8
  37.5 2.8 %collective-permute-done.8.second = f32[2,8,8,128]{3,2,1,0:T(8,128)S(1)} collective-permute-done((f32[2,8,8,128]{3,2,1,0:T(8,128)S(1)}, f32[2,8,8,128]{3,2,1,0:T(8,128)S(1)}, u32[]{:S(2)}, u32[]{:S(2)}) %collective-permute-start.8) | collective-permute-done | bytes 65568 | tf_op jit(solution)/shard_map/ppermute | solution.py:269
  40.3 4.7 %collective-permute-start.9 = (f32[4,8,8,128]{3,2,1,0:T(8,128)S(1)}, f32[4,8,8,128]{3,2,1,0:T(8,128)S(1)}, u32[]{:S(2)}, u32[]{:S(2)}) collective-permute-start(f32[4,8,8,128]{3,2,1,0:T(8,128)S(1)} %join.3.near), channel_id=1, source_target_pairs={{0,1},{1,0},{2,3},{3,2},{4,5},{5,4},{6,7},{7,6},{8,9},{9,8},{10,11... | collective-permute-start | bytes 393224 | tf_op jit(solution)/shard_map/ppermute | solution.py:269
  45.0 5.3 %ordinary_tiles.1 = (f32[1,1,8,3,32,1024]{5,4,3,2,1,0:T(8,128)}, f32[8,6,8,128]{3,2,1,0:T(8,128)S(1)}) custom-call(s32[1,1,8]{2,1,0:T(1,128)S(1)} %copy-done.4, f32[1,1,8,3,32,1024]{5,4,3,2,1,0:T(8,128)} %base.5, bf16[1,1,8,2,3,32,1024]{6,5,4,3,2,1,0:T(8,128)(2,1)} %noise.5, f32[576,128]{1,0:T(8,128)S(1)} %get-tuple-element.30.grad), custom_call_target="tpu_custom_call" | custom-call | flops 33554432 | bytes 10485760 | tf_op jit(solution)/shard_map/ordinary_tiles/pallas_call | solution.py:405
  50.3 2.5 %heavy_tiles.1 = (f32[1,1,8,3,32,1024]{5,4,3,2,1,0:T(8,128)}, f32[1,1,6,8,1024]{4,3,2,1,0:T(8,128)}) custom-call(s32[1,8]{1,0:T(1,128)S(1)} %copy-done.3, f32[4,3,32,1024]{3,2,1,0:T(8,128)S(1)} %get-tuple-element.23.base, bf16[4,2,3,32,1024]{4,3,2,1,0:T(8,128)(2,1)S(1)} %get-tuple-element.24.noise, ...), custom_call_target="tpu_custom_call", output_to_operand_aliasing={{0}: (6, {})} | custom-call | flops 8388608 | bytes 4194304 | tf_op jit(solution)/shard_map/heavy_tiles/pallas_call | solution.py:599
  (8 shorter events, 0.0 us)
Async XLA Ops:
  0.6 0.9 %copy-start = (f32[3,8,8,128]{3,2,1,0:T(8,128)S(1)}, f32[3,8,8,128]{3,2,1,0:T(8,128)}, u32[]{:S(2)}) copy-start(f32[3,8,8,128]{3,2,1,0:T(8,128)} %velocity.3) | copy-start | bytes 294916
  1.5 13.7 %collective-permute-start = (f32[3,8,128]{2,1,0:T(8,128)S(1)}, f32[3,8,128]{2,1,0:T(8,128)S(1)}, u32[]{:S(2)}, u32[]{:S(2)}) collective-permute-start(f32[3,8,128]{2,1,0:T(8,128)S(1)} %get-tuple-element.25), channel_id=1, source_target_pairs={{0,8},{8,16},{16,24},{1,9},{9,17},{17,25},{2,10},{10,18},{18,26},{... | collective-permute-start | bytes 36872 | tf_op jit(solution)/shard_map/ppermute | solution.py:624
  4.8 10.5 %collective-permute-start.1 = (f32[3,8,128]{2,1,0:T(8,128)S(1)}, f32[3,8,128]{2,1,0:T(8,128)S(1)}, u32[]{:S(2)}, u32[]{:S(2)}) collective-permute-start(f32[3,8,128]{2,1,0:T(8,128)S(1)} %get-tuple-element.26), channel_id=1, source_target_pairs={{8,0},{16,8},{24,16},{9,1},{17,9},{25,17},{10,2},{18,10},{26,18},{... | collective-permute-start | bytes 36872 | tf_op jit(solution)/shard_map/ppermute | solution.py:624
  6.8 8.4 %collective-permute-start.2 = (f32[3,8,128]{2,1,0:T(8,128)S(1)}, f32[3,8,128]{2,1,0:T(8,128)S(1)}, u32[]{:S(2)}, u32[]{:S(2)}) collective-permute-start(f32[3,8,128]{2,1,0:T(8,128)S(1)} %get-tuple-element.27), channel_id=1, source_target_pairs={{0,1},{1,2},{2,3},{3,4},{4,5},{5,6},{6,7},{8,9},{9,10},{10,11},{11... | collective-permute-start | bytes 36872 | tf_op jit(solution)/shard_map/ppermute | solution.py:624
  8.1 7.1 %copy-start.1 = (f32[3,8,8,128]{3,2,1,0:T(8,128)S(1)}, f32[3,8,8,128]{3,2,1,0:T(8,128)}, u32[]{:S(2)}) copy-start(f32[3,8,8,128]{3,2,1,0:T(8,128)} %velocity.3) | copy-start | bytes 294916
  8.2 7.1 %copy-start.2 = (s32[8,8,128]{2,1,0:T(8,128)S(1)}, s32[8,8,128]{2,1,0:T(8,128)}, u32[]{:S(2)}) copy-start(s32[8,8,128]{2,1,0:T(8,128)} %wall.1) | copy-start | bytes 98308
  8.2 7.1 %collective-permute-start.3 = (f32[3,8,128]{2,1,0:T(8,128)S(1)}, f32[3,8,128]{2,1,0:T(8,128)S(1)}, u32[]{:S(2)}, u32[]{:S(2)}) collective-permute-start(f32[3,8,128]{2,1,0:T(8,128)S(1)} %get-tuple-element.28), channel_id=1, source_target_pairs={{1,0},{2,1},{3,2},{4,3},{5,4},{6,5},{7,6},{9,8},{10,9},{11,10},{12... | collective-permute-start | bytes 36872 | tf_op jit(solution)/shard_map/ppermute | solution.py:624
  12.1 0.7 %copy-start.3 = (s32[1,8]{1,0:T(1,128)S(1)}, s32[1,8]{1,0:T(1,128)}, u32[]{:S(2)}) copy-start(s32[1,8]{1,0:T(1,128)} %helper.11) | copy-start | bytes 100
  16.5 3.6 %collective-permute-start.4 = (f32[4,12,8,128]{3,2,1,0:T(8,128)S(1)}, f32[4,12,8,128]{3,2,1,0:T(8,128)S(1)}, u32[]{:S(2)}, u32[]{:S(2)}) collective-permute-start(f32[4,12,8,128]{3,2,1,0:T(8,128)S(1)} %get-tuple-element.32), channel_id=1, source_target_pairs={{0,1},{1,0},{2,3},{3,2},{4,5},{5,4},{6,7},{7,6},{8,9},{9,8},{10,11... | collective-permute-start | bytes 589832 | tf_op jit(solution)/shard_map/ppermute | solution.py:269
  20.8 4.1 %collective-permute-start.5 = (f32[2,12,8,128]{3,2,1,0:T(8,128)S(1)}, f32[2,12,8,128]{3,2,1,0:T(8,128)S(1)}, u32[]{:S(2)}, u32[]{:S(2)}) collective-permute-start(f32[2,12,8,128]{3,2,1,0:T(8,128)S(1)} %get-tuple-element.34), channel_id=1, source_target_pairs={{0,2},{1,3},{2,0},{3,1},{4,6},{5,7},{6,4},{7,5},{8,10},{9,11},{10,... | collective-permute-start | bytes 294920 | tf_op jit(solution)/shard_map/ppermute | solution.py:269
  25.5 3.0 %collective-permute-start.6 = (f32[1,12,8,128]{3,2,1,0:T(8,128)S(1)}, f32[1,12,8,128]{3,2,1,0:T(8,128)S(1)}, u32[]{:S(2)}, u32[]{:S(2)}) collective-permute-start(f32[1,12,8,128]{3,2,1,0:T(8,128)S(1)} %get-tuple-element.36), channel_id=1, source_target_pairs={{0,4},{1,5},{2,6},{3,7},{4,0},{5,1},{6,2},{7,3},{8,12},{9,13},{10,... | collective-permute-start | bytes 147464 | tf_op jit(solution)/shard_map/ppermute | solution.py:269
  28.5 16.5 %copy-start.4 = (s32[1,1,8]{2,1,0:T(1,128)S(1)}, s32[1,1,8]{2,1,0:T(1,128)}, u32[]{:S(2)}) copy-start(s32[1,1,8]{2,1,0:T(1,128)} %counts.1) | copy-start | bytes 100
  34.3 2.8 %collective-permute-start.7 = (f32[1,8,8,128]{3,2,1,0:T(8,128)S(1)}, f32[1,8,8,128]{3,2,1,0:T(8,128)S(1)}, u32[]{:S(2)}, u32[]{:S(2)}) collective-permute-start(f32[1,8,8,128]{3,2,1,0:T(8,128)S(1)} %bitcast.2), channel_id=1, source_target_pairs={{0,4},{1,5},{2,6},{3,7},{4,0},{5,1},{6,2},{7,3},{8,12},{9,13},{10,... | collective-permute-start | bytes 98312 | tf_op jit(solution)/shard_map/ppermute | solution.py:269
  37.2 3.1 %collective-permute-start.8 = (f32[2,8,8,128]{3,2,1,0:T(8,128)S(1)}, f32[2,8,8,128]{3,2,1,0:T(8,128)S(1)}, u32[]{:S(2)}, u32[]{:S(2)}) collective-permute-start(f32[2,8,8,128]{3,2,1,0:T(8,128)S(1)} %join.2.first), channel_id=1, source_target_pairs={{0,2},{1,3},{2,0},{3,1},{4,6},{5,7},{6,4},{7,5},{8,10},{9,11},{10,... | collective-permute-start | bytes 196616 | tf_op jit(solution)/shard_map/ppermute | solution.py:269
  40.3 10.0 %collective-permute-start.9 = (f32[4,8,8,128]{3,2,1,0:T(8,128)S(1)}, f32[4,8,8,128]{3,2,1,0:T(8,128)S(1)}, u32[]{:S(2)}, u32[]{:S(2)}) collective-permute-start(f32[4,8,8,128]{3,2,1,0:T(8,128)S(1)} %join.3.near), channel_id=1, source_target_pairs={{0,1},{1,0},{2,3},{3,2},{4,5},{5,4},{6,7},{7,6},{8,9},{9,8},{10,11... | collective-permute-start | bytes 393224 | tf_op jit(solution)/shard_map/ppermute | solution.py:269
where the time goes:
time: 53.4 us; the launch traced here: 52.8 us
  Pallas kernels  18.6 us (35%)
  starting transfers between devices  18.6 us (35%)
  waiting for transfers between devices  13.3 us (25%)
  local copies, waits for them, and re-layouts  1.55 us (3%)
  between operations  0.82 us (2%)
    ppermute x6, waiting for transfers between devices, swapped(): return lax.ppermute(block, 'gy', [(i, i ^ 1 << bit) for i in range(size)])  13.3 us
    ppermute x4, starting transfers between devices, both_ways(): return (lax.ppermute(last, axis, up), lax.ppermute(first, axis, down))  10.5 us
    ppermute x6, starting transfers between devices, swapped(): return lax.ppermute(block, 'gy', [(i, i ^ 1 << bit) for i in range(size)])  8.11 us
    pallas_call x1, Pallas kernels, call_extra(): pl.pallas_call(functools.partial(extra, tiles, bit, rows_each), out_shape...  5.8 us
    pallas_call x1, Pallas kernels, call_ordinary(): pl.pallas_call(ordinary, out_shape=(jax.ShapeDtypeStruct(base_fields.shap...  5.27 us
    pallas_call x1, Pallas kernels, call_heavy(): pl.pallas_call(functools.partial(heavy, bits), out_shape=(jax.ShapeDtypeS...  2.52 us
    pallas_call x1, Pallas kernels, call_heavy_moments(): pl.pallas_call(heavy_moments, out_shape=(jax.ShapeDtypeStruct((slots, 16,...  2.5 us
    unnamed x10, local copies, waits for them, and re-layouts  1.55 us
  transfers between devices with their start and end apart: 10, of which 5 were waited for; matrix products, arithmetic and copies ran while one was open for 0% of the time, Pallas kernels for 15%

commit v1 on v0

v1 whole, which is shorter than its diff:
```python
import functools

import jax
import jax.numpy as jnp
from jax import lax
from jax.experimental import pallas as pl
from jax.experimental.pallas import tpu as pltpu
from jax.sharding import PartitionSpec as P

ALL_FIELDS = 256
LANES = 128
SUB = 8
SMALL = 10 << 20
LARGE = 14 << 20

time_step = 0.05
weissenberg = 0.25
max_extension = 50.0
noise_scale = (time_step / weissenberg) ** 0.5
component_pairs = ((0, 0), (1, 1), (2, 2), (0, 1), (0, 2), (1, 2))
moment_of = {(0, 0): 0, (1, 1): 1, (2, 2): 2, (0, 1): 3, (1, 0): 3, (0, 2): 4, (2, 0): 4, (1, 2): 5, (2, 1): 5}
f32 = jnp.float32

smem = pl.BlockSpec(memory_space=pltpu.SMEM)
vmem = pl.BlockSpec(memory_space=pltpu.VMEM)
hbm = pl.BlockSpec(memory_space=pltpu.HBM)
anywhere = pl.BlockSpec(memory_space=pl.ANY)


def far_memory(*arrays):
    return [pltpu.with_memory_space_constraint(array, pltpu.HBM) for array in arrays]


def near_memory(*arrays):
    return [pltpu.with_memory_space_constraint(array, pltpu.VMEM) for array in arrays]


def column_sum(value):
    return jnp.sum(value, axis=0, keepdims=True)


def wide(row):
    return jnp.broadcast_to(row, (SUB, LANES))


def turned(value, cell_z):
    sub = lax.broadcasted_iota(jnp.int32, value.shape, 0)
    group = lax.broadcasted_iota(jnp.int32, value.shape, 1) // cell_z
    skewed = pltpu.roll(value, cell_z, 1, stride=cell_z, stride_axis=0)
    mixed = jnp.take_along_axis(skewed, (group + sub) & (SUB - 1), axis=0, mode="promise_in_bounds")
    return pltpu.roll(mixed, 0, 1, stride=cell_z, stride_axis=0)


def relax_of(total, inverse):
    factor = 1.0 / (1.0 - total * inverse / max_extension)
    return 1.0 - (time_step * 0.5 / weissenberg) * factor


def stepped(vectors, noise, matrix):
    return [
        matrix[3 * a] * vectors[0]
        + matrix[3 * a + 1] * vectors[1]
        + matrix[3 * a + 2] * vectors[2]
        + noise_scale * noise[a]
        for a in range(3)
    ]


def with_diagonal(grad, relax):
    return [g + relax if i % 4 == 0 else g for i, g in enumerate(grad)]


def noise_rows(ref, start):
    both = [ref(a, pl.ds(start, 2 * SUB)).astype(f32) for a in range(3)]
    return [[w[:SUB] for w in both], [w[SUB:] for w in both]]


def add_moments(sums, q):
    return [s + q[a] * q[b] for s, (a, b) in zip(sums, component_pairs)]


def product_sums(sums, q, w):
    terms = [q[a] * q[b] for a, b in component_pairs]
    terms += [q[a] * w[b] for a in range(3) for b in range(3)]
    terms += [w[0] * w[0] + w[1] * w[1] + w[2] * w[2]]
    return [s + t for s, t in zip(sums, terms)]


def coefficients(g, m):
    cross = lambda a, b: m[6 + 3 * a + b]
    square = lambda a, b: m[moment_of[a, b]]
    once, twice, kick = 0.0, 0.0, 0.0
    for a in range(3):
        for b in range(3):
            once += g[3 * a + b] * square(a, b)
            kick += g[3 * a + b] * cross(b, a)
            inner = 0.0
            for c in range(3):
                inner += g[3 * a + c] * square(b, c)
            twice += g[3 * a + b] * inner
    return [
        twice + (2 * noise_scale) * kick + noise_scale**2 * m[15],
        2.0 * once + (2 * noise_scale) * (cross(0, 0) + cross(1, 1) + cross(2, 2)),
        m[0] + m[1] + m[2],
    ]


def owned_slots(tiles, me, helper):
    found = []
    for h in range(helper.shape[1]):
        tile = helper[0, h] - me * tiles
        found.append((h, (tile >= 0) & (tile < tiles), tile))
    return found


def small(flops, traffic):
    return pl.CostEstimate(flops=flops, bytes_accessed=traffic, transcendentals=0)


def edges(helper, velocity, x_last, x_first, y_last, y_first):
    depth, width = velocity.shape[1:3]
    for a in range(3):
        x_last[a] = velocity[a, depth - 1]
        x_first[a] = velocity[a, 0]
        for x in range(depth):
            y_last[a, pl.ds(x, 1), :] = velocity[a, x, pl.ds(width - 1, 1), :]
            y_first[a, pl.ds(x, 1), :] = velocity[a, x, pl.ds(0, 1), :]


def call_edges(helper_tile, velocity):
    _, depth, width, length = velocity.shape
    along_x = jax.ShapeDtypeStruct((3, width, length), f32)
    along_y = jax.ShapeDtypeStruct((3, depth, length), f32)
    return pl.pallas_call(
        edges,
        out_shape=(along_x, along_x, along_y, along_y),
        in_specs=[smem, vmem],
        out_specs=(vmem,) * 4,
        compiler_params=pltpu.CompilerParams(vmem_limit_bytes=4 << 20),
        cost_estimate=small(1 << 10, 1 << 17),
        name="edges",
    )(helper_tile, velocity)


def heavy_moments(helper, base, noise, out, fields, shocks, sems):
    slots, _, count, cells = fields.shape
    tiles = base.shape[2]
    me = lax.axis_index("gy")

    def loads(h, tile):
        return (
            pltpu.make_async_copy(base.at[0, 0, tile], fields.at[h], sems.at[0, h]),
            pltpu.make_async_copy(noise.at[0, 0, tile, 0], shocks.at[h], sems.at[1, h]),
        )

    found = owned_slots(tiles, me, helper)
    for h, owned, tile in found:

        @pl.when(owned)
        def _(h=h, tile=tile):
            for copy in loads(h, tile):
                copy.start()

    for h, owned, tile in found:

        @pl.when(owned)
        def _(h=h, tile=tile):
            for copy in loads(h, tile):
                copy.wait()

            @pl.loop(0, cells // LANES)
            def _(x):
                lanes = pl.ds(pl.multiple_of(x * LANES, LANES), LANES)
                sums = [jnp.zeros((SUB, LANES), f32)] * 16
                for group in range(count // (2 * SUB)):
                    pair = noise_rows(lambda a, rows: shocks[h, a, rows, lanes], group * 2 * SUB)
                    for half in range(2):
                        rows = pl.ds((2 * group + half) * SUB, SUB)
                        sums = product_sums(sums, [fields[h, a, rows, lanes] for a in range(3)], pair[half])
                for i, s in enumerate(sums):
                    out[h, i, pl.ds(x, 1), :] = column_sum(s)


def call_heavy_moments(helper_tile, base_fields, base_noise):
    slots = helper_tile.shape[1]
    count, cells = base_fields.shape[-2:]
    return pl.pallas_call(
        heavy_moments,
        out_shape=jax.ShapeDtypeStruct((slots, 16, cells // LANES, LANES), f32),
        in_specs=[smem, hbm, hbm],
        out_specs=vmem,
        scratch_shapes=[
            pltpu.VMEM((slots, 3, count, cells), f32),
            pltpu.VMEM((slots, 3, count, cells), jnp.bfloat16),
            pltpu.SemaphoreType.DMA((2, slots)),
        ],
        compiler_params=pltpu.CompilerParams(vmem_limit_bytes=LARGE),
        cost_estimate=small(8 << 20, 3 << 20),
        name="heavy_moments",
    )(helper_tile, *far_memory(base_fields, base_noise))


def extra_moments(unroll, before, base, noise, out):
    _, _, _, count, cells = base.shape
    zero = jnp.zeros((SUB, LANES), f32)

    @pl.loop(0, cells // LANES)
    def _(x):
        lanes = pl.ds(pl.multiple_of(x * LANES, LANES), LANES)

        def body(i, sums):
            start = pl.multiple_of(i * 2 * SUB, 2 * SUB)
            pair = noise_rows(lambda a, rows: noise[0, 0, 0, a, rows, lanes], start)
            for half in range(2):
                rows = pl.ds(start + half * SUB, SUB)
                sums = product_sums(sums, [base[0, 0, a, rows, lanes] for a in range(3)], pair[half])
            return sums

        for i, s in enumerate(lax.fori_loop(0, count // (2 * SUB), body, [zero] * 16, unroll=unroll)):
            out[i, pl.ds(x, 1), :] = column_sum(s)


def call_extra_moments(before, extra_fields, extra_noise):
    cells = extra_fields.shape[-1]
    return pl.pallas_call(
        functools.partial(extra_moments, 7),
        out_shape=jax.ShapeDtypeStruct((16, cells // LANES, LANES), f32),
        in_specs=[anywhere, vmem, vmem],
        out_specs=vmem,
        compiler_params=pltpu.CompilerParams(vmem_limit_bytes=SMALL),
        cost_estimate=small(8 << 20, 5 << 20),
        name="extra_moments",
    )(before, *near_memory(extra_fields, extra_noise))


def gradients(tiles, helper, velocity, x_low, x_high, y_low, y_high, wall, moments, grad, keep, send):
    me = lax.axis_index("gy")
    depth = velocity.shape[1]
    cell_z = velocity.shape[3] // tiles
    sub = lax.broadcasted_iota(jnp.int32, (SUB, LANES), 0)
    lane = lax.broadcasted_iota(jnp.int32, (SUB, LANES), 1)
    z = lane % cell_z
    scales = [turned(jnp.where(wall[x] == 0, 0.5 * time_step, 0.0).astype(f32), cell_z) for x in range(depth)]
    for a in range(3):
        rows = [x_low[a]] + [velocity[a, x] for x in range(depth)] + [x_high[a]]
        rows = [turned(row, cell_z) for row in rows]
        low, high = turned(y_low[a], cell_z), turned(y_high[a], cell_z)
        for x in range(depth):
            here = rows[x + 1]
            above = high if x == depth - 1 else pltpu.roll(high, LANES - cell_z * (x + 1), 1)
            below = low if x == 0 else pltpu.roll(low, LANES - cell_z * x, 1)
            y_up = jnp.where(lane < LANES - cell_z, pltpu.roll(here, LANES - cell_z, 1), above)
            y_down = jnp.where(lane >= cell_z, pltpu.roll(here, cell_z, 1), below)
            next_tile = pltpu.roll(pltpu.roll(here, cell_z - 1, 1), 1, 0)
            last_tile = pltpu.roll(pltpu.roll(here, LANES - cell_z + 1, 1), SUB - 1, 0)
            next_tile = jnp.where(sub == 0, 0.0, next_tile)
            last_tile = jnp.where(sub == SUB - 1, 0.0, last_tile)
            z_up = jnp.where(z == cell_z - 1, next_tile, pltpu.roll(here, LANES - 1, 1))
            z_down = jnp.where(z == 0, last_tile, pltpu.roll(here, 1, 1))
            for b, difference in enumerate((rows[x + 2] - rows[x], y_up - y_down, z_up - z_down)):
                grad[pl.ds(((3 * a + b) * depth + x) * SUB, SUB), :] = difference * scales[x]
    for h, owned, tile in owned_slots(tiles, me, helper):

        @pl.when(owned)
        def _(h=h, tile=tile):
            g = [grad[pl.ds(i * depth * SUB + SUB - 1 - tile, depth, stride=SUB), :] for i in range(9)]
            rows = g + coefficients(g, [moments[h, i] for i in range(16)])
            stays = (me & 1) == (h & 1)

            @pl.when(stays)
            def _():
                for i, row in enumerate(rows):
                    keep[h >> 1, i] = row

            @pl.when(jnp.logical_not(stays))
            def _():
                for i, row in enumerate(rows):
                    send[h >> 1, i] = row


def call_gradients(tiles, helper_tile, velocity, halos, wall_cells, moments):
    slots = helper_tile.shape[1]
    depth = velocity.shape[1]
    half = jax.ShapeDtypeStruct((slots // 2, 12, depth, LANES), f32)
    return pl.pallas_call(
        functools.partial(gradients, tiles),
        out_shape=(jax.ShapeDtypeStruct((9 * depth * SUB, LANES), f32), half, half),
        in_specs=[smem] + [vmem] * 7,
        out_specs=(vmem,) * 3,
        compiler_params=pltpu.CompilerParams(vmem_limit_bytes=8 << 20),
        cost_estimate=small(4 << 20, 1 << 20),
        name="gradients",
    )(helper_tile, velocity, *halos, wall_cells, moments)


def swapped(block, bit):
    size = lax.axis_size("gy")
    return lax.ppermute(block, "gy", [(i, i ^ (1 << bit)) for i in range(size)])


def arrived(tiles, me, helper, slot, bit):
    owner = helper[0, slot] // tiles
    return (((owner ^ me) >> bit) & 1) == 1


def merge(tiles, bit, helper, before, kept, received, keep, send):
    me = lax.axis_index("gy")
    below = me & ((2 << bit) - 1)
    mine = (me >> (bit + 1)) & 1
    for j in range(kept.shape[0]):
        pick = arrived(tiles, me, helper, (j << (bit + 1)) | below, bit)
        stays = mine == (j & 1)
        for source, chosen in ((received, pick), (kept, jnp.logical_not(pick))):
            for out, there in ((keep, stays), (send, jnp.logical_not(stays))):

                @pl.when(chosen & there)
                def _(j=j, source=source, out=out):
                    for i in range(kept.shape[1]):
                        out[j >> 1, i] = source[j, i]


def call_merge(tiles, bit, helper_tile, before, kept, received):
    half = jax.ShapeDtypeStruct((kept.shape[0] // 2,) + kept.shape[1:], f32)
    return pl.pallas_call(
        functools.partial(merge, tiles, bit),
        out_shape=(half, half),
        in_specs=[smem, anywhere, vmem, vmem],
        out_specs=(vmem, vmem),
        compiler_params=pltpu.CompilerParams(vmem_limit_bytes=4 << 20),
        cost_estimate=small(1 << 10, 1 << 18),
        name="merge",
    )(helper_tile, before, kept, received)


def call_join(before, first, second):
    def join(before, first, second, out):
        out[: first.shape[0]] = first[...]
        out[first.shape[0] :] = second[...]

    return pl.pallas_call(
        join,
        out_shape=jax.ShapeDtypeStruct((2 * first.shape[0],) + first.shape[1:], f32),
        in_specs=[anywhere, vmem, vmem],
        out_specs=vmem,
        compiler_params=pltpu.CompilerParams(vmem_limit_bytes=4 << 20),
        cost_estimate=small(1 << 10, 1 << 18),
        name="join",
    )(before, first, second)


def stress_rows(sums, inverse):
    second = [s * inverse for s in sums]
    stretch = 1.0 / (1.0 - (second[0] + second[1] + second[2]) / max_extension)
    return [(stretch * s - (1.0 if i < 3 else 0.0)) * (1.0 / weissenberg) for i, s in enumerate(second)]


def tile_grad(grad, depth, tile, x):
    return [wide(grad[pl.ds((i * depth + x + 1) * SUB - 1 - tile, 1), :]) for i in range(9)]


def ordinary(first, counts, before, base, noise, grad, old_base, new_base, stress, halfway, fields, totals, relaxes, sems):
    here, _, count, cells = fields.shape
    depth = cells // LANES
    groups = count // (2 * SUB)
    zero = jnp.zeros((SUB, LANES), f32)

    def store(place):
        return pltpu.make_async_copy(fields.at[place], new_base.at[0, 0, first + place], sems.at[place])

    for place in range(here):
        tile = first + place
        tile_count = counts[0, 0, tile]

        @pl.when(tile_count != ALL_FIELDS)
        def _(place=place, tile=tile, tile_count=tile_count):
            inverse = 1.0 / jnp.full((1, LANES), tile_count.astype(f32))
            for x in range(depth):
                total = zero
                for group in range(2 * groups):
                    for a in range(3):
                        q = base[0, 0, tile, a, pl.ds(group * SUB, SUB), pl.ds(x * LANES, LANES)]
                        total = total + q * q
                totals[pl.ds(x, 1), :] = column_sum(total)
            for step in range(2):
                relaxes[...] = relax_of(totals[...], inverse)

                def body(x, step=step):
                    lanes = pl.ds(pl.multiple_of(x * LANES, LANES), LANES)
                    matrix = with_diagonal(tile_grad(grad, depth, tile, x), wide(relaxes[pl.ds(x, 1), :]))
                    sums = [zero] * (1 if step == 0 else 6)
                    for group in range(groups):
                        pair = noise_rows(lambda a, rows: noise[0, 0, tile, step, a, rows, lanes], group * 2 * SUB)
                        for half in range(2):
                            rows = pl.ds((2 * group + half) * SUB, SUB)
                            if step == 0:
                                q = [base[0, 0, tile, a, rows, lanes] for a in range(3)]
                            else:
                                q = [halfway[a, rows, lanes] for a in range(3)]
                            q = stepped(q, pair[half], matrix)
                            for a in range(3):
                                if step == 0:
                                    halfway[a, rows, lanes] = q[a]
                                else:
                                    fields[place, a, rows, lanes] = q[a]
                            if step == 0:
                                sums[0] = sums[0] + (q[0] * q[0] + q[1] * q[1] + q[2] * q[2])
                            else:
                                sums = add_moments(sums, q)
                    if step == 0:
                        totals[pl.ds(x, 1), :] = column_sum(sums[0])
                    else:
                        for i, row in enumerate(stress_rows([column_sum(s) for s in sums], inverse)):
                            stress[x, i, pl.ds(place, 1), :] = row

                @pl.loop(0, depth // 2)
                def _(x):
                    body(2 * x)
                    body(2 * x + 1)

            store(place).start()

    for place in range(here):

        @pl.when(counts[0, 0, first + place] != ALL_FIELDS)
        def _(place=place):
            store(place).wait()


def call_ordinary(first, here, tile_counts, before, base_fields, base_noise, grad, new_base):
    count, cells = base_fields.shape[-2:]
    depth = cells // LANES
    body = functools.partial(ordinary, first)
    if new_base is None:
        body = lambda *refs: ordinary(first, *refs[:5], None, *refs[5:])
    return pl.pallas_call(
        body,
        out_shape=(
            jax.ShapeDtypeStruct(base_fields.shape, f32),
            jax.ShapeDtypeStruct((depth, 6, here, LANES), f32),
        ),
        in_specs=[smem, anywhere, vmem, vmem, vmem] + [hbm] * (new_base is not None),
        out_specs=(hbm, vmem),
        input_output_aliases={} if new_base is None else {5: 0},
        scratch_shapes=[
            pltpu.VMEM((3, count, cells), f32),
            pltpu.VMEM((here, 3, count, cells), f32),
            pltpu.VMEM((depth, LANES), f32),
            pltpu.VMEM((depth, LANES), f32),
            pltpu.SemaphoreType.DMA((here,)),
        ],
        compiler_params=pltpu.CompilerParams(vmem_limit_bytes=SMALL),
        cost_estimate=small(8 << 20, 3 << 20),
        name="ordinary_tiles",
    )(tile_counts, before, *near_memory(base_fields, base_noise), grad, *([] if new_base is None else [new_base]))


def extra(tiles, bit, unroll, helper, base, noise, moments, kept, received, new_fields, reply, message):
    me = lax.axis_index("gy")
    _, _, _, count, cells = base.shape
    inverse = 1.0 / float(ALL_FIELDS)
    zero = jnp.zeros((SUB, LANES), f32)
    pick = arrived(tiles, me, helper, me, bit)
    for i in range(message.shape[0]):
        message[i] = jnp.where(pick, received[0, i], kept[0, i])
    own = coefficients([message[i] for i in range(9)], [moments[i] for i in range(16)])
    both = [message[9 + i] + own[i] for i in range(3)]
    first = relax_of(both[2], inverse)
    second = relax_of(both[0] + first * (both[1] + first * both[2]), inverse)
    reply[0], reply[1] = first, second

    @pl.loop(0, cells // LANES)
    def _(x):
        lanes = pl.ds(pl.multiple_of(x * LANES, LANES), LANES)
        grad = [wide(message[i, pl.ds(x, 1), :]) for i in range(9)]
        matrices = [with_diagonal(grad, wide(reply[step, pl.ds(x, 1), :])) for step in range(2)]

        def body(i, sums):
            start = pl.multiple_of(i * 2 * SUB, 2 * SUB)
            pairs = [noise_rows(lambda a, rows: noise[0, 0, step, a, rows, lanes], start) for step in range(2)]
            for half in range(2):
                rows = pl.ds(start + half * SUB, SUB)
                q = [base[0, 0, a, rows, lanes] for a in range(3)]
                for step in range(2):
                    q = stepped(q, pairs[step][half], matrices[step])
                for a in range(3):
                    new_fields[0, 0, a, rows, lanes] = q[a]
                sums = add_moments(sums, q)
            return sums

        for i, s in enumerate(lax.fori_loop(0, count // (2 * SUB), body, [zero] * 6, unroll=unroll)):
            reply[2 + i, pl.ds(x, 1), :] = column_sum(s)


def call_extra(tiles, bit, helper_tile, extra_fields, extra_noise, moments, kept, received):
    depth = extra_fields.shape[-1] // LANES
    return pl.pallas_call(
        functools.partial(extra, tiles, bit, 7),
        out_shape=(
            pltpu.VMEM(extra_fields.shape, f32),
            jax.ShapeDtypeStruct((8, depth, LANES), f32),
        ),
        in_specs=[smem, vmem, vmem, vmem, vmem, vmem],
        out_specs=(vmem, vmem),
        scratch_shapes=[pltpu.VMEM(kept.shape[1:], f32)],
        compiler_params=pltpu.CompilerParams(vmem_limit_bytes=SMALL),
        cost_estimate=small(32 << 20, 9 << 20),
        name="extra_fields",
    )(helper_tile, *near_memory(extra_fields, extra_noise), moments, kept, received)


def heavy(bits, piece_count, helper, base, noise, grad, near, far, *refs):
    pieces, (_, new_base, stress, fields, rows, answer, sems) = refs[:piece_count], refs[piece_count:]
    _, _, tiles, _, count, cells = base.shape
    slots = helper.shape[1]
    me = lax.axis_index("gy")
    depth = cells // LANES
    groups = count // (2 * SUB)

    def store(h, tile):
        return pltpu.make_async_copy(fields.at[h], new_base.at[0, 0, tile], sems.at[h])

    def result(x):
        target = stress.at[0, 0, :, :, pl.ds(x * LANES, LANES)]
        return pltpu.make_async_copy(rows.at[x], target, sems.at[slots + x])

    at = 0
    for piece in pieces:
        rows[:, :, at : at + piece.shape[2], :] = piece[...]
        at += piece.shape[2]
    found = owned_slots(tiles, me, helper)
    for h, owned, tile in found:

        @pl.when(owned)
        def _(h=h, tile=tile):
            flips = me ^ h
            place = sum(((flips >> (bits - 1 - i)) & 1) << i for i in range(bits))
            is_far = place >= slots // 2
            place = place & (slots // 2 - 1)
            for i in range(near.shape[1]):
                answer[i] = jnp.where(is_far, far[place, i], near[place, i])

            def body(x):
                lanes = pl.ds(pl.multiple_of(x * LANES, LANES), LANES)
                g = tile_grad(grad, depth, tile, x)
                matrices = [with_diagonal(g, wide(answer[s, pl.ds(x, 1), :])) for s in range(2)]
                sums = [jnp.zeros((SUB, LANES), f32)] * 6
                for group in range(groups):
                    pairs = [
                        noise_rows(lambda a, r: noise[0, 0, tile, s, a, r, lanes], group * 2 * SUB) for s in range(2)
                    ]
                    for half in range(2):
                        part = pl.ds((2 * group + half) * SUB, SUB)
                        q = [base[0, 0, tile, a, part, lanes] for a in range(3)]
                        for s in range(2):
                            q = stepped(q, pairs[s][half], matrices[s])
                        for a in range(3):
                            fields[h, a, part, lanes] = q[a]
                        sums = add_moments(sums, q)
                sums = [column_sum(s) + answer[2 + i, pl.ds(x, 1), :] for i, s in enumerate(sums)]
                for i, row in enumerate(stress_rows(sums, 1.0 / float(ALL_FIELDS))):
                    rows[x, i, pl.ds(tile, 1), :] = row

            @pl.loop(0, depth // 2)
            def _(x):
                body(2 * x)
                body(2 * x + 1)

            store(h, tile).start()

    for x in range(depth):
        result(x).start()
    for h, owned, tile in found:

        @pl.when(owned)
        def _(h=h, tile=tile):
            store(h, tile).wait()

    for x in range(depth):
        result(x).wait()


def call_heavy(bits, helper_tile, base_fields, base_noise, grad, near, far, pieces, new_base):
    _, _, tiles, _, count, cells = base_fields.shape
    depth = cells // LANES
    slots = helper_tile.shape[1]
    return pl.pallas_call(
        functools.partial(heavy, bits, len(pieces)),
        out_shape=(
            jax.ShapeDtypeStruct(new_base.shape, f32),
            jax.ShapeDtypeStruct((1, 1, 6, tiles, cells), f32),
        ),
        in_specs=[smem] + [vmem] * (5 + len(pieces)) + [hbm],
        out_specs=(hbm, hbm),
        input_output_aliases={6 + len(pieces): 0},
        scratch_shapes=[
            pltpu.VMEM((slots, 3, count, cells), f32),
            pltpu.VMEM((depth, 6, tiles, LANES), f32),
            pltpu.VMEM(near.shape[1:], f32),
            pltpu.SemaphoreType.DMA((slots + depth,)),
        ],
        compiler_params=pltpu.CompilerParams(vmem_limit_bytes=SMALL),
        cost_estimate=small(8 << 20, 4 << 20),
        name="heavy_tiles",
    )(helper_tile, *near_memory(base_fields, base_noise), grad, near, far, *pieces, new_base)


def both_ways(last, first, axis):
    size = lax.axis_size(axis)
    up = [(i, i + 1) for i in range(size - 1)]
    down = [(i + 1, i) for i in range(size - 1)]
    return lax.ppermute(last, axis, up), lax.ppermute(first, axis, down)


def per_device(
    velocity, wall_cells, tile_counts, helper_tile, base_fields, extra_fields, base_noise, extra_noise
):
    tiles = tile_counts.shape[2]
    bits = lax.axis_size("gy").bit_length() - 1
    x_last, x_first, y_last, y_first = call_edges(helper_tile, velocity)
    halos = both_ways(x_last, x_first, "gx") + both_ways(y_last, y_first, "gy")
    moments = call_heavy_moments(helper_tile, base_fields, base_noise)
    grad, keep, send = call_gradients(tiles, helper_tile, velocity, halos, wall_cells, moments)
    gaps = 2 * bits - 2
    new_base, pieces, done = None, [], 0

    def fill(before):
        nonlocal new_base, done
        here = (tiles - done) // (gaps - len(pieces))
        new_base, piece = call_ordinary(done, here, tile_counts, before, base_fields, base_noise, grad, new_base)
        pieces.append(piece)
        done += here
        return piece

    for bit in range(bits):
        received = swapped(send, bit)
        if bit == 1:
            before = extra_sums = call_extra_moments(send, extra_fields, extra_noise)
        else:
            before = fill(send)
        if bit < bits - 1:
            keep, send = call_merge(tiles, bit, helper_tile, before, keep, received)
    new_extra, reply = call_extra(tiles, bits - 1, helper_tile, extra_fields, extra_noise, extra_sums, keep, received)
    near = reply[None]
    for bit in range(bits - 1, 0, -1):
        received = swapped(near, bit)
        near = call_join(fill(near), near, received)
    far = swapped(near, 0)
    new_base, stress = call_heavy(bits, helper_tile, base_fields, base_noise, grad, near, far, pieces, new_base)
    return new_base, new_extra, jnp.swapaxes(stress, 2, 3)


def solution(mesh):
    in_specs = (
        P(None, "gx", "gy", None),
        P("gx", "gy", None),
        P("gx", "gy", None),
        P("gx", None),
        P("gx", "gy", None, None, None, None),
        P("gx", "gy", None, None, None),
        P("gx", "gy", None, None, None, None, None),
        P("gx", "gy", None, None, None, None),
    )
    out_specs = (
        P("gx", "gy", None, None, None, None),
        P("gx", "gy", None, None, None),
        P("gx", "gy", None, None, None),
    )
    return jax.shard_map(
        per_device, mesh=mesh, in_specs=in_specs, out_specs=out_specs, check_vma=False
    )
```

time: 53.4 us -> 51.3 us (0.961)
  the two profiles are of different devices: /device:TPU:15 before, /device:TPU:25 now
where the time goes in v1:
time: 51.3 us; the launch traced here: 50.8 us
  starting transfers between devices  21.9 us (43%)
  Pallas kernels  19.5 us (38%)
  waiting for transfers between devices  4.69 us (9%)
  local copies, waits for them, and re-layouts  3.78 us (7%)
  between operations  0.91 us (2%)
    ppermute x4, starting transfers between devices, both_ways(): return (lax.ppermute(last, axis, up), lax.ppermute(first, axis, down))  11.8 us
    pallas_call x4, Pallas kernels, call_ordinary(): pl.pallas_call(body, out_shape=(jax.ShapeDtypeStruct(base_fields.shape, f...  10.1 us
    ppermute x6, starting transfers between devices, swapped(): return lax.ppermute(block, 'gy', [(i, i ^ 1 << bit) for i in range(size)])  10.1 us
    unnamed x23, local copies, waits for them, and re-layouts  3.78 us
    ppermute x6, waiting for transfers between devices, swapped(): return lax.ppermute(block, 'gy', [(i, i ^ 1 << bit) for i in range(size)])  3.17 us
    pallas_call x1, Pallas kernels, call_extra(): pl.pallas_call(functools.partial(extra, tiles, bit, 7), out_shape=(pltpu....  2.81 us
    ppermute x4, waiting for transfers between devices, both_ways(): return (lax.ppermute(last, axis, up), lax.ppermute(first, axis, down))  1.51 us
    pallas_call x1, Pallas kernels, call_heavy(): pl.pallas_call(functools.partial(heavy, bits, len(pieces)), out_shape=(ja...  1.46 us
  transfers between devices with their start and end apart: 10, of which 4 were waited for; matrix products, arithmetic and copies ran while one was open for 3% of the time, Pallas kernels for 24%

profile of v1, /device:TPU:25, one launch (start us, length us, event | category | flops | bytes accessed | tf_op | source)
XLA Modules:
  0.0 50.8 jit_solution(9382226623936710689)
XLA Ops:
  0.6 0.9 %copy-done.4 = f32[3,8,8,128]{3,2,1,0:T(8,128)S(1)} copy-done((f32[3,8,8,128]{3,2,1,0:T(8,128)S(1)}, f32[3,8,8,128]{3,2,1,0:T(8,128)}, u32[]{:S(2)}) %copy-start.4) | copy-done | bytes 98328
  1.5 0.7 %copy-done.7 = s32[1,8]{1,0:T(1,128)S(1)} copy-done((s32[1,8]{1,0:T(1,128)S(1)}, s32[1,8]{1,0:T(1,128)}, u32[]{:S(2)}) %copy-start.7) | copy-done | bytes 56
  2.2 0.6 %edges.1 = (f32[3,8,128]{2,1,0:T(8,128)S(1)}, f32[3,8,128]{2,1,0:T(8,128)S(1)}, f32[3,8,128]{2,1,0:T(8,128)S(1)}, f32[3,8,128]{2,1,0:T(8,128)S(1)}) custom-call(s32[1,8]{1,0:T(1,128)S(1)} %copy-done.7, f32[3,8,8,128]{3,2,1,0:T(8,128)S(1)} %copy-done.4), custom_call_target="tpu_custom_call" | custom-call | flops 1024 | bytes 131072 | tf_op jit(solution)/shard_map/edges/pallas_call | solution.py:134
  2.7 1.3 %collective-permute-start = (f32[3,8,128]{2,1,0:T(8,128)S(1)}, f32[3,8,128]{2,1,0:T(8,128)S(1)}, u32[]{:S(2)}, u32[]{:S(2)}) collective-permute-start(f32[3,8,128]{2,1,0:T(8,128)S(1)} %get-tuple-element.26), channel_id=1, source_target_pairs={{0,8},{8,16},{16,24},{1,9},{9,17},{17,25},{2,10},{10,18},{18,26},{... | collective-permute-start | bytes 36872 | tf_op jit(solution)/shard_map/ppermute | solution.py:611
  4.0 4.0 %collective-permute-start.1 = (f32[3,8,128]{2,1,0:T(8,128)S(1)}, f32[3,8,128]{2,1,0:T(8,128)S(1)}, u32[]{:S(2)}, u32[]{:S(2)}) collective-permute-start(f32[3,8,128]{2,1,0:T(8,128)S(1)} %get-tuple-element.27), channel_id=1, source_target_pairs={{8,0},{16,8},{24,16},{9,1},{17,9},{25,17},{10,2},{18,10},{26,18},{... | collective-permute-start | bytes 36872 | tf_op jit(solution)/shard_map/ppermute | solution.py:611
  8.0 4.2 %collective-permute-start.2 = (f32[3,8,128]{2,1,0:T(8,128)S(1)}, f32[3,8,128]{2,1,0:T(8,128)S(1)}, u32[]{:S(2)}, u32[]{:S(2)}) collective-permute-start(f32[3,8,128]{2,1,0:T(8,128)S(1)} %get-tuple-element.28), channel_id=1, source_target_pairs={{0,1},{1,2},{2,3},{3,4},{4,5},{5,6},{6,7},{8,9},{9,10},{10,11},{11... | collective-permute-start | bytes 36872 | tf_op jit(solution)/shard_map/ppermute | solution.py:611
  12.3 0.0 copy-start.5
  12.3 0.0 copy-start.1
  12.3 2.3 %collective-permute-start.3 = (f32[3,8,128]{2,1,0:T(8,128)S(1)}, f32[3,8,128]{2,1,0:T(8,128)S(1)}, u32[]{:S(2)}, u32[]{:S(2)}) collective-permute-start(f32[3,8,128]{2,1,0:T(8,128)S(1)} %get-tuple-element.29), channel_id=1, source_target_pairs={{1,0},{2,1},{3,2},{4,3},{5,4},{6,5},{7,6},{9,8},{10,9},{11,10},{12... | collective-permute-start | bytes 36872 | tf_op jit(solution)/shard_map/ppermute | solution.py:611
  14.7 0.6 %copy-done.8 = s32[1,8]{1,0:T(1,128)S(1)} copy-done((s32[1,8]{1,0:T(1,128)S(1)}, s32[1,8]{1,0:T(1,128)}, u32[]{:S(2)}) %copy-start.8) | copy-done | bytes 56
  15.3 0.7 %heavy_moments.1.moments = f32[8,16,8,128]{3,2,1,0:T(8,128)S(1)} custom-call(s32[1,8]{1,0:T(1,128)S(1)} %copy-done.8, f32[1,1,8,3,32,1024]{5,4,3,2,1,0:T(8,128)} %base.13, bf16[1,1,8,2,3,32,1024]{6,5,4,3,2,1,0:T(8,128)(2,1)} %noise.13), custom_call_target="tpu_custom_call" | custom-call | flops 8388608 | bytes 3145728 | tf_op jit(solution)/shard_map/heavy_moments/pallas_call | solution.py:187
  16.1 1.5 %collective-permute-done.3.y_high = f32[3,8,128]{2,1,0:T(8,128)S(1)} collective-permute-done((f32[3,8,128]{2,1,0:T(8,128)S(1)}, f32[3,8,128]{2,1,0:T(8,128)S(1)}, u32[]{:S(2)}, u32[]{:S(2)}) %collective-permute-start.3) | collective-permute-done | bytes 12320 | tf_op jit(solution)/shard_map/ppermute | solution.py:611
  17.6 1.2 %gradients.1 = (f32[576,128]{1,0:T(8,128)S(1)}, f32[4,12,8,128]{3,2,1,0:T(8,128)S(1)}, f32[4,12,8,128]{3,2,1,0:T(8,128)S(1)}) custom-call(s32[1,8]{1,0:T(1,128)S(1)} %copy-done.8, f32[3,8,8,128]{3,2,1,0:T(8,128)S(1)} %copy-done.5, f32[3,8,128]{2,1,0:T(8,128)S(1)} %collective-permute-done.x_low, f32[3,8,128]{2,1,0:T(8,128)S(1)} %collective-permute-done.1.x_high, ...), custom_call_target="tpu_custom_call" | custom-call | flops 4194304 | bytes 1048576 | tf_op jit(solution)/shard_map/gradients/pallas_call | solution.py:285
  18.8 0.1 collective-permute-start.4
  18.9 2.5 %ordinary_tiles.4 = (f32[1,1,8,3,32,1024]{5,4,3,2,1,0:T(8,128)}, f32[8,6,2,128]{3,2,1,0:T(2,128)S(1)}) custom-call(s32[1,1,8]{2,1,0:T(1,128)S(1)} %copy-done.10, f32[4,12,8,128]{3,2,1,0:T(8,128)S(1)} %get-tuple-element.31.refs_1_, f32[1,1,8,3,32,1024]{5,4,3,2,1,0:T(8,128)S(1)} %copy-done, bf16[1,1,8,2,3,32,1024]{6,5,4,3,2,1,0:T(8,128)(2,1)S(1)} %copy-done.1, ...), custom_call_target="tpu_custom_call" | custom-call | flops 8388608 | bytes 3145728 | tf_op jit(solution)/shard_map/ordinary_tiles/pallas_call | solution.py:435
  21.5 0.7 %merge.2 = (f32[2,12,8,128]{3,2,1,0:T(8,128)S(1)}, f32[2,12,8,128]{3,2,1,0:T(8,128)S(1)}) custom-call(s32[1,8]{1,0:T(1,128)S(1)} %copy-done.8, f32[8,6,2,128]{3,2,1,0:T(2,128)S(1)} %get-tuple-element.32.before.refs_0_, f32[4,12,8,128]{3,2,1,0:T(8,128)S(1)} %get-tuple-element.33.kept, f32[4,12,8,128]{3,2,1,0:T(8,128)S(1)} %collective-permute-done.4.received), custom_call_target="tpu_custom_call" | custom-call | flops 1024 | bytes 262144 | tf_op jit(solution)/shard_map/merge/pallas_call | solution.py:324
  22.1 2.2 %collective-permute-start.5 = (f32[2,12,8,128]{3,2,1,0:T(8,128)S(1)}, f32[2,12,8,128]{3,2,1,0:T(8,128)S(1)}, u32[]{:S(2)}, u32[]{:S(2)}) collective-permute-start(f32[2,12,8,128]{3,2,1,0:T(8,128)S(1)} %get-tuple-element.34.before), channel_id=1, source_target_pairs={{0,2},{1,3},{2,0},{3,1},{4,6},{5,7},{6,4},{7,5},{8,10},{9,11},{10,... | collective-permute-start | bytes 294920 | tf_op jit(solution)/shard_map/ppermute | solution.py:298
  24.3 1.4 %extra_moments.1.before.moments = f32[16,8,128]{2,1,0:T(8,128)S(1)} custom-call(f32[2,12,8,128]{3,2,1,0:T(8,128)S(1)} %get-tuple-element.34.before, f32[1,1,3,224,1024]{4,3,2,1,0:T(8,128)S(1)} %copy-done.2, bf16[1,1,2,3,224,1024]{5,4,3,2,1,0:T(8,128)(2,1)S(1)} %copy-done.3), custom_call_target="tpu_custom_call" | custom-call | flops 8388608 | bytes 5242880 | tf_op jit(solution)/shard_map/extra_moments/pallas_call | solution.py:225
  25.7 1.3 %collective-permute-done.5.received = f32[2,12,8,128]{3,2,1,0:T(8,128)S(1)} collective-permute-done((f32[2,12,8,128]{3,2,1,0:T(8,128)S(1)}, f32[2,12,8,128]{3,2,1,0:T(8,128)S(1)}, u32[]{:S(2)}, u32[]{:S(2)}) %collective-permute-start.5) | collective-permute-done | bytes 98336 | tf_op jit(solution)/shard_map/ppermute | solution.py:298
  27.1 0.6 %merge.3 = (f32[1,12,8,128]{3,2,1,0:T(8,128)S(1)}, f32[1,12,8,128]{3,2,1,0:T(8,128)S(1)}) custom-call(s32[1,8]{1,0:T(1,128)S(1)} %copy-done.8, f32[16,8,128]{2,1,0:T(8,128)S(1)} %extra_moments.1.before.moments, f32[2,12,8,128]{3,2,1,0:T(8,128)S(1)} %get-tuple-element.35.kept, f32[2,12,8,128]{3,2,1,0:T(8,128)S(1)} %collective-permute-done.5.received), custom_call_target="tpu_custom_call" | custom-call | flops 1024 | bytes 262144 | tf_op jit(solution)/shard_map/merge/pallas_call | solution.py:324
  27.7 3.2 %collective-permute-start.6 = (f32[1,12,8,128]{3,2,1,0:T(8,128)S(1)}, f32[1,12,8,128]{3,2,1,0:T(8,128)S(1)}, u32[]{:S(2)}, u32[]{:S(2)}) collective-permute-start(f32[1,12,8,128]{3,2,1,0:T(8,128)S(1)} %get-tuple-element.37.before), channel_id=1, source_target_pairs={{0,4},{1,5},{2,6},{3,7},{4,0},{5,1},{6,2},{7,3},{8,12},{9,13},{10,... | collective-permute-start | bytes 147464 | tf_op jit(solution)/shard_map/ppermute | solution.py:298
  30.9 1.5 %collective-permute-done.6.received = f32[1,12,8,128]{3,2,1,0:T(8,128)S(1)} collective-permute-done((f32[1,12,8,128]{3,2,1,0:T(8,128)S(1)}, f32[1,12,8,128]{3,2,1,0:T(8,128)S(1)}, u32[]{:S(2)}, u32[]{:S(2)}) %collective-permute-start.6) | collective-permute-done | bytes 49184 | tf_op jit(solution)/shard_map/ppermute | solution.py:298
  32.4 2.8 %extra_fields.1 = (f32[1,1,3,224,1024]{4,3,2,1,0:T(8,128)S(1)}, f32[8,8,128]{2,1,0:T(8,128)S(1)}) custom-call(s32[1,8]{1,0:T(1,128)S(1)} %copy-done.8, f32[1,1,3,224,1024]{4,3,2,1,0:T(8,128)S(1)} %copy-done.2, bf16[1,1,2,3,224,1024]{5,4,3,2,1,0:T(8,128)(2,1)S(1)} %copy-done.3, f32[16,8,128]{2,1,0:T(8,128)S(1)} %extra_moments.1.before.moments, ...), custom_call_target="tpu_custom_call" | custom-call | flops 33554432 | bytes 9437184 | tf_op jit(solution)/shard_map/extra_fields/pallas_call | solution.py:496
  35.2 1.5 %collective-permute-start.7 = (f32[1,8,8,128]{3,2,1,0:T(8,128)S(1)}, f32[1,8,8,128]{3,2,1,0:T(8,128)S(1)}, u32[]{:S(2)}, u32[]{:S(2)}) collective-permute-start(f32[1,8,8,128]{3,2,1,0:T(8,128)S(1)} %bitcast.2), channel_id=1, source_target_pairs={{0,4},{1,5},{2,6},{3,7},{4,0},{5,1},{6,2},{7,3},{8,12},{9,13},{10,... | collective-permute-start | bytes 98312 | tf_op jit(solution)/shard_map/ppermute | solution.py:298
  36.7 2.5 %ordinary_tiles.5 = (f32[1,1,8,3,32,1024]{5,4,3,2,1,0:T(8,128)}, f32[8,6,2,128]{3,2,1,0:T(2,128)S(1)}) custom-call(s32[1,1,8]{2,1,0:T(1,128)S(1)} %copy-done.10, f32[1,12,8,128]{3,2,1,0:T(8,128)S(1)} %get-tuple-element.37.before, f32[1,1,8,3,32,1024]{5,4,3,2,1,0:T(8,128)S(1)} %copy-done, ...), custom_call_target="tpu_custom_call", output_to_operand_aliasing={{0}: (5, {})} | custom-call | flops 8388608 | bytes 3145728 | tf_op jit(solution)/shard_map/ordinary_tiles/pallas_call | solution.py:435
  39.2 2.5 %ordinary_tiles.6 = (f32[1,1,8,3,32,1024]{5,4,3,2,1,0:T(8,128)}, f32[8,6,2,128]{3,2,1,0:T(2,128)S(1)}) custom-call(s32[1,1,8]{2,1,0:T(1,128)S(1)} %copy-done.10, f32[1,8,8,128]{3,2,1,0:T(8,128)S(1)} %bitcast.3, f32[1,1,8,3,32,1024]{5,4,3,2,1,0:T(8,128)S(1)} %copy-done, ...), custom_call_target="tpu_custom_call", output_to_operand_aliasing={{0}: (5, {})} | custom-call | flops 8388608 | bytes 3145728 | tf_op jit(solution)/shard_map/ordinary_tiles/pallas_call | solution.py:435
  41.8 0.3 collective-permute-start.8
  42.1 2.5 %ordinary_tiles.7 = (f32[1,1,8,3,32,1024]{5,4,3,2,1,0:T(8,128)}, f32[8,6,2,128]{3,2,1,0:T(2,128)S(1)}) custom-call(s32[1,1,8]{2,1,0:T(1,128)S(1)} %copy-done.10, f32[2,8,8,128]{3,2,1,0:T(8,128)S(1)} %join.2.before.first, f32[1,1,8,3,32,1024]{5,4,3,2,1,0:T(8,128)S(1)} %copy-done, ...), custom_call_target="tpu_custom_call", output_to_operand_aliasing={{0}: (5, {})} | custom-call | flops 8388608 | bytes 3145728 | tf_op jit(solution)/shard_map/ordinary_tiles/pallas_call | solution.py:435
  44.6 0.4 collective-permute-done.8.second
  45.0 2.8 %collective-permute-start.9 = (f32[4,8,8,128]{3,2,1,0:T(8,128)S(1)}, f32[4,8,8,128]{3,2,1,0:T(8,128)S(1)}, u32[]{:S(2)}, u32[]{:S(2)}) collective-permute-start(f32[4,8,8,128]{3,2,1,0:T(8,128)S(1)} %join.3.near), channel_id=1, source_target_pairs={{0,1},{1,0},{2,3},{3,2},{4,5},{5,4},{6,7},{7,6},{8,9},{9,8},{10,11... | collective-permute-start | bytes 393224 | tf_op jit(solution)/shard_map/ppermute | solution.py:298
  47.8 1.5 %copy.19 = f32[1,1,3,224,1024]{4,3,2,1,0:T(8,128)} copy(f32[1,1,3,224,1024]{4,3,2,1,0:T(8,128)S(1)} %get-tuple-element.50) | data formatting | bytes 5505024
  49.4 1.5 %heavy_tiles.1 = (f32[1,1,8,3,32,1024]{5,4,3,2,1,0:T(8,128)}, f32[1,1,6,8,1024]{4,3,2,1,0:T(8,128)}) custom-call(s32[1,8]{1,0:T(1,128)S(1)} %copy-done.9, f32[1,1,8,3,32,1024]{5,4,3,2,1,0:T(8,128)S(1)} %copy-done, bf16[1,1,8,2,3,32,1024]{6,5,4,3,2,1,0:T(8,128)(2,1)S(1)} %copy-done.1, ...), custom_call_target="tpu_custom_call", output_to_operand_aliasing={{0}: (10, {})} | custom-call | flops 8388608 | bytes 4194304 | tf_op jit(solution)/shard_map/heavy_tiles/pallas_call | solution.py:586
  (25 shorter events, 0.1 us)
Async XLA Ops:
  0.6 0.9 %copy-start.4 = (f32[3,8,8,128]{3,2,1,0:T(8,128)S(1)}, f32[3,8,8,128]{3,2,1,0:T(8,128)}, u32[]{:S(2)}) copy-start(f32[3,8,8,128]{3,2,1,0:T(8,128)} %velocity.3) | copy-start | bytes 294916
  1.5 0.7 %copy-start.7 = (s32[1,8]{1,0:T(1,128)S(1)}, s32[1,8]{1,0:T(1,128)}, u32[]{:S(2)}) copy-start(s32[1,8]{1,0:T(1,128)} %helper.13) | copy-start | bytes 100
  2.7 13.3 %collective-permute-start = (f32[3,8,128]{2,1,0:T(8,128)S(1)}, f32[3,8,128]{2,1,0:T(8,128)S(1)}, u32[]{:S(2)}, u32[]{:S(2)}) collective-permute-start(f32[3,8,128]{2,1,0:T(8,128)S(1)} %get-tuple-element.26), channel_id=1, source_target_pairs={{0,8},{8,16},{16,24},{1,9},{9,17},{17,25},{2,10},{10,18},{18,26},{... | collective-permute-start | bytes 36872 | tf_op jit(solution)/shard_map/ppermute | solution.py:611
  4.0 12.0 %collective-permute-start.1 = (f32[3,8,128]{2,1,0:T(8,128)S(1)}, f32[3,8,128]{2,1,0:T(8,128)S(1)}, u32[]{:S(2)}, u32[]{:S(2)}) collective-permute-start(f32[3,8,128]{2,1,0:T(8,128)S(1)} %get-tuple-element.27), channel_id=1, source_target_pairs={{8,0},{16,8},{24,16},{9,1},{17,9},{25,17},{10,2},{18,10},{26,18},{... | collective-permute-start | bytes 36872 | tf_op jit(solution)/shard_map/ppermute | solution.py:611
  8.0 8.1 %collective-permute-start.2 = (f32[3,8,128]{2,1,0:T(8,128)S(1)}, f32[3,8,128]{2,1,0:T(8,128)S(1)}, u32[]{:S(2)}, u32[]{:S(2)}) collective-permute-start(f32[3,8,128]{2,1,0:T(8,128)S(1)} %get-tuple-element.28), channel_id=1, source_target_pairs={{0,1},{1,2},{2,3},{3,4},{4,5},{5,6},{6,7},{8,9},{9,10},{10,11},{11... | collective-permute-start | bytes 36872 | tf_op jit(solution)/shard_map/ppermute | solution.py:611
  12.3 5.3 %copy-start.5 = (f32[3,8,8,128]{3,2,1,0:T(8,128)S(1)}, f32[3,8,8,128]{3,2,1,0:T(8,128)}, u32[]{:S(2)}) copy-start(f32[3,8,8,128]{3,2,1,0:T(8,128)} %velocity.3) | copy-start | bytes 294916
  12.3 5.3 %copy-start.6 = (s32[8,8,128]{2,1,0:T(8,128)S(1)}, s32[8,8,128]{2,1,0:T(8,128)}, u32[]{:S(2)}) copy-start(s32[8,8,128]{2,1,0:T(8,128)} %wall.1) | copy-start | bytes 98308
  12.3 6.5 %copy-start = (f32[1,1,8,3,32,1024]{5,4,3,2,1,0:T(8,128)S(1)}, f32[1,1,8,3,32,1024]{5,4,3,2,1,0:T(8,128)}, u32[]{:S(2)}) copy-start(f32[1,1,8,3,32,1024]{5,4,3,2,1,0:T(8,128)} %base.13) | copy-start | bytes 9437188
  12.3 6.5 %copy-start.1 = (bf16[1,1,8,2,3,32,1024]{6,5,4,3,2,1,0:T(8,128)(2,1)S(1)}, bf16[1,1,8,2,3,32,1024]{6,5,4,3,2,1,0:T(8,128)(2,1)}, u32[]{:S(2)}) copy-start(bf16[1,1,8,2,3,32,1024]{6,5,4,3,2,1,0:T(8,128)(2,1)} %noise.13) | copy-start | bytes 9437188
  12.3 5.3 %collective-permute-start.3 = (f32[3,8,128]{2,1,0:T(8,128)S(1)}, f32[3,8,128]{2,1,0:T(8,128)S(1)}, u32[]{:S(2)}, u32[]{:S(2)}) collective-permute-start(f32[3,8,128]{2,1,0:T(8,128)S(1)} %get-tuple-element.29), channel_id=1, source_target_pairs={{1,0},{2,1},{3,2},{4,3},{5,4},{6,5},{7,6},{9,8},{10,9},{11,10},{12... | collective-permute-start | bytes 36872 | tf_op jit(solution)/shard_map/ppermute | solution.py:611
  14.7 0.7 %copy-start.8 = (s32[1,8]{1,0:T(1,128)S(1)}, s32[1,8]{1,0:T(1,128)}, u32[]{:S(2)}) copy-start(s32[1,8]{1,0:T(1,128)} %helper.13) | copy-start | bytes 100
  15.3 3.6 %copy-start.10 = (s32[1,1,8]{2,1,0:T(1,128)S(1)}, s32[1,1,8]{2,1,0:T(1,128)}, u32[]{:S(2)}) copy-start(s32[1,1,8]{2,1,0:T(1,128)} %counts.5) | copy-start | bytes 100
  18.8 2.7 %collective-permute-start.4 = (f32[4,12,8,128]{3,2,1,0:T(8,128)S(1)}, f32[4,12,8,128]{3,2,1,0:T(8,128)S(1)}, u32[]{:S(2)}, u32[]{:S(2)}) collective-permute-start(f32[4,12,8,128]{3,2,1,0:T(8,128)S(1)} %get-tuple-element.31.refs_1_), channel_id=1, source_target_pairs={{0,1},{1,0},{2,3},{3,2},{4,5},{5,4},{6,7},{7,6},{8,9},{9,8},{10,11... | collective-permute-start | bytes 589832 | tf_op jit(solution)/shard_map/ppermute | solution.py:298
  18.9 5.4 %copy-start.2 = (f32[1,1,3,224,1024]{4,3,2,1,0:T(8,128)S(1)}, f32[1,1,3,224,1024]{4,3,2,1,0:T(8,128)}, u32[]{:S(2)}) copy-start(f32[1,1,3,224,1024]{4,3,2,1,0:T(8,128)} %base.9) | copy-start | bytes 8257540
  18.9 5.4 %copy-start.3 = (bf16[1,1,2,3,224,1024]{5,4,3,2,1,0:T(8,128)(2,1)S(1)}, bf16[1,1,2,3,224,1024]{5,4,3,2,1,0:T(8,128)(2,1)}, u32[]{:S(2)}) copy-start(bf16[1,1,2,3,224,1024]{5,4,3,2,1,0:T(8,128)(2,1)} %noise.9) | copy-start | bytes 8257540
  22.1 4.9 %collective-permute-start.5 = (f32[2,12,8,128]{3,2,1,0:T(8,128)S(1)}, f32[2,12,8,128]{3,2,1,0:T(8,128)S(1)}, u32[]{:S(2)}, u32[]{:S(2)}) collective-permute-start(f32[2,12,8,128]{3,2,1,0:T(8,128)S(1)} %get-tuple-element.34.before), channel_id=1, source_target_pairs={{0,2},{1,3},{2,0},{3,1},{4,6},{5,7},{6,4},{7,5},{8,10},{9,11},{10,... | collective-permute-start | bytes 294920 | tf_op jit(solution)/shard_map/ppermute | solution.py:298
  27.7 4.7 %collective-permute-start.6 = (f32[1,12,8,128]{3,2,1,0:T(8,128)S(1)}, f32[1,12,8,128]{3,2,1,0:T(8,128)S(1)}, u32[]{:S(2)}, u32[]{:S(2)}) collective-permute-start(f32[1,12,8,128]{3,2,1,0:T(8,128)S(1)} %get-tuple-element.37.before), channel_id=1, source_target_pairs={{0,4},{1,5},{2,6},{3,7},{4,0},{5,1},{6,2},{7,3},{8,12},{9,13},{10,... | collective-permute-start | bytes 147464 | tf_op jit(solution)/shard_map/ppermute | solution.py:298
  35.2 6.6 %collective-permute-start.7 = (f32[1,8,8,128]{3,2,1,0:T(8,128)S(1)}, f32[1,8,8,128]{3,2,1,0:T(8,128)S(1)}, u32[]{:S(2)}, u32[]{:S(2)}) collective-permute-start(f32[1,8,8,128]{3,2,1,0:T(8,128)S(1)} %bitcast.2), channel_id=1, source_target_pairs={{0,4},{1,5},{2,6},{3,7},{4,0},{5,1},{6,2},{7,3},{8,12},{9,13},{10,... | collective-permute-start | bytes 98312 | tf_op jit(solution)/shard_map/ppermute | solution.py:298
  41.8 3.2 %collective-permute-start.8 = (f32[2,8,8,128]{3,2,1,0:T(8,128)S(1)}, f32[2,8,8,128]{3,2,1,0:T(8,128)S(1)}, u32[]{:S(2)}, u32[]{:S(2)}) collective-permute-start(f32[2,8,8,128]{3,2,1,0:T(8,128)S(1)} %join.2.before.first), channel_id=1, source_target_pairs={{0,2},{1,3},{2,0},{3,1},{4,6},{5,7},{6,4},{7,5},{8,10},{9,11},{10,... | collective-permute-start | bytes 196616 | tf_op jit(solution)/shard_map/ppermute | solution.py:298
  44.6 4.8 %copy-start.9 = (s32[1,8]{1,0:T(1,128)S(1)}, s32[1,8]{1,0:T(1,128)}, u32[]{:S(2)}) copy-start(s32[1,8]{1,0:T(1,128)} %helper.13) | copy-start | bytes 100
  45.0 4.4 %collective-permute-start.9 = (f32[4,8,8,128]{3,2,1,0:T(8,128)S(1)}, f32[4,8,8,128]{3,2,1,0:T(8,128)S(1)}, u32[]{:S(2)}, u32[]{:S(2)}) collective-permute-start(f32[4,8,8,128]{3,2,1,0:T(8,128)S(1)} %join.3.near), channel_id=1, source_target_pairs={{0,1},{1,0},{2,3},{3,2},{4,5},{5,4},{6,7},{7,6},{8,9},{9,8},{10,11... | collective-permute-start | bytes 393224 | tf_op jit(solution)/shard_map/ppermute | solution.py:298

commit v2 on v1

--- a/solution.py
+++ b/solution.py
@@ -37,6 +37,19 @@
 
 def column_sum(value):
     return jnp.sum(value, axis=0, keepdims=True)
+
+
+def packed_sum(values):
+    sub = lax.broadcasted_iota(jnp.int32, (SUB, LANES), 0)
+    bit = 1
+    while len(values) > 1:
+        low = (sub & bit) == 0
+        values = [
+            jnp.where(low, a, b) + pltpu.roll(jnp.where(low, b, a), bit, 0)
+            for a, b in zip(values[0::2], values[1::2])
+        ]
+        bit *= 2
+    return values[0]
 
 
 def wide(row):
@@ -117,29 +130,52 @@
     return pl.CostEstimate(flops=flops, bytes_accessed=traffic, transcendentals=0)
 
 
-def edges(helper, velocity, x_last, x_first, y_last, y_first):
+def is_even(axis):
+    return (lax.axis_index(axis) & 1) == 0
+
+
+def edges(velocity, x_one, x_two, y_one, y_two):
     depth, width = velocity.shape[1:3]
+    even = is_even("gx")
     for a in range(3):
-        x_last[a] = velocity[a, depth - 1]
-        x_first[a] = velocity[a, 0]
+        first, last = velocity[a, 0], velocity[a, depth - 1]
+        x_one[a] = jnp.where(even, last, first)
+        x_two[a] = jnp.where(even, first, last)
+    even = is_even("gy")
+    for a in range(3):
         for x in range(depth):
-            y_last[a, pl.ds(x, 1), :] = velocity[a, x, pl.ds(width - 1, 1), :]
-            y_first[a, pl.ds(x, 1), :] = velocity[a, x, pl.ds(0, 1), :]
-
-
-def call_edges(helper_tile, velocity):
+            first, last = velocity[a, x, pl.ds(0, 1), :], velocity[a, x, pl.ds(width - 1, 1), :]
+            y_one[a, pl.ds(x, 1), :] = jnp.where(even, last, first)
+            y_two[a, pl.ds(x, 1), :] = jnp.where(even, first, last)
+
+
+def call_edges(velocity):
     _, depth, width, length = velocity.shape
     along_x = jax.ShapeDtypeStruct((3, width, length), f32)
     along_y = jax.ShapeDtypeStruct((3, depth, length), f32)
     return pl.pallas_call(
         edges,
         out_shape=(along_x, along_x, along_y, along_y),
-        in_specs=[smem, vmem],
+        in_specs=[vmem],
         out_specs=(vmem,) * 4,
         compiler_params=pltpu.CompilerParams(vmem_limit_bytes=4 << 20),
         cost_estimate=small(1 << 10, 1 << 17),
         name="edges",
-    )(helper_tile, velocity)
+    )(velocity)
+
+
+def two_swaps(one, two, axis):
+    size = lax.axis_size(axis)
+    within = [(i, i ^ 1) for i in range(size)]
+    across = [(i, min(max(i - 1 + 2 * (i & 1), 0), size - 1)) for i in range(size)]
+    return lax.ppermute(one, axis, within), lax.ppermute(two, axis, across)
+
+
+def low_and_high(axis, one, two, a):
+    even, place = is_even(axis), lax.axis_index(axis)
+    low = jnp.where(even, two[a], one[a])
+    high = jnp.where(even, one[a], two[a])
+    return jnp.where(place == 0, 0.0, low), jnp.where(place == lax.axis_size(axis) - 1, 0.0, high)
 
 
 def heavy_moments(helper, base, noise, out, fields, shocks, sems):
@@ -233,7 +269,7 @@
     )(before, *near_memory(extra_fields, extra_noise))
 
 
-def gradients(tiles, helper, velocity, x_low, x_high, y_low, y_high, wall, moments, grad, keep, send):
+def gradients(tiles, helper, velocity, x_one, x_two, y_one, y_two, wall, moments, grad, keep, send):
     me = lax.axis_index("gy")
     depth = velocity.shape[1]
     cell_z = velocity.shape[3] // tiles
@@ -242,9 +278,11 @@
     z = lane % cell_z
     scales = [turned(jnp.where(wall[x] == 0, 0.5 * time_step, 0.0).astype(f32), cell_z) for x in range(depth)]
     for a in range(3):
-        rows = [x_low[a]] + [velocity[a, x] for x in range(depth)] + [x_high[a]]
+        x_low, x_high = low_and_high("gx", x_one, x_two, a)
+        y_low, y_high = low_and_high("gy", y_one, y_two, a)
+        rows = [x_low] + [velocity[a, x] for x in range(depth)] + [x_high]
         rows = [turned(row, cell_z) for row in rows]
-        low, high = turned(y_low[a], cell_z), turned(y_high[a], cell_z)
+        low, high = turned(y_low, cell_z), turned(y_high, cell_z)
         for x in range(depth):
             here = rows[x + 1]
             above = high if x == depth - 1 else pltpu.roll(high, LANES - cell_z * (x + 1), 1)
@@ -259,6 +297,8 @@
             z_down = jnp.where(z == 0, last_tile, pltpu.roll(here, 1, 1))
             for b, difference in enumerate((rows[x + 2] - rows[x], y_up - y_down, z_up - z_down)):
                 grad[pl.ds(((3 * a + b) * depth + x) * SUB, SUB), :] = difference * scales[x]
+    keep[...] = jnp.zeros(keep.shape, f32)
+    send[...] = jnp.zeros(send.shape, f32)
     for h, owned, tile in owned_slots(tiles, me, helper):
 
         @pl.when(owned)
@@ -298,38 +338,26 @@
     return lax.ppermute(block, "gy", [(i, i ^ (1 << bit)) for i in range(size)])
 
 
-def arrived(tiles, me, helper, slot, bit):
-    owner = helper[0, slot] // tiles
-    return (((owner ^ me) >> bit) & 1) == 1
-
-
-def merge(tiles, bit, helper, before, kept, received, keep, send):
-    me = lax.axis_index("gy")
-    below = me & ((2 << bit) - 1)
-    mine = (me >> (bit + 1)) & 1
-    for j in range(kept.shape[0]):
-        pick = arrived(tiles, me, helper, (j << (bit + 1)) | below, bit)
-        stays = mine == (j & 1)
-        for source, chosen in ((received, pick), (kept, jnp.logical_not(pick))):
-            for out, there in ((keep, stays), (send, jnp.logical_not(stays))):
-
-                @pl.when(chosen & there)
-                def _(j=j, source=source, out=out):
-                    for i in range(kept.shape[1]):
-                        out[j >> 1, i] = source[j, i]
-
-
-def call_merge(tiles, bit, helper_tile, before, kept, received):
+def merge(bit, before, kept, received, keep, send):
+    mine = (lax.axis_index("gy") >> (bit + 1)) & 1
+    for j in range(0, kept.shape[0], 2):
+        for i in range(kept.shape[1]):
+            even, odd = [kept[k, i] + received[k, i] for k in (j, j + 1)]
+            keep[j // 2, i] = jnp.where(mine == 0, even, odd)
+            send[j // 2, i] = jnp.where(mine == 0, odd, even)
+
+
+def call_merge(bit, before, kept, received):
     half = jax.ShapeDtypeStruct((kept.shape[0] // 2,) + kept.shape[1:], f32)
     return pl.pallas_call(
-        functools.partial(merge, tiles, bit),
+        functools.partial(merge, bit),
         out_shape=(half, half),
-        in_specs=[smem, anywhere, vmem, vmem],
+        in_specs=[anywhere, vmem, vmem],
         out_specs=(vmem, vmem),
         compiler_params=pltpu.CompilerParams(vmem_limit_bytes=4 << 20),
         cost_estimate=small(1 << 10, 1 << 18),
         name="merge",
-    )(helper_tile, before, kept, received)
+    )(before, kept, received)
 
 
 def call_join(before, first, second):
@@ -358,110 +386,146 @@
     return [wide(grad[pl.ds((i * depth + x + 1) * SUB - 1 - tile, 1), :]) for i in range(9)]
 
 
-def ordinary(first, counts, before, base, noise, grad, old_base, new_base, stress, halfway, fields, totals, relaxes, sems):
+def tile_sums(read, write, noise, matrices, count, add, many):
+    sums = [jnp.zeros((SUB, LANES), f32)] * many
+    for group in range(count // (2 * SUB)):
+        pairs = [noise_rows(functools.partial(noise, step), group * 2 * SUB) for step in range(len(matrices))]
+        for half in range(2):
+            rows = pl.ds((2 * group + half) * SUB, SUB)
+            q = [read(a, rows) for a in range(3)]
+            for step, matrix in enumerate(matrices):
+                q = stepped(q, pairs[step][half], matrix)
+            for a in range(3):
+                write(a, rows, q[a])
+            sums = add(sums, q)
+    return sums
+
+
+def add_square(sums, q):
+    return [sums[0] + (q[0] * q[0] + q[1] * q[1] + q[2] * q[2])]
+
+
+def ordinary(first, has_block, has_base, has_extra, *refs):
+    refs = list(refs)
+    before, base, noise, grad = refs[:4]
+    del refs[:4]
+    block = refs.pop(0) if has_block else None
+    if has_base:
+        refs.pop(0)
+    extra_near = refs.pop(0) if has_extra else None
+    new_base = refs.pop(0) if has_block else None
+    new_extra = refs.pop(0) if has_extra else None
+    fields, stress, halfway, relaxes, sems = refs
     here, _, count, cells = fields.shape
     depth = cells // LANES
-    groups = count // (2 * SUB)
-    zero = jnp.zeros((SUB, LANES), f32)
-
-    def store(place):
-        return pltpu.make_async_copy(fields.at[place], new_base.at[0, 0, first + place], sems.at[place])
-
+    inverse = 1.0 / count
+    copies = []
+    if has_block:
+        last = block.shape[0]
+        copies += [
+            pltpu.make_async_copy(block.at[i], new_base.at[0, 0, first - last + i], sems.at[i]) for i in range(last)
+        ]
+    if has_extra:
+        copies += [
+            pltpu.make_async_copy(extra_near.at[0, 0, a], new_extra.at[0, 0, a], sems.at[len(copies) + a])
+            for a in range(3)
+        ]
+    for copy in copies:
+        copy.start()
     for place in range(here):
         tile = first + place
-        tile_count = counts[0, 0, tile]
-
-        @pl.when(tile_count != ALL_FIELDS)
-        def _(place=place, tile=tile, tile_count=tile_count):
-            inverse = 1.0 / jnp.full((1, LANES), tile_count.astype(f32))
+        totals = []
+        for x in range(depth):
+            total = jnp.zeros((SUB, LANES), f32)
+            for group in range(count // SUB):
+                for a in range(3):
+                    q = base[0, 0, tile, a, pl.ds(group * SUB, SUB), pl.ds(x * LANES, LANES)]
+                    total = total + q * q
+            totals.append(total)
+        for step in range(2):
+            relaxes[place, step] = relax_of(packed_sum(totals), inverse)
+            totals = []
             for x in range(depth):
-                total = zero
-                for group in range(2 * groups):
-                    for a in range(3):
-                        q = base[0, 0, tile, a, pl.ds(group * SUB, SUB), pl.ds(x * LANES, LANES)]
-                        total = total + q * q
-                totals[pl.ds(x, 1), :] = column_sum(total)
-            for step in range(2):
-                relaxes[...] = relax_of(totals[...], inverse)
-
-                def body(x, step=step):
-                    lanes = pl.ds(pl.multiple_of(x * LANES, LANES), LANES)
-                    matrix = with_diagonal(tile_grad(grad, depth, tile, x), wide(relaxes[pl.ds(x, 1), :]))
-                    sums = [zero] * (1 if step == 0 else 6)
-                    for group in range(groups):
-                        pair = noise_rows(lambda a, rows: noise[0, 0, tile, step, a, rows, lanes], group * 2 * SUB)
-                        for half in range(2):
-                            rows = pl.ds((2 * group + half) * SUB, SUB)
-                            if step == 0:
-                                q = [base[0, 0, tile, a, rows, lanes] for a in range(3)]
-                            else:
-                                q = [halfway[a, rows, lanes] for a in range(3)]
-                            q = stepped(q, pair[half], matrix)
-                            for a in range(3):
-                                if step == 0:
-                                    halfway[a, rows, lanes] = q[a]
-                                else:
-                                    fields[place, a, rows, lanes] = q[a]
-                            if step == 0:
-                                sums[0] = sums[0] + (q[0] * q[0] + q[1] * q[1] + q[2] * q[2])
-                            else:
-                                sums = add_moments(sums, q)
+                lanes = pl.ds(x * LANES, LANES)
+                matrix = with_diagonal(tile_grad(grad, depth, tile, x), wide(relaxes[place, step, pl.ds(x, 1), :]))
+
+                def read(a, rows):
+                    return base[0, 0, tile, a, rows, lanes] if step == 0 else halfway[place, a, rows, lanes]
+
+                def write(a, rows, value):
                     if step == 0:
-                        totals[pl.ds(x, 1), :] = column_sum(sums[0])
+                        halfway[place, a, rows, lanes] = value
                     else:
-                        for i, row in enumerate(stress_rows([column_sum(s) for s in sums], inverse)):
-                            stress[x, i, pl.ds(place, 1), :] = row
-
-                @pl.loop(0, depth // 2)
-                def _(x):
-                    body(2 * x)
-                    body(2 * x + 1)
-
-            store(place).start()
-
-    for place in range(here):
-
-        @pl.when(counts[0, 0, first + place] != ALL_FIELDS)
-        def _(place=place):
-            store(place).wait()
-
-
-def call_ordinary(first, here, tile_counts, before, base_fields, base_noise, grad, new_base):
+                        fields[place, a, rows, lanes] = value
+
+                def shock(_, a, rows):
+                    return noise[0, 0, tile, step, a, rows, lanes]
+
+                if step == 0:
+                    totals += tile_sums(read, write, shock, [matrix], count, add_square, 1)
+                else:
+                    totals.append(tile_sums(read, write, shock, [matrix], count, add_moments, 6))
+        for i, row in enumerate(stress_rows([packed_sum(list(same)) for same in zip(*totals)], inverse)):
+            stress[i, place] = row
+    for copy in copies:
+        copy.wait()
+
+
+def call_ordinary(first, here, before, base_fields, base_noise, grad, block, new_base, new_extra):
     count, cells = base_fields.shape[-2:]
     depth = cells // LANES
-    body = functools.partial(ordinary, first)
-    if new_base is None:
-        body = lambda *refs: ordinary(first, *refs[:5], None, *refs[5:])
-    return pl.pallas_call(
-        body,
-        out_shape=(
-            jax.ShapeDtypeStruct(base_fields.shape, f32),
-            jax.ShapeDtypeStruct((depth, 6, here, LANES), f32),
-        ),
-        in_specs=[smem, anywhere, vmem, vmem, vmem] + [hbm] * (new_base is not None),
-        out_specs=(hbm, vmem),
-        input_output_aliases={} if new_base is None else {5: 0},
+    has_block, has_base, has_extra = block is not None, new_base is not None, new_extra is not None
+    operands = [before, *near_memory(base_fields, base_noise), grad]
+    specs = [anywhere, vmem, vmem, vmem]
+    shapes, out_specs, aliases = [], [], {}
+    copies = 0
+    if has_block:
+        operands += near_memory(block)
+        specs.append(vmem)
+        shapes.append(jax.ShapeDtypeStruct(base_fields.shape, f32))
+        out_specs.append(hbm)
+        copies += block.shape[0]
+    if has_base:
+        aliases[len(operands)] = 0
+        operands.append(new_base)
+        specs.append(hbm)
+    if has_extra:
+        operands += near_memory(new_extra)
+        specs.append(vmem)
+        shapes.append(jax.ShapeDtypeStruct(new_extra.shape, f32))
+        out_specs.append(hbm)
+        copies += 3
+    shapes += [
+        pltpu.VMEM((here, 3, count, cells), f32),
+        jax.ShapeDtypeStruct((6, here, depth, LANES), f32),
+    ]
+    out_specs += [vmem, vmem]
+    results = pl.pallas_call(
+        functools.partial(ordinary, first, has_block, has_base, has_extra),
+        out_shape=tuple(shapes),
+        in_specs=specs,
+        out_specs=tuple(out_specs),
+        input_output_aliases=aliases,
         scratch_shapes=[
-            pltpu.VMEM((3, count, cells), f32),
             pltpu.VMEM((here, 3, count, cells), f32),
-            pltpu.VMEM((depth, LANES), f32),
-            pltpu.VMEM((depth, LANES), f32),
-            pltpu.SemaphoreType.DMA((here,)),
+            pltpu.VMEM((here, 2, depth, LANES), f32),
+            pltpu.SemaphoreType.DMA((max(copies, 1),)),
         ],
         compiler_params=pltpu.CompilerParams(vmem_limit_bytes=SMALL),
         cost_estimate=small(8 << 20, 3 << 20),
         name="ordinary_tiles",
-    )(tile_counts, before, *near_memory(base_fields, base_noise), grad, *([] if new_base is None else [new_base]))
-
-
-def extra(tiles, bit, unroll, helper, base, noise, moments, kept, received, new_fields, reply, message):
-    me = lax.axis_index("gy")
+    )(*operands)
+    results = list(results)
+    piece, block = results.pop(), results.pop()
+    new_base = results.pop(0) if has_block else None
+    return new_base, block, piece, (results[0] if has_extra else None)
+
+
+def extra(unroll, before, base, noise, moments, kept, received, new_fields, reply, message):
     _, _, _, count, cells = base.shape
     inverse = 1.0 / float(ALL_FIELDS)
     zero = jnp.zeros((SUB, LANES), f32)
-    pick = arrived(tiles, me, helper, me, bit)
-    for i in range(message.shape[0]):
-        message[i] = jnp.where(pick, received[0, i], kept[0, i])
+    message[...] = kept[0] + received[0]
     own = coefficients([message[i] for i in range(9)], [moments[i] for i in range(16)])
     both = [message[9 + i] + own[i] for i in range(3)]
     first = relax_of(both[2], inverse)
@@ -491,95 +555,106 @@
             reply[2 + i, pl.ds(x, 1), :] = column_sum(s)
 
 
-def call_extra(tiles, bit, helper_tile, extra_fields, extra_noise, moments, kept, received):
+def call_extra(before, extra_fields, extra_noise, moments, kept, received):
     depth = extra_fields.shape[-1] // LANES
     return pl.pallas_call(
-        functools.partial(extra, tiles, bit, 7),
+        functools.partial(extra, 7),
         out_shape=(
             pltpu.VMEM(extra_fields.shape, f32),
             jax.ShapeDtypeStruct((8, depth, LANES), f32),
         ),
-        in_specs=[smem, vmem, vmem, vmem, vmem, vmem],
+        in_specs=[anywhere, vmem, vmem, vmem, vmem, vmem],
         out_specs=(vmem, vmem),
         scratch_shapes=[pltpu.VMEM(kept.shape[1:], f32)],
         compiler_params=pltpu.CompilerParams(vmem_limit_bytes=SMALL),
         cost_estimate=small(32 << 20, 9 << 20),
         name="extra_fields",
-    )(helper_tile, *near_memory(extra_fields, extra_noise), moments, kept, received)
-
-
-def heavy(bits, piece_count, helper, base, noise, grad, near, far, *refs):
+    )(before, *near_memory(extra_fields, extra_noise), moments, kept, received)
+
+
+def heavy(bits, piece_count, helper, base, noise, grad, near, far, block, *refs):
     pieces, (_, new_base, stress, fields, rows, answer, sems) = refs[:piece_count], refs[piece_count:]
     _, _, tiles, _, count, cells = base.shape
     slots = helper.shape[1]
     me = lax.axis_index("gy")
     depth = cells // LANES
-    groups = count // (2 * SUB)
+    last = block.shape[0]
+    flat = rows.reshape(6 * depth * tiles, LANES)
+
+    def put_stress(tile, packed):
+        for i, value in enumerate(packed):
+            flat[pl.ds(i * depth * tiles + tile, depth, stride=tiles), :] = value
+
+    def leave(i):
+        return pltpu.make_async_copy(block.at[i], new_base.at[0, 0, tiles - last + i], sems.at[slots + depth + i])
 
     def store(h, tile):
         return pltpu.make_async_copy(fields.at[h], new_base.at[0, 0, tile], sems.at[h])
 
     def result(x):
         target = stress.at[0, 0, :, :, pl.ds(x * LANES, LANES)]
-        return pltpu.make_async_copy(rows.at[x], target, sems.at[slots + x])
-
-    at = 0
+        return pltpu.make_async_copy(rows.at[:, x], target, sems.at[slots + x])
+
+    for i in range(last):
+        leave(i).start()
+    tile = 0
     for piece in pieces:
-        rows[:, :, at : at + piece.shape[2], :] = piece[...]
-        at += piece.shape[2]
-    found = owned_slots(tiles, me, helper)
-    for h, owned, tile in found:
-
-        @pl.when(owned)
-        def _(h=h, tile=tile):
+        for place in range(piece.shape[1]):
+            put_stress(tile, [piece[i, place] for i in range(6)])
+            tile += 1
+
+    @pl.loop(0, slots)
+    def _(h):
+        tile = helper[0, h] - me * tiles
+
+        @pl.when((tile >= 0) & (tile < tiles))
+        def _():
             flips = me ^ h
             place = sum(((flips >> (bits - 1 - i)) & 1) << i for i in range(bits))
             is_far = place >= slots // 2
             place = place & (slots // 2 - 1)
             for i in range(near.shape[1]):
                 answer[i] = jnp.where(is_far, far[place, i], near[place, i])
-
-            def body(x):
-                lanes = pl.ds(pl.multiple_of(x * LANES, LANES), LANES)
+            totals = []
+            for x in range(depth):
+                lanes = pl.ds(x * LANES, LANES)
                 g = tile_grad(grad, depth, tile, x)
-                matrices = [with_diagonal(g, wide(answer[s, pl.ds(x, 1), :])) for s in range(2)]
-                sums = [jnp.zeros((SUB, LANES), f32)] * 6
-                for group in range(groups):
-                    pairs = [
-                        noise_rows(lambda a, r: noise[0, 0, tile, s, a, r, lanes], group * 2 * SUB) for s in range(2)
-                    ]
-                    for half in range(2):
-                        part = pl.ds((2 * group + half) * SUB, SUB)
-                        q = [base[0, 0, tile, a, part, lanes] for a in range(3)]
-                        for s in range(2):
-                            q = stepped(q, pairs[s][half], matrices[s])
-                        for a in range(3):
-                            fields[h, a, part, lanes] = q[a]
-                        sums = add_moments(sums, q)
-                sums = [column_sum(s) + answer[2 + i, pl.ds(x, 1), :] for i, s in enumerate(sums)]
-                for i, row in enumerate(stress_rows(sums, 1.0 / float(ALL_FIELDS))):
-                    rows[x, i, pl.ds(tile, 1), :] = row
-
-            @pl.loop(0, depth // 2)
-            def _(x):
-                body(2 * x)
-                body(2 * x + 1)
-
-            store(h, tile).start()
+                matrices = [with_diagonal(g, wide(answer[step, pl.ds(x, 1), :])) for step in range(2)]
+
+                def read(a, part):
+                    return base[0, 0, tile, a, part, lanes]
+
+                def write(a, part, value):
+                    fields[h, a, part, lanes] = value
+
+                def shock(step, a, part):
+                    return noise[0, 0, tile, step, a, part, lanes]
+
+                totals.append(tile_sums(read, write, shock, matrices, count, add_moments, 6))
+            sums = [packed_sum(list(same)) + answer[2 + i] for i, same in enumerate(zip(*totals))]
+            put_stress(tile, stress_rows(sums, 1.0 / ALL_FIELDS))
 
     for x in range(depth):
         result(x).start()
-    for h, owned, tile in found:
-
-        @pl.when(owned)
-        def _(h=h, tile=tile):
-            store(h, tile).wait()
-
+    for i in range(last):
+        leave(i).wait()
+
+    def each_owned(act):
+        @pl.loop(0, slots)
+        def _(h):
+            tile = helper[0, h] - me * tiles
+
+            @pl.when((tile >= 0) & (tile < tiles))
+            def _():
+                act(store(h, tile))
+
+    each_owned(lambda copy: copy.start())
     for x in range(depth):
         result(x).wait()
-
-
-def call_heavy(bits, helper_tile, base_fields, base_noise, grad, near, far, pieces, new_base):
+    each_owned(lambda copy: copy.wait())
+
+
+def call_heavy(bits, helper_tile, base_fields, base_noise, grad, near, far, block, pieces, new_base):
     _, _, tiles, _, count, cells = base_fields.shape
     depth = cells // LANES
     slots = helper_tile.shape[1]
@@ -589,26 +664,19 @@
             jax.ShapeDtypeStruct(new_base.shape, f32),
             jax.ShapeDtypeStruct((1, 1, 6, tiles, cells), f32),
         ),
-        in_specs=[smem] + [vmem] * (5 + len(pieces)) + [hbm],
+        in_specs=[smem] + [vmem] * (6 + len(pieces)) + [hbm],
         out_specs=(hbm, hbm),
-        input_output_aliases={6 + len(pieces): 0},
+        input_output_aliases={7 + len(pieces): 0},
         scratch_shapes=[
             pltpu.VMEM((slots, 3, count, cells), f32),
-            pltpu.VMEM((depth, 6, tiles, LANES), f32),
+            pltpu.VMEM((6, depth, tiles, LANES), f32),
             pltpu.VMEM(near.shape[1:], f32),
-            pltpu.SemaphoreType.DMA((slots + depth,)),
+            pltpu.SemaphoreType.DMA((slots + depth + block.shape[0],)),
         ],
         compiler_params=pltpu.CompilerParams(vmem_limit_bytes=SMALL),
         cost_estimate=small(8 << 20, 4 << 20),
         name="heavy_tiles",
-    )(helper_tile, *near_memory(base_fields, base_noise), grad, near, far, *pieces, new_base)
-
-
-def both_ways(last, first, axis):
-    size = lax.axis_size(axis)
-    up = [(i, i + 1) for i in range(size - 1)]
-    down = [(i + 1, i) for i in range(size - 1)]
-    return lax.ppermute(last, axis, up), lax.ppermute(first, axis, down)
+    )(helper_tile, *near_memory(base_fields, base_noise), grad, near, far, *near_memory(block), *pieces, new_base)
 
 
 def per_device(
@@ -616,36 +684,44 @@
 ):
     tiles = tile_counts.shape[2]
     bits = lax.axis_size("gy").bit_length() - 1
-    x_last, x_first, y_last, y_first = call_edges(helper_tile, velocity)
-    halos = both_ways(x_last, x_first, "gx") + both_ways(y_last, y_first, "gy")
+    x_one, x_two, y_one, y_two = call_edges(velocity)
+    halos = two_swaps(x_one, x_two, "gx") + two_swaps(y_one, y_two, "gy")
     moments = call_heavy_moments(helper_tile, base_fields, base_noise)
     grad, keep, send = call_gradients(tiles, helper_tile, velocity, halos, wall_cells, moments)
     gaps = 2 * bits - 2
-    new_base, pieces, done = None, [], 0
-
-    def fill(before):
-        nonlocal new_base, done
+    new_base, block, pieces, done = None, None, [], 0
+
+    def fill(before, extra_near=None):
+        nonlocal new_base, block, done
         here = (tiles - done) // (gaps - len(pieces))
-        new_base, piece = call_ordinary(done, here, tile_counts, before, base_fields, base_noise, grad, new_base)
+        new_base, block, piece, extra_far = call_ordinary(
+            done, here, before, base_fields, base_noise, grad, block, new_base, extra_near
+        )
         pieces.append(piece)
         done += here
-        return piece
+        return piece, extra_far
 
     for bit in range(bits):
         received = swapped(send, bit)
         if bit == 1:
             before = extra_sums = call_extra_moments(send, extra_fields, extra_noise)
         else:
-            before = fill(send)
+            before, _ = fill(send)
         if bit < bits - 1:
-            keep, send = call_merge(tiles, bit, helper_tile, before, keep, received)
-    new_extra, reply = call_extra(tiles, bits - 1, helper_tile, extra_fields, extra_noise, extra_sums, keep, received)
+            keep, send = call_merge(bit, before, keep, received)
+    extra_near, reply = call_extra(before, extra_fields, extra_noise, extra_sums, keep, received)
     near = reply[None]
     for bit in range(bits - 1, 0, -1):
         received = swapped(near, bit)
-        near = call_join(fill(near), near, received)
+        if bit == bits - 1:
+            before, new_extra = fill(near, extra_near)
+        else:
+            before, _ = fill(near)
+        near = call_join(before, near, received)
     far = swapped(near, 0)
-    new_base, stress = call_heavy(bits, helper_tile, base_fields, base_noise, grad, near, far, pieces, new_base)
+    new_base, stress = call_heavy(
+        bits, helper_tile, base_fields, base_noise, grad, near, far, block, pieces, new_base
+    )
     return new_base, new_extra, jnp.swapaxes(stress, 2, 3)
 
 

time: 51.3 us -> 41 us (0.80)
  the two profiles are of different devices: /device:TPU:25 before, /device:TPU:9 now
where the time goes in v2:
time: 41 us; the launch traced here: 41.8 us
  Pallas kernels  15.8 us (39%)
  starting transfers between devices  14.7 us (36%)
  waiting for transfers between devices  7.89 us (19%)
  local copies, waits for them, and re-layouts  2.57 us (6%)
  between operations  0.85 us (2%)
    ppermute x4, starting transfers between devices, two_swaps(): return (lax.ppermute(one, axis, within), lax.ppermute(two, axis, across))  9.17 us
    ppermute x6, waiting for transfers between devices, swapped(): return lax.ppermute(block, 'gy', [(i, i ^ 1 << bit) for i in range(size)])  7.88 us
    ppermute x6, starting transfers between devices, swapped(): return lax.ppermute(block, 'gy', [(i, i ^ 1 << bit) for i in range(size)])  5.5 us
    pallas_call x4, Pallas kernels, call_ordinary(): pl.pallas_call(functools.partial(ordinary, first, has_block, has_base, ha...  4.35 us
    pallas_call x1, Pallas kernels, call_heavy(): pl.pallas_call(functools.partial(heavy, bits, len(pieces)), out_shape=(ja...  3.34 us
    pallas_call x1, Pallas kernels, call_heavy_moments(): pl.pallas_call(heavy_moments, out_shape=jax.ShapeDtypeStruct((slots, 16,...  3.13 us
    unnamed x16, local copies, waits for them, and re-layouts  2.57 us
    pallas_call x1, Pallas kernels, call_extra(): pl.pallas_call(functools.partial(extra, 7), out_shape=(pltpu.VMEM(extra_f...  2.25 us
  transfers between devices with their start and end apart: 10, of which 6 were waited for; matrix products, arithmetic and copies ran while one was open for 0% of the time, Pallas kernels for 21%

profile of v2, /device:TPU:9, one launch (start us, length us, event | category | flops | bytes accessed | tf_op | source)
XLA Modules:
  0.0 41.8 jit_solution(10020897928551372794)
XLA Ops:
  0.6 0.0 copy-start.4
  0.6 0.9 %copy-done.4 = f32[3,8,8,128]{3,2,1,0:T(8,128)S(1)} copy-done((f32[3,8,8,128]{3,2,1,0:T(8,128)S(1)}, f32[3,8,8,128]{3,2,1,0:T(8,128)}, u32[]{:S(2)}) %copy-start.4) | copy-done | bytes 98328
  1.6 0.1 collective-permute-start
  1.6 4.5 %collective-permute-start.1 = (f32[3,8,128]{2,1,0:T(8,128)S(1)}, f32[3,8,128]{2,1,0:T(8,128)S(1)}, u32[]{:S(2)}, u32[]{:S(2)}) collective-permute-start(f32[3,8,128]{2,1,0:T(8,128)S(1)} %get-tuple-element.31), channel_id=1, source_target_pairs={{0,0},{8,16},{16,8},{24,24},{1,1},{9,17},{17,9},{25,25},{2,2},{10,... | collective-permute-start | bytes 36872 | tf_op jit(solution)/shard_map/ppermute | solution.py:171
  6.1 1.3 %collective-permute-start.2 = (f32[3,8,128]{2,1,0:T(8,128)S(1)}, f32[3,8,128]{2,1,0:T(8,128)S(1)}, u32[]{:S(2)}, u32[]{:S(2)}) collective-permute-start(f32[3,8,128]{2,1,0:T(8,128)S(1)} %get-tuple-element.32), channel_id=1, source_target_pairs={{0,1},{1,0},{2,3},{3,2},{4,5},{5,4},{6,7},{7,6},{8,9},{9,8},{10,11... | collective-permute-start | bytes 36872 | tf_op jit(solution)/shard_map/ppermute | solution.py:171
  7.4 3.3 %collective-permute-start.3 = (f32[3,8,128]{2,1,0:T(8,128)S(1)}, f32[3,8,128]{2,1,0:T(8,128)S(1)}, u32[]{:S(2)}, u32[]{:S(2)}) collective-permute-start(f32[3,8,128]{2,1,0:T(8,128)S(1)} %get-tuple-element.33), channel_id=1, source_target_pairs={{0,0},{1,2},{2,1},{3,4},{4,3},{5,6},{6,5},{7,7},{8,8},{9,10},{10,9... | collective-permute-start | bytes 36872 | tf_op jit(solution)/shard_map/ppermute | solution.py:171
  10.8 0.6 %copy-done.7 = s32[1,8]{1,0:T(1,128)S(1)} copy-done((s32[1,8]{1,0:T(1,128)S(1)}, s32[1,8]{1,0:T(1,128)}, u32[]{:S(2)}) %copy-start.7) | copy-done | bytes 56
  11.4 3.1 %heavy_moments.1.moments = f32[8,16,8,128]{3,2,1,0:T(8,128)S(1)} custom-call(s32[1,8]{1,0:T(1,128)S(1)} %copy-done.7, f32[1,1,8,3,32,1024]{5,4,3,2,1,0:T(8,128)} %base.7, bf16[1,1,8,2,3,32,1024]{6,5,4,3,2,1,0:T(8,128)(2,1)} %noise.7), custom_call_target="tpu_custom_call" | custom-call | flops 8388608 | bytes 3145728 | tf_op jit(solution)/shard_map/heavy_moments/pallas_call | solution.py:223
  14.6 1.2 %gradients.1 = (f32[576,128]{1,0:T(8,128)S(1)}, f32[4,12,8,128]{3,2,1,0:T(8,128)S(1)}, f32[4,12,8,128]{3,2,1,0:T(8,128)S(1)}) custom-call(s32[1,8]{1,0:T(1,128)S(1)} %copy-done.7, f32[3,8,8,128]{3,2,1,0:T(8,128)S(1)} %copy-done.5, f32[3,8,128]{2,1,0:T(8,128)S(1)} %collective-permute-done.x_one, f32[3,8,128]{2,1,0:T(8,128)S(1)} %collective-permute-done.1.x_two, ...), custom_call_target="tpu_custom_call" | custom-call | flops 4194304 | bytes 1048576 | tf_op jit(solution)/shard_map/gradients/pallas_call | solution.py:325
  15.9 0.1 collective-permute-start.4
  16.0 0.0 copy-start.2
  16.0 0.0 copy-start.3
  16.0 0.7 %ordinary_tiles.4 = (f32[2,3,32,1024]{3,2,1,0:T(8,128)S(1)}, f32[6,2,8,128]{3,2,1,0:T(8,128)S(1)}) custom-call(f32[4,12,8,128]{3,2,1,0:T(8,128)S(1)} %get-tuple-element.35.refs_0_, f32[1,1,8,3,32,1024]{5,4,3,2,1,0:T(8,128)S(1)} %copy-done, bf16[1,1,8,2,3,32,1024]{6,5,4,3,2,1,0:T(8,128)(2,1)S(1)} %copy-done.1, f32[576,128]{1,0:T(8,128)S(1)} %get-tuple-element.34.refs_3_.grad), custom_call_target="tpu_custom_call" | custom-call | flops 8388608 | bytes 3145728 | tf_op jit(solution)/shard_map/ordinary_tiles/pallas_call | solution.py:503
  16.7 0.6 %collective-permute-done.4.received = f32[4,12,8,128]{3,2,1,0:T(8,128)S(1)} collective-permute-done((f32[4,12,8,128]{3,2,1,0:T(8,128)S(1)}, f32[4,12,8,128]{3,2,1,0:T(8,128)S(1)}, u32[]{:S(2)}, u32[]{:S(2)}) %collective-permute-start.4) | collective-permute-done | bytes 196640 | tf_op jit(solution)/shard_map/ppermute | solution.py:338
  17.4 0.2 collective-permute-start.5
  17.6 0.2 copy-done.2
  17.7 0.8 %copy-done.3 = bf16[1,1,2,3,224,1024]{5,4,3,2,1,0:T(8,128)(2,1)S(1)} copy-done((bf16[1,1,2,3,224,1024]{5,4,3,2,1,0:T(8,128)(2,1)S(1)}, bf16[1,1,2,3,224,1024]{5,4,3,2,1,0:T(8,128)(2,1)}, u32[]{:S(2)}) %copy-start.3) | copy-done | bytes 2752536
  18.6 1.4 %extra_moments.1.before.moments = f32[16,8,128]{2,1,0:T(8,128)S(1)} custom-call(f32[2,12,8,128]{3,2,1,0:T(8,128)S(1)} %get-tuple-element.38.before, f32[1,1,3,224,1024]{4,3,2,1,0:T(8,128)S(1)} %copy-done.2, bf16[1,1,2,3,224,1024]{5,4,3,2,1,0:T(8,128)(2,1)S(1)} %copy-done.3), custom_call_target="tpu_custom_call" | custom-call | flops 8388608 | bytes 5242880 | tf_op jit(solution)/shard_map/extra_moments/pallas_call | solution.py:261
  20.0 1.7 %collective-permute-done.5.received = f32[2,12,8,128]{3,2,1,0:T(8,128)S(1)} collective-permute-done((f32[2,12,8,128]{3,2,1,0:T(8,128)S(1)}, f32[2,12,8,128]{3,2,1,0:T(8,128)S(1)}, u32[]{:S(2)}, u32[]{:S(2)}) %collective-permute-start.5) | collective-permute-done | bytes 98336 | tf_op jit(solution)/shard_map/ppermute | solution.py:338
  21.7 0.3 collective-permute-start.6
  22.1 0.9 %ordinary_tiles.5 = (f32[1,1,8,3,32,1024]{5,4,3,2,1,0:T(8,128)}, f32[2,3,32,1024]{3,2,1,0:T(8,128)S(1)}, f32[6,2,8,128]{3,2,1,0:T(8,128)S(1)}) custom-call(f32[1,12,8,128]{3,2,1,0:T(8,128)S(1)} %get-tuple-element.40.refs_0_, f32[1,1,8,3,32,1024]{5,4,3,2,1,0:T(8,128)S(1)} %copy-done, bf16[1,1,8,2,3,32,1024]{6,5,4,3,2,1,0:T(8,128)(2,1)S(1)} %copy-done.1, ...), custom_call_target="tpu_custom_call" | custom-call | flops 8388608 | bytes 3145728 | tf_op jit(solution)/shard_map/ordinary_tiles/pallas_call | solution.py:503
  23.0 1.8 %collective-permute-done.6.received = f32[1,12,8,128]{3,2,1,0:T(8,128)S(1)} collective-permute-done((f32[1,12,8,128]{3,2,1,0:T(8,128)S(1)}, f32[1,12,8,128]{3,2,1,0:T(8,128)S(1)}, u32[]{:S(2)}, u32[]{:S(2)}) %collective-permute-start.6) | collective-permute-done | bytes 49184 | tf_op jit(solution)/shard_map/ppermute | solution.py:338
  24.7 2.3 %extra_fields.1 = (f32[1,1,3,224,1024]{4,3,2,1,0:T(8,128)S(1)}, f32[8,8,128]{2,1,0:T(8,128)S(1)}) custom-call(f32[6,2,8,128]{3,2,1,0:T(8,128)S(1)} %get-tuple-element.42.before.refs_1_, f32[1,1,3,224,1024]{4,3,2,1,0:T(8,128)S(1)} %copy-done.2, bf16[1,1,2,3,224,1024]{5,4,3,2,1,0:T(8,128)(2,1)S(1)} %copy-done.3, ...), custom_call_target="tpu_custom_call" | custom-call | flops 33554432 | bytes 9437184 | tf_op jit(solution)/shard_map/extra_fields/pallas_call | solution.py:560
  27.0 0.3 collective-permute-start.7
  27.3 1.8 %ordinary_tiles.6 = (f32[1,1,8,3,32,1024]{5,4,3,2,1,0:T(8,128)}, f32[1,1,3,224,1024]{4,3,2,1,0:T(8,128)}, f32[2,3,32,1024]{3,2,1,0:T(8,128)S(1)}, f32[6,2,8,128]{3,2,1,0:T(8,128)S(1)}) custom-call(f32[1,8,8,128]{3,2,1,0:T(8,128)S(1)} %bitcast.3, f32[1,1,8,3,32,1024]{5,4,3,2,1,0:T(8,128)S(1)} %copy-done, ...), custom_call_target="tpu_custom_call", output_to_operand_aliasing={{0}: (5, {})} | custom-call | flops 8388608 | bytes 3145728 | tf_op jit(solution)/shard_map/ordinary_tiles/pallas_call | solution.py:503
  29.2 0.6 %collective-permute-done.7.second = f32[1,8,8,128]{3,2,1,0:T(8,128)S(1)} collective-permute-done((f32[1,8,8,128]{3,2,1,0:T(8,128)S(1)}, f32[1,8,8,128]{3,2,1,0:T(8,128)S(1)}, u32[]{:S(2)}, u32[]{:S(2)}) %collective-permute-start.7) | collective-permute-done | bytes 32800 | tf_op jit(solution)/shard_map/ppermute | solution.py:338
  29.8 0.1 collective-permute-start.8
  29.9 0.9 %ordinary_tiles.7 = (f32[1,1,8,3,32,1024]{5,4,3,2,1,0:T(8,128)}, f32[2,3,32,1024]{3,2,1,0:T(8,128)S(1)}, f32[6,2,8,128]{3,2,1,0:T(8,128)S(1)}) custom-call(f32[2,8,8,128]{3,2,1,0:T(8,128)S(1)} %join.2.refs_0_.first, f32[1,1,8,3,32,1024]{5,4,3,2,1,0:T(8,128)S(1)} %copy-done, ...), custom_call_target="tpu_custom_call", output_to_operand_aliasing={{0}: (5, {})} | custom-call | flops 8388608 | bytes 3145728 | tf_op jit(solution)/shard_map/ordinary_tiles/pallas_call | solution.py:503
  30.8 2.1 %collective-permute-done.8.second = f32[2,8,8,128]{3,2,1,0:T(8,128)S(1)} collective-permute-done((f32[2,8,8,128]{3,2,1,0:T(8,128)S(1)}, f32[2,8,8,128]{3,2,1,0:T(8,128)S(1)}, u32[]{:S(2)}, u32[]{:S(2)}) %collective-permute-start.8) | collective-permute-done | bytes 65568 | tf_op jit(solution)/shard_map/ppermute | solution.py:338
  33.0 4.5 %collective-permute-start.9 = (f32[4,8,8,128]{3,2,1,0:T(8,128)S(1)}, f32[4,8,8,128]{3,2,1,0:T(8,128)S(1)}, u32[]{:S(2)}, u32[]{:S(2)}) collective-permute-start(f32[4,8,8,128]{3,2,1,0:T(8,128)S(1)} %join.3.near), channel_id=1, source_target_pairs={{0,1},{1,0},{2,3},{3,2},{4,5},{5,4},{6,7},{7,6},{8,9},{9,8},{10,11... | collective-permute-start | bytes 393224 | tf_op jit(solution)/shard_map/ppermute | solution.py:338
  37.4 1.0 %collective-permute-done.9.far = f32[4,8,8,128]{3,2,1,0:T(8,128)S(1)} collective-permute-done((f32[4,8,8,128]{3,2,1,0:T(8,128)S(1)}, f32[4,8,8,128]{3,2,1,0:T(8,128)S(1)}, u32[]{:S(2)}, u32[]{:S(2)}) %collective-permute-start.9) | collective-permute-done | bytes 131104 | tf_op jit(solution)/shard_map/ppermute | solution.py:338
  38.4 3.3 %heavy_tiles.1 = (f32[1,1,8,3,32,1024]{5,4,3,2,1,0:T(8,128)}, f32[1,1,6,8,1024]{4,3,2,1,0:T(8,128)}) custom-call(s32[1,8]{1,0:T(1,128)S(1)} %copy-done.7, f32[1,1,8,3,32,1024]{5,4,3,2,1,0:T(8,128)S(1)} %copy-done, bf16[1,1,8,2,3,32,1024]{6,5,4,3,2,1,0:T(8,128)(2,1)S(1)} %copy-done.1, ...), custom_call_target="tpu_custom_call", output_to_operand_aliasing={{0}: (11, {})} | custom-call | flops 8388608 | bytes 4194304 | tf_op jit(solution)/shard_map/heavy_tiles/pallas_call | solution.py:661
  (18 shorter events, 0.1 us)
Async XLA Ops:
  0.6 0.9 %copy-start.4 = (f32[3,8,8,128]{3,2,1,0:T(8,128)S(1)}, f32[3,8,8,128]{3,2,1,0:T(8,128)}, u32[]{:S(2)}) copy-start(f32[3,8,8,128]{3,2,1,0:T(8,128)} %velocity.3) | copy-start | bytes 294916
  1.6 13.0 %collective-permute-start = (f32[3,8,128]{2,1,0:T(8,128)S(1)}, f32[3,8,128]{2,1,0:T(8,128)S(1)}, u32[]{:S(2)}, u32[]{:S(2)}) collective-permute-start(f32[3,8,128]{2,1,0:T(8,128)S(1)} %get-tuple-element.30), channel_id=1, source_target_pairs={{0,8},{8,0},{16,24},{24,16},{1,9},{9,1},{17,25},{25,17},{2,10},{10... | collective-permute-start | bytes 36872 | tf_op jit(solution)/shard_map/ppermute | solution.py:171
  1.6 12.9 %collective-permute-start.1 = (f32[3,8,128]{2,1,0:T(8,128)S(1)}, f32[3,8,128]{2,1,0:T(8,128)S(1)}, u32[]{:S(2)}, u32[]{:S(2)}) collective-permute-start(f32[3,8,128]{2,1,0:T(8,128)S(1)} %get-tuple-element.31), channel_id=1, source_target_pairs={{0,0},{8,16},{16,8},{24,24},{1,1},{9,17},{17,9},{25,25},{2,2},{10,... | collective-permute-start | bytes 36872 | tf_op jit(solution)/shard_map/ppermute | solution.py:171
  6.1 8.5 %collective-permute-start.2 = (f32[3,8,128]{2,1,0:T(8,128)S(1)}, f32[3,8,128]{2,1,0:T(8,128)S(1)}, u32[]{:S(2)}, u32[]{:S(2)}) collective-permute-start(f32[3,8,128]{2,1,0:T(8,128)S(1)} %get-tuple-element.32), channel_id=1, source_target_pairs={{0,1},{1,0},{2,3},{3,2},{4,5},{5,4},{6,7},{7,6},{8,9},{9,8},{10,11... | collective-permute-start | bytes 36872 | tf_op jit(solution)/shard_map/ppermute | solution.py:171
  7.4 7.2 %copy-start.5 = (f32[3,8,8,128]{3,2,1,0:T(8,128)S(1)}, f32[3,8,8,128]{3,2,1,0:T(8,128)}, u32[]{:S(2)}) copy-start(f32[3,8,8,128]{3,2,1,0:T(8,128)} %velocity.3) | copy-start | bytes 294916
  7.4 7.2 %copy-start.6 = (s32[8,8,128]{2,1,0:T(8,128)S(1)}, s32[8,8,128]{2,1,0:T(8,128)}, u32[]{:S(2)}) copy-start(s32[8,8,128]{2,1,0:T(8,128)} %wall.1) | copy-start | bytes 98308
  7.4 8.5 %copy-start = (f32[1,1,8,3,32,1024]{5,4,3,2,1,0:T(8,128)S(1)}, f32[1,1,8,3,32,1024]{5,4,3,2,1,0:T(8,128)}, u32[]{:S(2)}) copy-start(f32[1,1,8,3,32,1024]{5,4,3,2,1,0:T(8,128)} %base.7) | copy-start | bytes 9437188
  7.4 8.5 %copy-start.1 = (bf16[1,1,8,2,3,32,1024]{6,5,4,3,2,1,0:T(8,128)(2,1)S(1)}, bf16[1,1,8,2,3,32,1024]{6,5,4,3,2,1,0:T(8,128)(2,1)}, u32[]{:S(2)}) copy-start(bf16[1,1,8,2,3,32,1024]{6,5,4,3,2,1,0:T(8,128)(2,1)} %noise.7) | copy-start | bytes 9437188
  7.4 7.2 %collective-permute-start.3 = (f32[3,8,128]{2,1,0:T(8,128)S(1)}, f32[3,8,128]{2,1,0:T(8,128)S(1)}, u32[]{:S(2)}, u32[]{:S(2)}) collective-permute-start(f32[3,8,128]{2,1,0:T(8,128)S(1)} %get-tuple-element.33), channel_id=1, source_target_pairs={{0,0},{1,2},{2,1},{3,4},{4,3},{5,6},{6,5},{7,7},{8,8},{9,10},{10,9... | collective-permute-start | bytes 36872 | tf_op jit(solution)/shard_map/ppermute | solution.py:171
  10.8 0.7 %copy-start.7 = (s32[1,8]{1,0:T(1,128)S(1)}, s32[1,8]{1,0:T(1,128)}, u32[]{:S(2)}) copy-start(s32[1,8]{1,0:T(1,128)} %helper.5) | copy-start | bytes 100
  15.9 1.5 %collective-permute-start.4 = (f32[4,12,8,128]{3,2,1,0:T(8,128)S(1)}, f32[4,12,8,128]{3,2,1,0:T(8,128)S(1)}, u32[]{:S(2)}, u32[]{:S(2)}) collective-permute-start(f32[4,12,8,128]{3,2,1,0:T(8,128)S(1)} %get-tuple-element.35.refs_0_), channel_id=1, source_target_pairs={{0,1},{1,0},{2,3},{3,2},{4,5},{5,4},{6,7},{7,6},{8,9},{9,8},{10,11... | collective-permute-start | bytes 589832 | tf_op jit(solution)/shard_map/ppermute | solution.py:338
  16.0 1.8 %copy-start.2 = (f32[1,1,3,224,1024]{4,3,2,1,0:T(8,128)S(1)}, f32[1,1,3,224,1024]{4,3,2,1,0:T(8,128)}, u32[]{:S(2)}) copy-start(f32[1,1,3,224,1024]{4,3,2,1,0:T(8,128)} %base.6) | copy-start | bytes 8257540
  16.0 2.6 %copy-start.3 = (bf16[1,1,2,3,224,1024]{5,4,3,2,1,0:T(8,128)(2,1)S(1)}, bf16[1,1,2,3,224,1024]{5,4,3,2,1,0:T(8,128)(2,1)}, u32[]{:S(2)}) copy-start(bf16[1,1,2,3,224,1024]{5,4,3,2,1,0:T(8,128)(2,1)} %noise.6) | copy-start | bytes 8257540
  17.4 4.3 %collective-permute-start.5 = (f32[2,12,8,128]{3,2,1,0:T(8,128)S(1)}, f32[2,12,8,128]{3,2,1,0:T(8,128)S(1)}, u32[]{:S(2)}, u32[]{:S(2)}) collective-permute-start(f32[2,12,8,128]{3,2,1,0:T(8,128)S(1)} %get-tuple-element.38.before), channel_id=1, source_target_pairs={{0,2},{1,3},{2,0},{3,1},{4,6},{5,7},{6,4},{7,5},{8,10},{9,11},{10,... | collective-permute-start | bytes 294920 | tf_op jit(solution)/shard_map/ppermute | solution.py:338
  21.7 3.0 %collective-permute-start.6 = (f32[1,12,8,128]{3,2,1,0:T(8,128)S(1)}, f32[1,12,8,128]{3,2,1,0:T(8,128)S(1)}, u32[]{:S(2)}, u32[]{:S(2)}) collective-permute-start(f32[1,12,8,128]{3,2,1,0:T(8,128)S(1)} %get-tuple-element.40.refs_0_), channel_id=1, source_target_pairs={{0,4},{1,5},{2,6},{3,7},{4,0},{5,1},{6,2},{7,3},{8,12},{9,13},{10,... | collective-permute-start | bytes 147464 | tf_op jit(solution)/shard_map/ppermute | solution.py:338
  27.0 2.8 %collective-permute-start.7 = (f32[1,8,8,128]{3,2,1,0:T(8,128)S(1)}, f32[1,8,8,128]{3,2,1,0:T(8,128)S(1)}, u32[]{:S(2)}, u32[]{:S(2)}) collective-permute-start(f32[1,8,8,128]{3,2,1,0:T(8,128)S(1)} %bitcast.2), channel_id=1, source_target_pairs={{0,4},{1,5},{2,6},{3,7},{4,0},{5,1},{6,2},{7,3},{8,12},{9,13},{10,... | collective-permute-start | bytes 98312 | tf_op jit(solution)/shard_map/ppermute | solution.py:338
  29.8 3.1 %collective-permute-start.8 = (f32[2,8,8,128]{3,2,1,0:T(8,128)S(1)}, f32[2,8,8,128]{3,2,1,0:T(8,128)S(1)}, u32[]{:S(2)}, u32[]{:S(2)}) collective-permute-start(f32[2,8,8,128]{3,2,1,0:T(8,128)S(1)} %join.2.refs_0_.first), channel_id=1, source_target_pairs={{0,2},{1,3},{2,0},{3,1},{4,6},{5,7},{6,4},{7,5},{8,10},{9,11},{10,... | collective-permute-start | bytes 196616 | tf_op jit(solution)/shard_map/ppermute | solution.py:338
  33.0 5.5 %collective-permute-start.9 = (f32[4,8,8,128]{3,2,1,0:T(8,128)S(1)}, f32[4,8,8,128]{3,2,1,0:T(8,128)S(1)}, u32[]{:S(2)}, u32[]{:S(2)}) collective-permute-start(f32[4,8,8,128]{3,2,1,0:T(8,128)S(1)} %join.3.near), channel_id=1, source_target_pairs={{0,1},{1,0},{2,3},{3,2},{4,5},{5,4},{6,7},{7,6},{8,9},{9,8},{10,11... | collective-permute-start | bytes 393224 | tf_op jit(solution)/shard_map/ppermute | solution.py:338

commit v3 on v2

--- a/solution.py
+++ b/solution.py
@@ -8,6 +8,7 @@
 from jax.sharding import PartitionSpec as P
 
 ALL_FIELDS = 256
+HEAVY_MOST = 4
 LANES = 128
 SUB = 8
 SMALL = 10 << 20
@@ -21,7 +22,6 @@
 moment_of = {(0, 0): 0, (1, 1): 1, (2, 2): 2, (0, 1): 3, (1, 0): 3, (0, 2): 4, (2, 0): 4, (1, 2): 5, (2, 1): 5}
 f32 = jnp.float32
 
-smem = pl.BlockSpec(memory_space=pltpu.SMEM)
 vmem = pl.BlockSpec(memory_space=pltpu.VMEM)
 hbm = pl.BlockSpec(memory_space=pltpu.HBM)
 anywhere = pl.BlockSpec(memory_space=pl.ANY)
@@ -120,8 +120,9 @@
 
 def owned_slots(tiles, me, helper):
     found = []
+    row = helper[...]
     for h in range(helper.shape[1]):
-        tile = helper[0, h] - me * tiles
+        tile = row[0, h] - me * tiles
         found.append((h, (tile >= 0) & (tile < tiles), tile))
     return found
 
@@ -134,8 +135,9 @@
     return (lax.axis_index(axis) & 1) == 0
 
 
-def edges(velocity, x_one, x_two, y_one, y_two):
+def edges(helper, velocity, helper_near, x_one, x_two, y_one, y_two):
     depth, width = velocity.shape[1:3]
+    helper_near[...] = helper[...]
     even = is_even("gx")
     for a in range(3):
         first, last = velocity[a, 0], velocity[a, depth - 1]
@@ -149,25 +151,25 @@
             y_two[a, pl.ds(x, 1), :] = jnp.where(even, first, last)
 
 
-def call_edges(velocity):
+def call_edges(helper_tile, velocity):
     _, depth, width, length = velocity.shape
     along_x = jax.ShapeDtypeStruct((3, width, length), f32)
     along_y = jax.ShapeDtypeStruct((3, depth, length), f32)
     return pl.pallas_call(
         edges,
-        out_shape=(along_x, along_x, along_y, along_y),
-        in_specs=[vmem],
-        out_specs=(vmem,) * 4,
+        out_shape=(jax.ShapeDtypeStruct(helper_tile.shape, jnp.int32), along_x, along_x, along_y, along_y),
+        in_specs=[vmem, vmem],
+        out_specs=(vmem,) * 5,
         compiler_params=pltpu.CompilerParams(vmem_limit_bytes=4 << 20),
         cost_estimate=small(1 << 10, 1 << 17),
         name="edges",
-    )(velocity)
+    )(*far_memory(helper_tile, velocity))
 
 
 def two_swaps(one, two, axis):
     size = lax.axis_size(axis)
     within = [(i, i ^ 1) for i in range(size)]
-    across = [(i, min(max(i - 1 + 2 * (i & 1), 0), size - 1)) for i in range(size)]
+    across = [(i, (i - 1 + 2 * (i & 1)) % size) for i in range(size)]
     return lax.ppermute(one, axis, within), lax.ppermute(two, axis, across)
 
 
@@ -223,7 +225,7 @@
     return pl.pallas_call(
         heavy_moments,
         out_shape=jax.ShapeDtypeStruct((slots, 16, cells // LANES, LANES), f32),
-        in_specs=[smem, hbm, hbm],
+        in_specs=[vmem, hbm, hbm],
         out_specs=vmem,
         scratch_shapes=[
             pltpu.VMEM((slots, 3, count, cells), f32),
@@ -325,7 +327,7 @@
     return pl.pallas_call(
         functools.partial(gradients, tiles),
         out_shape=(jax.ShapeDtypeStruct((9 * depth * SUB, LANES), f32), half, half),
-        in_specs=[smem] + [vmem] * 7,
+        in_specs=[vmem] * 8,
         out_specs=(vmem,) * 3,
         compiler_params=pltpu.CompilerParams(vmem_limit_bytes=8 << 20),
         cost_estimate=small(4 << 20, 1 << 20),
@@ -572,21 +574,48 @@
     )(before, *near_memory(extra_fields, extra_noise), moments, kept, received)
 
 
-def heavy(bits, piece_count, helper, base, noise, grad, near, far, block, *refs):
-    pieces, (_, new_base, stress, fields, rows, answer, sems) = refs[:piece_count], refs[piece_count:]
+def finish(piece_count, before, block, *refs):
+    pieces, (_, new_base, rows, sems) = refs[:piece_count], refs[piece_count:]
+    _, depth, tiles, _ = rows.shape
+    last = block.shape[0]
+    flat = rows.reshape(6 * depth * tiles, LANES)
+    copies = [pltpu.make_async_copy(block.at[i], new_base.at[0, 0, tiles - last + i], sems.at[i]) for i in range(last)]
+    for copy in copies:
+        copy.start()
+    tile = 0
+    for piece in pieces:
+        for place in range(piece.shape[1]):
+            for i in range(6):
+                flat[pl.ds(i * depth * tiles + tile, depth, stride=tiles), :] = piece[i, place]
+            tile += 1
+    for copy in copies:
+        copy.wait()
+
+
+def call_finish(before, block, pieces, new_base):
+    tiles, cells = new_base.shape[2], new_base.shape[-1]
+    return pl.pallas_call(
+        functools.partial(finish, len(pieces)),
+        out_shape=(
+            jax.ShapeDtypeStruct(new_base.shape, f32),
+            jax.ShapeDtypeStruct((6, cells // LANES, tiles, LANES), f32),
+        ),
+        in_specs=[anywhere, vmem] + [vmem] * len(pieces) + [hbm],
+        out_specs=(hbm, vmem),
+        input_output_aliases={2 + len(pieces): 0},
+        scratch_shapes=[pltpu.SemaphoreType.DMA((block.shape[0],))],
+        compiler_params=pltpu.CompilerParams(vmem_limit_bytes=4 << 20),
+        cost_estimate=small(1 << 10, 1 << 20),
+        name="finish",
+    )(before, *near_memory(block), *pieces, new_base)
+
+
+def heavy(bits, helper, base, noise, grad, near, far, ready, old_base, new_base, stress, fields, rows, answer, sems):
     _, _, tiles, _, count, cells = base.shape
     slots = helper.shape[1]
     me = lax.axis_index("gy")
     depth = cells // LANES
-    last = block.shape[0]
     flat = rows.reshape(6 * depth * tiles, LANES)
-
-    def put_stress(tile, packed):
-        for i, value in enumerate(packed):
-            flat[pl.ds(i * depth * tiles + tile, depth, stride=tiles), :] = value
-
-    def leave(i):
-        return pltpu.make_async_copy(block.at[i], new_base.at[0, 0, tiles - last + i], sems.at[slots + depth + i])
 
     def store(h, tile):
         return pltpu.make_async_copy(fields.at[h], new_base.at[0, 0, tile], sems.at[h])
@@ -595,20 +624,20 @@
         target = stress.at[0, 0, :, :, pl.ds(x * LANES, LANES)]
         return pltpu.make_async_copy(rows.at[:, x], target, sems.at[slots + x])
 
-    for i in range(last):
-        leave(i).start()
-    tile = 0
-    for piece in pieces:
-        for place in range(piece.shape[1]):
-            put_stress(tile, [piece[i, place] for i in range(6)])
-            tile += 1
-
-    @pl.loop(0, slots)
-    def _(h):
-        tile = helper[0, h] - me * tiles
-
-        @pl.when((tile >= 0) & (tile < tiles))
-        def _():
+    rows[...] = ready[...]
+    found = owned_slots(tiles, me, helper)
+    places = jnp.int32(0)
+    order = [jnp.int32(0)] * HEAVY_MOST
+    for h, owned, tile in found:
+        entry = h * tiles + tile
+        order = [jnp.where(owned & (places == k), entry, kept) for k, kept in enumerate(order)]
+        places = places + owned.astype(jnp.int32)
+
+    for k, entry in enumerate(order):
+
+        @pl.when(k < places)
+        def _(entry=entry):
+            h, tile = entry // tiles, entry % tiles
             flips = me ^ h
             place = sum(((flips >> (bits - 1 - i)) & 1) << i for i in range(bits))
             is_far = place >= slots // 2
@@ -631,52 +660,46 @@
                     return noise[0, 0, tile, step, a, part, lanes]
 
                 totals.append(tile_sums(read, write, shock, matrices, count, add_moments, 6))
+            store(h, tile).start()
             sums = [packed_sum(list(same)) + answer[2 + i] for i, same in enumerate(zip(*totals))]
-            put_stress(tile, stress_rows(sums, 1.0 / ALL_FIELDS))
+            for i, value in enumerate(stress_rows(sums, 1.0 / ALL_FIELDS)):
+                flat[pl.ds(i * depth * tiles + tile, depth, stride=tiles), :] = value
 
     for x in range(depth):
         result(x).start()
-    for i in range(last):
-        leave(i).wait()
-
-    def each_owned(act):
-        @pl.loop(0, slots)
-        def _(h):
-            tile = helper[0, h] - me * tiles
-
-            @pl.when((tile >= 0) & (tile < tiles))
-            def _():
-                act(store(h, tile))
-
-    each_owned(lambda copy: copy.start())
+    for k, entry in enumerate(order):
+
+        @pl.when(k < places)
+        def _(entry=entry):
+            store(entry // tiles, entry % tiles).wait()
+
     for x in range(depth):
         result(x).wait()
-    each_owned(lambda copy: copy.wait())
-
-
-def call_heavy(bits, helper_tile, base_fields, base_noise, grad, near, far, block, pieces, new_base):
+
+
+def call_heavy(bits, helper_tile, base_fields, base_noise, grad, near, far, ready, new_base):
     _, _, tiles, _, count, cells = base_fields.shape
     depth = cells // LANES
     slots = helper_tile.shape[1]
     return pl.pallas_call(
-        functools.partial(heavy, bits, len(pieces)),
+        functools.partial(heavy, bits),
         out_shape=(
             jax.ShapeDtypeStruct(new_base.shape, f32),
             jax.ShapeDtypeStruct((1, 1, 6, tiles, cells), f32),
         ),
-        in_specs=[smem] + [vmem] * (6 + len(pieces)) + [hbm],
+        in_specs=[vmem] * 7 + [hbm],
         out_specs=(hbm, hbm),
-        input_output_aliases={7 + len(pieces): 0},
+        input_output_aliases={7: 0},
         scratch_shapes=[
             pltpu.VMEM((slots, 3, count, cells), f32),
             pltpu.VMEM((6, depth, tiles, LANES), f32),
             pltpu.VMEM(near.shape[1:], f32),
-            pltpu.SemaphoreType.DMA((slots + depth + block.shape[0],)),
+            pltpu.SemaphoreType.DMA((slots + depth,)),
         ],
         compiler_params=pltpu.CompilerParams(vmem_limit_bytes=SMALL),
         cost_estimate=small(8 << 20, 4 << 20),
         name="heavy_tiles",
-    )(helper_tile, *near_memory(base_fields, base_noise), grad, near, far, *near_memory(block), *pieces, new_base)
+    )(helper_tile, *near_memory(base_fields, base_noise), grad, near, far, ready, new_base)
 
 
 def per_device(
@@ -684,7 +707,7 @@
 ):
     tiles = tile_counts.shape[2]
     bits = lax.axis_size("gy").bit_length() - 1
-    x_one, x_two, y_one, y_two = call_edges(velocity)
+    helper_tile, x_one, x_two, y_one, y_two = call_edges(helper_tile, velocity)
     halos = two_swaps(x_one, x_two, "gx") + two_swaps(y_one, y_two, "gy")
     moments = call_heavy_moments(helper_tile, base_fields, base_noise)
     grad, keep, send = call_gradients(tiles, helper_tile, velocity, halos, wall_cells, moments)
@@ -719,9 +742,8 @@
             before, _ = fill(near)
         near = call_join(before, near, received)
     far = swapped(near, 0)
-    new_base, stress = call_heavy(
-        bits, helper_tile, base_fields, base_noise, grad, near, far, block, pieces, new_base
-    )
+    new_base, ready = call_finish(near, block, pieces, new_base)
+    new_base, stress = call_heavy(bits, helper_tile, base_fields, base_noise, grad, near, far, ready, new_base)
     return new_base, new_extra, jnp.swapaxes(stress, 2, 3)
 
 

time: 41 us -> 36.4 us (0.89)
  the two profiles are of different devices: /device:TPU:9 before, /device:TPU:0 now
where the time goes in v3:
time: 36.4 us; the launch traced here: 36.2 us
  starting transfers between devices  14.1 us (39%)
  Pallas kernels  13.8 us (38%)
  waiting for transfers between devices  6.81 us (19%)
  between operations  0.8 us (2%)
  local copies, waits for them, and re-layouts  0.79 us (2%)
    ppermute x4, starting transfers between devices, two_swaps(): return (lax.ppermute(one, axis, within), lax.ppermute(two, axis, across))  8.13 us
    ppermute x6, waiting for transfers between devices, swapped(): return lax.ppermute(block, 'gy', [(i, i ^ 1 << bit) for i in range(size)])  6.8 us
    ppermute x6, starting transfers between devices, swapped(): return lax.ppermute(block, 'gy', [(i, i ^ 1 << bit) for i in range(size)])  5.93 us
    pallas_call x4, Pallas kernels, call_ordinary(): pl.pallas_call(functools.partial(ordinary, first, has_block, has_base, ha...  4.35 us
    pallas_call x1, Pallas kernels, call_extra(): pl.pallas_call(functools.partial(extra, 7), out_shape=(pltpu.VMEM(extra_f...  2.25 us
    pallas_call x1, Pallas kernels, call_heavy_moments(): pl.pallas_call(heavy_moments, out_shape=jax.ShapeDtypeStruct((slots, 16,...  1.81 us
    pallas_call x1, Pallas kernels, call_extra_moments(): pl.pallas_call(functools.partial(extra_moments, 7), out_shape=jax.ShapeDt...  1.4 us
    pallas_call x1, Pallas kernels, call_heavy(): pl.pallas_call(functools.partial(heavy, bits), out_shape=(jax.ShapeDtypeS...  1.37 us
  transfers between devices with their start and end apart: 10, of which 6 were waited for; matrix products, arithmetic and copies ran while one was open for 0% of the time, Pallas kernels for 23%

profile of v3, /device:TPU:0, one launch (start us, length us, event | category | flops | bytes accessed | tf_op | source)
XLA Modules:
  0.0 36.2 jit_solution(2986368672084709421)
XLA Ops:
  0.6 0.9 %edges.1 = (s32[1,8]{1,0:T(1,128)S(1)}, f32[3,8,128]{2,1,0:T(8,128)S(1)}, f32[3,8,128]{2,1,0:T(8,128)S(1)}, f32[3,8,128]{2,1,0:T(8,128)S(1)}, f32[3,8,128]{2,1,0:T(8,128)S(1)}) custom-call(s32[1,8]{1,0:T(1,128)} %helper.1, f32[3,8,8,128]{3,2,1,0:T(8,128)} %velocity.3), custom_call_target="tpu_custom_call" | custom-call | flops 1024 | bytes 131072 | tf_op jit(solution)/shard_map/edges/pallas_call | solution.py:158
  1.6 3.1 %collective-permute-start = (f32[3,8,128]{2,1,0:T(8,128)S(1)}, f32[3,8,128]{2,1,0:T(8,128)S(1)}, u32[]{:S(2)}, u32[]{:S(2)}) collective-permute-start(f32[3,8,128]{2,1,0:T(8,128)S(1)} %get-tuple-element.34), channel_id=1, source_target_pairs={{0,8},{8,0},{16,24},{24,16},{1,9},{9,1},{17,25},{25,17},{2,10},{10... | collective-permute-start | bytes 36872 | tf_op jit(solution)/shard_map/ppermute | solution.py:173
  4.7 2.5 %collective-permute-start.1 = (f32[3,8,128]{2,1,0:T(8,128)S(1)}, f32[3,8,128]{2,1,0:T(8,128)S(1)}, u32[]{:S(2)}, u32[]{:S(2)}) collective-permute-start(f32[3,8,128]{2,1,0:T(8,128)S(1)} %get-tuple-element.35), channel_id=1, source_target_pairs={{0,24},{8,16},{16,8},{24,0},{1,25},{9,17},{17,9},{25,1},{2,26},{10... | collective-permute-start | bytes 36872 | tf_op jit(solution)/shard_map/ppermute | solution.py:173
  7.1 0.0 collective-permute-start.2
  7.1 2.6 %collective-permute-start.3 = (f32[3,8,128]{2,1,0:T(8,128)S(1)}, f32[3,8,128]{2,1,0:T(8,128)S(1)}, u32[]{:S(2)}, u32[]{:S(2)}) collective-permute-start(f32[3,8,128]{2,1,0:T(8,128)S(1)} %get-tuple-element.37), channel_id=1, source_target_pairs={{0,7},{1,2},{2,1},{3,4},{4,3},{5,6},{6,5},{7,0},{8,15},{9,10},{10,... | collective-permute-start | bytes 36872 | tf_op jit(solution)/shard_map/ppermute | solution.py:173
  9.7 1.8 %heavy_moments.1.moments = f32[8,16,8,128]{3,2,1,0:T(8,128)S(1)} custom-call(s32[1,8]{1,0:T(1,128)S(1)} %get-tuple-element.33.helper, f32[1,1,8,3,32,1024]{5,4,3,2,1,0:T(8,128)} %base.7, bf16[1,1,8,2,3,32,1024]{6,5,4,3,2,1,0:T(8,128)(2,1)} %noise.7), custom_call_target="tpu_custom_call" | custom-call | flops 8388608 | bytes 3145728 | tf_op jit(solution)/shard_map/heavy_moments/pallas_call | solution.py:225
  11.5 0.0 collective-permute-done.x_one
  11.5 0.0 collective-permute-done.1.x_two
  11.5 0.0 collective-permute-done.2.y_one
  11.6 0.7 %gradients.1 = (f32[576,128]{1,0:T(8,128)S(1)}, f32[4,12,8,128]{3,2,1,0:T(8,128)S(1)}, f32[4,12,8,128]{3,2,1,0:T(8,128)S(1)}) custom-call(s32[1,8]{1,0:T(1,128)S(1)} %get-tuple-element.33.helper, f32[3,8,8,128]{3,2,1,0:T(8,128)S(1)} %copy-done.4, f32[3,8,128]{2,1,0:T(8,128)S(1)} %collective-permute-done.x_one, ...), custom_call_target="tpu_custom_call" | custom-call | flops 4194304 | bytes 1048576 | tf_op jit(solution)/shard_map/gradients/pallas_call | solution.py:327
  12.3 0.1 collective-permute-start.4
  12.4 0.4 %copy-done.1 = bf16[1,1,8,2,3,32,1024]{6,5,4,3,2,1,0:T(8,128)(2,1)S(1)} copy-done((bf16[1,1,8,2,3,32,1024]{6,5,4,3,2,1,0:T(8,128)(2,1)S(1)}, bf16[1,1,8,2,3,32,1024]{6,5,4,3,2,1,0:T(8,128)(2,1)}, u32[]{:S(2)}) %copy-start.1) | copy-done | bytes 3145752
  12.8 0.7 %ordinary_tiles.4 = (f32[2,3,32,1024]{3,2,1,0:T(8,128)S(1)}, f32[6,2,8,128]{3,2,1,0:T(8,128)S(1)}) custom-call(f32[4,12,8,128]{3,2,1,0:T(8,128)S(1)} %get-tuple-element.39.refs_0_, f32[1,1,8,3,32,1024]{5,4,3,2,1,0:T(8,128)S(1)} %copy-done, bf16[1,1,8,2,3,32,1024]{6,5,4,3,2,1,0:T(8,128)(2,1)S(1)} %copy-done.1, f32[576,128]{1,0:T(8,128)S(1)} %get-tuple-element.38.refs_3_.grad), custom_call_target="tpu_custom_call" | custom-call | flops 8388608 | bytes 3145728 | tf_op jit(solution)/shard_map/ordinary_tiles/pallas_call | solution.py:505
  13.6 0.2 collective-permute-done.4.received
  13.8 1.3 %collective-permute-start.5 = (f32[2,12,8,128]{3,2,1,0:T(8,128)S(1)}, f32[2,12,8,128]{3,2,1,0:T(8,128)S(1)}, u32[]{:S(2)}, u32[]{:S(2)}) collective-permute-start(f32[2,12,8,128]{3,2,1,0:T(8,128)S(1)} %get-tuple-element.42.before), channel_id=1, source_target_pairs={{0,2},{1,3},{2,0},{3,1},{4,6},{5,7},{6,4},{7,5},{8,10},{9,11},{10,... | collective-permute-start | bytes 294920 | tf_op jit(solution)/shard_map/ppermute | solution.py:340
  15.1 0.3 copy-done.3
  15.4 1.4 %extra_moments.1.before.moments = f32[16,8,128]{2,1,0:T(8,128)S(1)} custom-call(f32[2,12,8,128]{3,2,1,0:T(8,128)S(1)} %get-tuple-element.42.before, f32[1,1,3,224,1024]{4,3,2,1,0:T(8,128)S(1)} %copy-done.2, bf16[1,1,2,3,224,1024]{5,4,3,2,1,0:T(8,128)(2,1)S(1)} %copy-done.3), custom_call_target="tpu_custom_call" | custom-call | flops 8388608 | bytes 5242880 | tf_op jit(solution)/shard_map/extra_moments/pallas_call | solution.py:263
  16.8 1.9 %collective-permute-done.5.received = f32[2,12,8,128]{3,2,1,0:T(8,128)S(1)} collective-permute-done((f32[2,12,8,128]{3,2,1,0:T(8,128)S(1)}, f32[2,12,8,128]{3,2,1,0:T(8,128)S(1)}, u32[]{:S(2)}, u32[]{:S(2)}) %collective-permute-start.5) | collective-permute-done | bytes 98336 | tf_op jit(solution)/shard_map/ppermute | solution.py:340
  18.7 1.5 %collective-permute-start.6 = (f32[1,12,8,128]{3,2,1,0:T(8,128)S(1)}, f32[1,12,8,128]{3,2,1,0:T(8,128)S(1)}, u32[]{:S(2)}, u32[]{:S(2)}) collective-permute-start(f32[1,12,8,128]{3,2,1,0:T(8,128)S(1)} %get-tuple-element.44.refs_0_), channel_id=1, source_target_pairs={{0,4},{1,5},{2,6},{3,7},{4,0},{5,1},{6,2},{7,3},{8,12},{9,13},{10,... | collective-permute-start | bytes 147464 | tf_op jit(solution)/shard_map/ppermute | solution.py:340
  20.3 0.9 %ordinary_tiles.5 = (f32[1,1,8,3,32,1024]{5,4,3,2,1,0:T(8,128)}, f32[2,3,32,1024]{3,2,1,0:T(8,128)S(1)}, f32[6,2,8,128]{3,2,1,0:T(8,128)S(1)}) custom-call(f32[1,12,8,128]{3,2,1,0:T(8,128)S(1)} %get-tuple-element.44.refs_0_, f32[1,1,8,3,32,1024]{5,4,3,2,1,0:T(8,128)S(1)} %copy-done, bf16[1,1,8,2,3,32,1024]{6,5,4,3,2,1,0:T(8,128)(2,1)S(1)} %copy-done.1, ...), custom_call_target="tpu_custom_call" | custom-call | flops 8388608 | bytes 3145728 | tf_op jit(solution)/shard_map/ordinary_tiles/pallas_call | solution.py:505
  21.2 1.7 %collective-permute-done.6.received = f32[1,12,8,128]{3,2,1,0:T(8,128)S(1)} collective-permute-done((f32[1,12,8,128]{3,2,1,0:T(8,128)S(1)}, f32[1,12,8,128]{3,2,1,0:T(8,128)S(1)}, u32[]{:S(2)}, u32[]{:S(2)}) %collective-permute-start.6) | collective-permute-done | bytes 49184 | tf_op jit(solution)/shard_map/ppermute | solution.py:340
  22.9 2.3 %extra_fields.1 = (f32[1,1,3,224,1024]{4,3,2,1,0:T(8,128)S(1)}, f32[8,8,128]{2,1,0:T(8,128)S(1)}) custom-call(f32[6,2,8,128]{3,2,1,0:T(8,128)S(1)} %get-tuple-element.46.before.refs_1_, f32[1,1,3,224,1024]{4,3,2,1,0:T(8,128)S(1)} %copy-done.2, bf16[1,1,2,3,224,1024]{5,4,3,2,1,0:T(8,128)(2,1)S(1)} %copy-done.3, ...), custom_call_target="tpu_custom_call" | custom-call | flops 33554432 | bytes 9437184 | tf_op jit(solution)/shard_map/extra_fields/pallas_call | solution.py:562
  25.2 1.5 %collective-permute-start.7 = (f32[1,8,8,128]{3,2,1,0:T(8,128)S(1)}, f32[1,8,8,128]{3,2,1,0:T(8,128)S(1)}, u32[]{:S(2)}, u32[]{:S(2)}) collective-permute-start(f32[1,8,8,128]{3,2,1,0:T(8,128)S(1)} %bitcast.2), channel_id=1, source_target_pairs={{0,4},{1,5},{2,6},{3,7},{4,0},{5,1},{6,2},{7,3},{8,12},{9,13},{10,... | collective-permute-start | bytes 98312 | tf_op jit(solution)/shard_map/ppermute | solution.py:340
  26.7 1.8 %ordinary_tiles.6 = (f32[1,1,8,3,32,1024]{5,4,3,2,1,0:T(8,128)}, f32[1,1,3,224,1024]{4,3,2,1,0:T(8,128)}, f32[2,3,32,1024]{3,2,1,0:T(8,128)S(1)}, f32[6,2,8,128]{3,2,1,0:T(8,128)S(1)}) custom-call(f32[1,8,8,128]{3,2,1,0:T(8,128)S(1)} %bitcast.3, f32[1,1,8,3,32,1024]{5,4,3,2,1,0:T(8,128)S(1)} %copy-done, ...), custom_call_target="tpu_custom_call", output_to_operand_aliasing={{0}: (5, {})} | custom-call | flops 8388608 | bytes 3145728 | tf_op jit(solution)/shard_map/ordinary_tiles/pallas_call | solution.py:505
  28.5 0.6 %collective-permute-done.7.second = f32[1,8,8,128]{3,2,1,0:T(8,128)S(1)} collective-permute-done((f32[1,8,8,128]{3,2,1,0:T(8,128)S(1)}, f32[1,8,8,128]{3,2,1,0:T(8,128)S(1)}, u32[]{:S(2)}, u32[]{:S(2)}) %collective-permute-start.7) | collective-permute-done | bytes 32800 | tf_op jit(solution)/shard_map/ppermute | solution.py:340
  29.1 1.4 %collective-permute-start.8 = (f32[2,8,8,128]{3,2,1,0:T(8,128)S(1)}, f32[2,8,8,128]{3,2,1,0:T(8,128)S(1)}, u32[]{:S(2)}, u32[]{:S(2)}) collective-permute-start(f32[2,8,8,128]{3,2,1,0:T(8,128)S(1)} %join.2.refs_0_.first), channel_id=1, source_target_pairs={{0,2},{1,3},{2,0},{3,1},{4,6},{5,7},{6,4},{7,5},{8,10},{9,11},{10,... | collective-permute-start | bytes 196616 | tf_op jit(solution)/shard_map/ppermute | solution.py:340
  30.6 0.9 %ordinary_tiles.7 = (f32[1,1,8,3,32,1024]{5,4,3,2,1,0:T(8,128)}, f32[2,3,32,1024]{3,2,1,0:T(8,128)S(1)}, f32[6,2,8,128]{3,2,1,0:T(8,128)S(1)}) custom-call(f32[2,8,8,128]{3,2,1,0:T(8,128)S(1)} %join.2.refs_0_.first, f32[1,1,8,3,32,1024]{5,4,3,2,1,0:T(8,128)S(1)} %copy-done, ...), custom_call_target="tpu_custom_call", output_to_operand_aliasing={{0}: (5, {})} | custom-call | flops 8388608 | bytes 3145728 | tf_op jit(solution)/shard_map/ordinary_tiles/pallas_call | solution.py:505
  31.5 1.9 %collective-permute-done.8.second = f32[2,8,8,128]{3,2,1,0:T(8,128)S(1)} collective-permute-done((f32[2,8,8,128]{3,2,1,0:T(8,128)S(1)}, f32[2,8,8,128]{3,2,1,0:T(8,128)S(1)}, u32[]{:S(2)}, u32[]{:S(2)}) %collective-permute-start.8) | collective-permute-done | bytes 65568 | tf_op jit(solution)/shard_map/ppermute | solution.py:340
  33.4 0.1 collective-permute-start.9
  33.5 0.9 %finish.1 = (f32[1,1,8,3,32,1024]{5,4,3,2,1,0:T(8,128)}, f32[6,8,8,128]{3,2,1,0:T(8,128)S(1)}) custom-call(f32[4,8,8,128]{3,2,1,0:T(8,128)S(1)} %join.3.before.near, f32[2,3,32,1024]{3,2,1,0:T(8,128)S(1)} %get-tuple-element.56.block, f32[6,2,8,128]{3,2,1,0:T(8,128)S(1)} %get-tuple-element.40.before.refs_0_, ...), custom_call_target="tpu_custom_call", output_to_operand_aliasing={{0}: (6, {})} | custom-call | flops 1024 | bytes 1048576 | tf_op jit(solution)/shard_map/finish/pallas_call | solution.py:597
  34.4 0.4 %collective-permute-done.9.far = f32[4,8,8,128]{3,2,1,0:T(8,128)S(1)} collective-permute-done((f32[4,8,8,128]{3,2,1,0:T(8,128)S(1)}, f32[4,8,8,128]{3,2,1,0:T(8,128)S(1)}, u32[]{:S(2)}, u32[]{:S(2)}) %collective-permute-start.9) | collective-permute-done | bytes 131104 | tf_op jit(solution)/shard_map/ppermute | solution.py:340
  34.8 1.4 %heavy_tiles.1 = (f32[1,1,8,3,32,1024]{5,4,3,2,1,0:T(8,128)}, f32[1,1,6,8,1024]{4,3,2,1,0:T(8,128)}) custom-call(s32[1,8]{1,0:T(1,128)S(1)} %get-tuple-element.33.helper, f32[1,1,8,3,32,1024]{5,4,3,2,1,0:T(8,128)S(1)} %copy-done, bf16[1,1,8,2,3,32,1024]{6,5,4,3,2,1,0:T(8,128)(2,1)S(1)} %copy-done.1, ...), custom_call_target="tpu_custom_call", output_to_operand_aliasing={{0}: (7, {})} | custom-call | flops 8388608 | bytes 4194304 | tf_op jit(solution)/shard_map/heavy_tiles/pallas_call | solution.py:684
  (15 shorter events, 0.1 us)
Async XLA Ops:
  1.6 10.0 %collective-permute-start = (f32[3,8,128]{2,1,0:T(8,128)S(1)}, f32[3,8,128]{2,1,0:T(8,128)S(1)}, u32[]{:S(2)}, u32[]{:S(2)}) collective-permute-start(f32[3,8,128]{2,1,0:T(8,128)S(1)} %get-tuple-element.34), channel_id=1, source_target_pairs={{0,8},{8,0},{16,24},{24,16},{1,9},{9,1},{17,25},{25,17},{2,10},{10... | collective-permute-start | bytes 36872 | tf_op jit(solution)/shard_map/ppermute | solution.py:173
  4.7 6.9 %collective-permute-start.1 = (f32[3,8,128]{2,1,0:T(8,128)S(1)}, f32[3,8,128]{2,1,0:T(8,128)S(1)}, u32[]{:S(2)}, u32[]{:S(2)}) collective-permute-start(f32[3,8,128]{2,1,0:T(8,128)S(1)} %get-tuple-element.35), channel_id=1, source_target_pairs={{0,24},{8,16},{16,8},{24,0},{1,25},{9,17},{17,9},{25,1},{2,26},{10... | collective-permute-start | bytes 36872 | tf_op jit(solution)/shard_map/ppermute | solution.py:173
  7.1 4.4 %collective-permute-start.2 = (f32[3,8,128]{2,1,0:T(8,128)S(1)}, f32[3,8,128]{2,1,0:T(8,128)S(1)}, u32[]{:S(2)}, u32[]{:S(2)}) collective-permute-start(f32[3,8,128]{2,1,0:T(8,128)S(1)} %get-tuple-element.36), channel_id=1, source_target_pairs={{0,1},{1,0},{2,3},{3,2},{4,5},{5,4},{6,7},{7,6},{8,9},{9,8},{10,11... | collective-permute-start | bytes 36872 | tf_op jit(solution)/shard_map/ppermute | solution.py:173
  7.1 4.4 %collective-permute-start.3 = (f32[3,8,128]{2,1,0:T(8,128)S(1)}, f32[3,8,128]{2,1,0:T(8,128)S(1)}, u32[]{:S(2)}, u32[]{:S(2)}) collective-permute-start(f32[3,8,128]{2,1,0:T(8,128)S(1)} %get-tuple-element.37), channel_id=1, source_target_pairs={{0,7},{1,2},{2,1},{3,4},{4,3},{5,6},{6,5},{7,0},{8,15},{9,10},{10,... | collective-permute-start | bytes 36872 | tf_op jit(solution)/shard_map/ppermute | solution.py:173
  9.7 1.9 %copy-start.4 = (f32[3,8,8,128]{3,2,1,0:T(8,128)S(1)}, f32[3,8,8,128]{3,2,1,0:T(8,128)}, u32[]{:S(2)}) copy-start(f32[3,8,8,128]{3,2,1,0:T(8,128)} %velocity.3) | copy-start | bytes 294916
  9.7 1.9 %copy-start.5 = (s32[8,8,128]{2,1,0:T(8,128)S(1)}, s32[8,8,128]{2,1,0:T(8,128)}, u32[]{:S(2)}) copy-start(s32[8,8,128]{2,1,0:T(8,128)} %wall.1) | copy-start | bytes 98308
  9.7 2.7 %copy-start = (f32[1,1,8,3,32,1024]{5,4,3,2,1,0:T(8,128)S(1)}, f32[1,1,8,3,32,1024]{5,4,3,2,1,0:T(8,128)}, u32[]{:S(2)}) copy-start(f32[1,1,8,3,32,1024]{5,4,3,2,1,0:T(8,128)} %base.7) | copy-start | bytes 9437188
  9.7 3.1 %copy-start.1 = (bf16[1,1,8,2,3,32,1024]{6,5,4,3,2,1,0:T(8,128)(2,1)S(1)}, bf16[1,1,8,2,3,32,1024]{6,5,4,3,2,1,0:T(8,128)(2,1)}, u32[]{:S(2)}) copy-start(bf16[1,1,8,2,3,32,1024]{6,5,4,3,2,1,0:T(8,128)(2,1)} %noise.7) | copy-start | bytes 9437188
  12.3 1.5 %collective-permute-start.4 = (f32[4,12,8,128]{3,2,1,0:T(8,128)S(1)}, f32[4,12,8,128]{3,2,1,0:T(8,128)S(1)}, u32[]{:S(2)}, u32[]{:S(2)}) collective-permute-start(f32[4,12,8,128]{3,2,1,0:T(8,128)S(1)} %get-tuple-element.39.refs_0_), channel_id=1, source_target_pairs={{0,1},{1,0},{2,3},{3,2},{4,5},{5,4},{6,7},{7,6},{8,9},{9,8},{10,11... | collective-permute-start | bytes 589832 | tf_op jit(solution)/shard_map/ppermute | solution.py:340
  12.8 2.3 %copy-start.2 = (f32[1,1,3,224,1024]{4,3,2,1,0:T(8,128)S(1)}, f32[1,1,3,224,1024]{4,3,2,1,0:T(8,128)}, u32[]{:S(2)}) copy-start(f32[1,1,3,224,1024]{4,3,2,1,0:T(8,128)} %base.6) | copy-start | bytes 8257540
  12.8 2.6 %copy-start.3 = (bf16[1,1,2,3,224,1024]{5,4,3,2,1,0:T(8,128)(2,1)S(1)}, bf16[1,1,2,3,224,1024]{5,4,3,2,1,0:T(8,128)(2,1)}, u32[]{:S(2)}) copy-start(bf16[1,1,2,3,224,1024]{5,4,3,2,1,0:T(8,128)(2,1)} %noise.6) | copy-start | bytes 8257540
  13.8 4.9 %collective-permute-start.5 = (f32[2,12,8,128]{3,2,1,0:T(8,128)S(1)}, f32[2,12,8,128]{3,2,1,0:T(8,128)S(1)}, u32[]{:S(2)}, u32[]{:S(2)}) collective-permute-start(f32[2,12,8,128]{3,2,1,0:T(8,128)S(1)} %get-tuple-element.42.before), channel_id=1, source_target_pairs={{0,2},{1,3},{2,0},{3,1},{4,6},{5,7},{6,4},{7,5},{8,10},{9,11},{10,... | collective-permute-start | bytes 294920 | tf_op jit(solution)/shard_map/ppermute | solution.py:340
  18.7 4.2 %collective-permute-start.6 = (f32[1,12,8,128]{3,2,1,0:T(8,128)S(1)}, f32[1,12,8,128]{3,2,1,0:T(8,128)S(1)}, u32[]{:S(2)}, u32[]{:S(2)}) collective-permute-start(f32[1,12,8,128]{3,2,1,0:T(8,128)S(1)} %get-tuple-element.44.refs_0_), channel_id=1, source_target_pairs={{0,4},{1,5},{2,6},{3,7},{4,0},{5,1},{6,2},{7,3},{8,12},{9,13},{10,... | collective-permute-start | bytes 147464 | tf_op jit(solution)/shard_map/ppermute | solution.py:340
  25.2 4.0 %collective-permute-start.7 = (f32[1,8,8,128]{3,2,1,0:T(8,128)S(1)}, f32[1,8,8,128]{3,2,1,0:T(8,128)S(1)}, u32[]{:S(2)}, u32[]{:S(2)}) collective-permute-start(f32[1,8,8,128]{3,2,1,0:T(8,128)S(1)} %bitcast.2), channel_id=1, source_target_pairs={{0,4},{1,5},{2,6},{3,7},{4,0},{5,1},{6,2},{7,3},{8,12},{9,13},{10,... | collective-permute-start | bytes 98312 | tf_op jit(solution)/shard_map/ppermute | solution.py:340
  29.1 4.3 %collective-permute-start.8 = (f32[2,8,8,128]{3,2,1,0:T(8,128)S(1)}, f32[2,8,8,128]{3,2,1,0:T(8,128)S(1)}, u32[]{:S(2)}, u32[]{:S(2)}) collective-permute-start(f32[2,8,8,128]{3,2,1,0:T(8,128)S(1)} %join.2.refs_0_.first), channel_id=1, source_target_pairs={{0,2},{1,3},{2,0},{3,1},{4,6},{5,7},{6,4},{7,5},{8,10},{9,11},{10,... | collective-permute-start | bytes 196616 | tf_op jit(solution)/shard_map/ppermute | solution.py:340
  33.4 1.4 %collective-permute-start.9 = (f32[4,8,8,128]{3,2,1,0:T(8,128)S(1)}, f32[4,8,8,128]{3,2,1,0:T(8,128)S(1)}, u32[]{:S(2)}, u32[]{:S(2)}) collective-permute-start(f32[4,8,8,128]{3,2,1,0:T(8,128)S(1)} %join.3.before.near), channel_id=1, source_target_pairs={{0,1},{1,0},{2,3},{3,2},{4,5},{5,4},{6,7},{7,6},{8,9},{9,8},{10,11... | collective-permute-start | bytes 393224 | tf_op jit(solution)/shard_map/ppermute | solution.py:340

commit v4 on v3

--- a/solution.py
+++ b/solution.py
@@ -12,7 +12,6 @@
 LANES = 128
 SUB = 8
 SMALL = 10 << 20
-LARGE = 14 << 20
 
 time_step = 0.05
 weissenberg = 0.25
@@ -39,17 +38,20 @@
     return jnp.sum(value, axis=0, keepdims=True)
 
 
-def packed_sum(values):
-    sub = lax.broadcasted_iota(jnp.int32, (SUB, LANES), 0)
-    bit = 1
-    while len(values) > 1:
-        low = (sub & bit) == 0
-        values = [
-            jnp.where(low, a, b) + pltpu.roll(jnp.where(low, b, a), bit, 0)
-            for a, b in zip(values[0::2], values[1::2])
-        ]
-        bit *= 2
-    return values[0]
+def interleaved(a, b, bit):
+    low = (lax.broadcasted_iota(jnp.int32, (SUB, LANES), 0) & bit) == 0
+    return jnp.where(low, a, b) + pltpu.roll(jnp.where(low, b, a), bit, 0)
+
+
+def packed_sums(values_of, count):
+    stack = []
+    for x in range(count):
+        bit, values = 1, values_of(x)
+        while stack and stack[-1][0] == bit:
+            values = [interleaved(a, b, bit) for a, b in zip(stack.pop()[1], values)]
+            bit *= 2
+        stack.append((bit, values))
+    return stack[0][1]
 
 
 def wide(row):
@@ -127,6 +129,16 @@
     return found
 
 
+def owned_order(tiles, me, helper):
+    places = jnp.int32(0)
+    order = [jnp.int32(0)] * HEAVY_MOST
+    for h, owned, tile in owned_slots(tiles, me, helper):
+        entry = h * tiles + tile
+        order = [jnp.where(owned & (places == k), entry, kept) for k, kept in enumerate(order)]
+        places = places + owned.astype(jnp.int32)
+    return places, [(entry // tiles, entry % tiles) for entry in order]
+
+
 def small(flops, traffic):
     return pl.CostEstimate(flops=flops, bytes_accessed=traffic, transcendentals=0)
 
@@ -181,42 +193,43 @@
 
 
 def heavy_moments(helper, base, noise, out, fields, shocks, sems):
-    slots, _, count, cells = fields.shape
+    _, _, count, cells = fields.shape
     tiles = base.shape[2]
     me = lax.axis_index("gy")
 
-    def loads(h, tile):
+    def loads(k, tile):
         return (
-            pltpu.make_async_copy(base.at[0, 0, tile], fields.at[h], sems.at[0, h]),
-            pltpu.make_async_copy(noise.at[0, 0, tile, 0], shocks.at[h], sems.at[1, h]),
+            pltpu.make_async_copy(base.at[0, 0, tile], fields.at[k], sems.at[0, k]),
+            pltpu.make_async_copy(noise.at[0, 0, tile, 0], shocks.at[k], sems.at[1, k]),
         )
 
-    found = owned_slots(tiles, me, helper)
-    for h, owned, tile in found:
-
-        @pl.when(owned)
-        def _(h=h, tile=tile):
-            for copy in loads(h, tile):
+    places, order = owned_order(tiles, me, helper)
+    for k, (_, tile) in enumerate(order):
+
+        @pl.when(k < places)
+        def _(k=k, tile=tile):
+            for copy in loads(k, tile):
                 copy.start()
 
-    for h, owned, tile in found:
-
-        @pl.when(owned)
-        def _(h=h, tile=tile):
-            for copy in loads(h, tile):
+    for k, (h, tile) in enumerate(order):
+
+        @pl.when(k < places)
+        def _(k=k, h=h, tile=tile):
+            for copy in loads(k, tile):
                 copy.wait()
 
-            @pl.loop(0, cells // LANES)
-            def _(x):
-                lanes = pl.ds(pl.multiple_of(x * LANES, LANES), LANES)
+            def sums_of(x):
+                lanes = pl.ds(x * LANES, LANES)
                 sums = [jnp.zeros((SUB, LANES), f32)] * 16
                 for group in range(count // (2 * SUB)):
-                    pair = noise_rows(lambda a, rows: shocks[h, a, rows, lanes], group * 2 * SUB)
+                    pair = noise_rows(lambda a, rows: shocks[k, a, rows, lanes], group * 2 * SUB)
                     for half in range(2):
                         rows = pl.ds((2 * group + half) * SUB, SUB)
-                        sums = product_sums(sums, [fields[h, a, rows, lanes] for a in range(3)], pair[half])
-                for i, s in enumerate(sums):
-                    out[h, i, pl.ds(x, 1), :] = column_sum(s)
+                        sums = product_sums(sums, [fields[k, a, rows, lanes] for a in range(3)], pair[half])
+                return sums
+
+            for i, value in enumerate(packed_sums(sums_of, cells // LANES)):
+                out[h, i] = value
 
 
 def call_heavy_moments(helper_tile, base_fields, base_noise):
@@ -228,11 +241,11 @@
         in_specs=[vmem, hbm, hbm],
         out_specs=vmem,
         scratch_shapes=[
-            pltpu.VMEM((slots, 3, count, cells), f32),
-            pltpu.VMEM((slots, 3, count, cells), jnp.bfloat16),
-            pltpu.SemaphoreType.DMA((2, slots)),
+            pltpu.VMEM((HEAVY_MOST, 3, count, cells), f32),
+            pltpu.VMEM((HEAVY_MOST, 3, count, cells), jnp.bfloat16),
+            pltpu.SemaphoreType.DMA((2, HEAVY_MOST)),
         ],
-        compiler_params=pltpu.CompilerParams(vmem_limit_bytes=LARGE),
+        compiler_params=pltpu.CompilerParams(vmem_limit_bytes=SMALL),
         cost_estimate=small(8 << 20, 3 << 20),
         name="heavy_moments",
     )(helper_tile, *far_memory(base_fields, base_noise))
@@ -335,47 +348,45 @@
     )(helper_tile, velocity, *halos, wall_cells, moments)
 
 
-def swapped(block, bit):
+def swapped(block, flip):
     size = lax.axis_size("gy")
-    return lax.ppermute(block, "gy", [(i, i ^ (1 << bit)) for i in range(size)])
-
-
-def merge(bit, before, kept, received, keep, send):
-    mine = (lax.axis_index("gy") >> (bit + 1)) & 1
-    for j in range(0, kept.shape[0], 2):
-        for i in range(kept.shape[1]):
-            even, odd = [kept[k, i] + received[k, i] for k in (j, j + 1)]
-            keep[j // 2, i] = jnp.where(mine == 0, even, odd)
-            send[j // 2, i] = jnp.where(mine == 0, odd, even)
-
-
-def call_merge(bit, before, kept, received):
-    half = jax.ShapeDtypeStruct((kept.shape[0] // 2,) + kept.shape[1:], f32)
-    return pl.pallas_call(
-        functools.partial(merge, bit),
-        out_shape=(half, half),
+    return lax.ppermute(block, "gy", [(i, i ^ flip) for i in range(size)])
+
+
+def merge(before, kept, received, keep, *sends):
+    pair = lax.axis_index("gy") >> 1
+    for flip, out in enumerate((keep,) + sends):
+        out[...] = kept[pair ^ flip] + received[pair ^ flip]
+
+
+def call_merge(before, kept, received):
+    one = jax.ShapeDtypeStruct(kept.shape[1:], f32)
+    return pl.pallas_call(
+        merge,
+        out_shape=(one,) * kept.shape[0],
         in_specs=[anywhere, vmem, vmem],
-        out_specs=(vmem, vmem),
+        out_specs=(vmem,) * kept.shape[0],
         compiler_params=pltpu.CompilerParams(vmem_limit_bytes=4 << 20),
         cost_estimate=small(1 << 10, 1 << 18),
         name="merge",
     )(before, kept, received)
 
 
-def call_join(before, first, second):
-    def join(before, first, second, out):
-        out[: first.shape[0]] = first[...]
-        out[first.shape[0] :] = second[...]
-
+def join(before, *refs):
+    for i, ref in enumerate(refs[:-1]):
+        refs[-1][i] = ref[...]
+
+
+def call_join(before, blocks):
     return pl.pallas_call(
         join,
-        out_shape=jax.ShapeDtypeStruct((2 * first.shape[0],) + first.shape[1:], f32),
-        in_specs=[anywhere, vmem, vmem],
+        out_shape=jax.ShapeDtypeStruct((len(blocks),) + blocks[0].shape, f32),
+        in_specs=[anywhere] + [vmem] * len(blocks),
         out_specs=vmem,
         compiler_params=pltpu.CompilerParams(vmem_limit_bytes=4 << 20),
         cost_estimate=small(1 << 10, 1 << 18),
         name="join",
-    )(before, first, second)
+    )(before, *blocks)
 
 
 def stress_rows(sums, inverse):
@@ -436,18 +447,20 @@
         copy.start()
     for place in range(here):
         tile = first + place
-        totals = []
-        for x in range(depth):
+
+        def squares(x):
             total = jnp.zeros((SUB, LANES), f32)
             for group in range(count // SUB):
                 for a in range(3):
                     q = base[0, 0, tile, a, pl.ds(group * SUB, SUB), pl.ds(x * LANES, LANES)]
                     total = total + q * q
-            totals.append(total)
+            return [total]
+
+        sums = packed_sums(squares, depth)
         for step in range(2):
-            relaxes[place, step] = relax_of(packed_sum(totals), inverse)
-            totals = []
-            for x in range(depth):
+            relaxes[place, step] = relax_of(sums[0], inverse)
+
+            def sums_of(x):
                 lanes = pl.ds(x * LANES, LANES)
                 matrix = with_diagonal(tile_grad(grad, depth, tile, x), wide(relaxes[place, step, pl.ds(x, 1), :]))
 
@@ -464,10 +477,11 @@
                     return noise[0, 0, tile, step, a, rows, lanes]
 
                 if step == 0:
-                    totals += tile_sums(read, write, shock, [matrix], count, add_square, 1)
-                else:
-                    totals.append(tile_sums(read, write, shock, [matrix], count, add_moments, 6))
-        for i, row in enumerate(stress_rows([packed_sum(list(same)) for same in zip(*totals)], inverse)):
+                    return tile_sums(read, write, shock, [matrix], count, add_square, 1)
+                return tile_sums(read, write, shock, [matrix], count, add_moments, 6)
+
+            sums = packed_sums(sums_of, depth)
+        for i, row in enumerate(stress_rows(sums, inverse)):
             stress[i, place] = row
     for copy in copies:
         copy.wait()
@@ -523,11 +537,12 @@
     return new_base, block, piece, (results[0] if has_extra else None)
 
 
-def extra(unroll, before, base, noise, moments, kept, received, new_fields, reply, message):
+def extra(unroll, before, base, noise, moments, *refs):
+    *parts, new_fields, reply, message = refs
     _, _, _, count, cells = base.shape
     inverse = 1.0 / float(ALL_FIELDS)
     zero = jnp.zeros((SUB, LANES), f32)
-    message[...] = kept[0] + received[0]
+    message[...] = sum(part[...] for part in parts)
     own = coefficients([message[i] for i in range(9)], [moments[i] for i in range(16)])
     both = [message[9 + i] + own[i] for i in range(3)]
     first = relax_of(both[2], inverse)
@@ -557,7 +572,7 @@
             reply[2 + i, pl.ds(x, 1), :] = column_sum(s)
 
 
-def call_extra(before, extra_fields, extra_noise, moments, kept, received):
+def call_extra(before, extra_fields, extra_noise, moments, parts):
     depth = extra_fields.shape[-1] // LANES
     return pl.pallas_call(
         functools.partial(extra, 7),
@@ -565,13 +580,13 @@
             pltpu.VMEM(extra_fields.shape, f32),
             jax.ShapeDtypeStruct((8, depth, LANES), f32),
         ),
-        in_specs=[anywhere, vmem, vmem, vmem, vmem, vmem],
+        in_specs=[anywhere, vmem, vmem, vmem] + [vmem] * len(parts),
         out_specs=(vmem, vmem),
-        scratch_shapes=[pltpu.VMEM(kept.shape[1:], f32)],
+        scratch_shapes=[pltpu.VMEM(parts[0].shape, f32)],
         compiler_params=pltpu.CompilerParams(vmem_limit_bytes=SMALL),
         cost_estimate=small(32 << 20, 9 << 20),
         name="extra_fields",
-    )(before, *near_memory(extra_fields, extra_noise), moments, kept, received)
+    )(before, *near_memory(extra_fields, extra_noise), moments, *parts)
 
 
 def finish(piece_count, before, block, *refs):
@@ -610,42 +625,31 @@
     )(before, *near_memory(block), *pieces, new_base)
 
 
-def heavy(bits, helper, base, noise, grad, near, far, ready, old_base, new_base, stress, fields, rows, answer, sems):
+def heavy(helper, base, noise, grad, near, far, ready, old_base, new_base, stress, fields, rows, answer, sems):
     _, _, tiles, _, count, cells = base.shape
-    slots = helper.shape[1]
     me = lax.axis_index("gy")
     depth = cells // LANES
     flat = rows.reshape(6 * depth * tiles, LANES)
 
-    def store(h, tile):
-        return pltpu.make_async_copy(fields.at[h], new_base.at[0, 0, tile], sems.at[h])
+    def store(k, tile):
+        return pltpu.make_async_copy(fields.at[k], new_base.at[0, 0, tile], sems.at[k])
 
     def result(x):
         target = stress.at[0, 0, :, :, pl.ds(x * LANES, LANES)]
-        return pltpu.make_async_copy(rows.at[:, x], target, sems.at[slots + x])
+        return pltpu.make_async_copy(rows.at[:, x], target, sems.at[HEAVY_MOST + x])
 
     rows[...] = ready[...]
-    found = owned_slots(tiles, me, helper)
-    places = jnp.int32(0)
-    order = [jnp.int32(0)] * HEAVY_MOST
-    for h, owned, tile in found:
-        entry = h * tiles + tile
-        order = [jnp.where(owned & (places == k), entry, kept) for k, kept in enumerate(order)]
-        places = places + owned.astype(jnp.int32)
-
-    for k, entry in enumerate(order):
+    places, order = owned_order(tiles, me, helper)
+    for k, (h, tile) in enumerate(order):
 
         @pl.when(k < places)
-        def _(entry=entry):
-            h, tile = entry // tiles, entry % tiles
-            flips = me ^ h
-            place = sum(((flips >> (bits - 1 - i)) & 1) << i for i in range(bits))
-            is_far = place >= slots // 2
-            place = place & (slots // 2 - 1)
+        def _(k=k, h=h, tile=tile):
+            flip = (me ^ h) >> 1
+            is_far = ((me ^ h) & 1) == 1
             for i in range(near.shape[1]):
-                answer[i] = jnp.where(is_far, far[place, i], near[place, i])
-            totals = []
-            for x in range(depth):
+                answer[i] = jnp.where(is_far, far[flip, i], near[flip, i])
+
+            def sums_of(x):
                 lanes = pl.ds(x * LANES, LANES)
                 g = tile_grad(grad, depth, tile, x)
                 matrices = [with_diagonal(g, wide(answer[step, pl.ds(x, 1), :])) for step in range(2)]
@@ -654,35 +658,36 @@
                     return base[0, 0, tile, a, part, lanes]
 
                 def write(a, part, value):
-                    fields[h, a, part, lanes] = value
+                    fields[k, a, part, lanes] = value
 
                 def shock(step, a, part):
                     return noise[0, 0, tile, step, a, part, lanes]
 
-                totals.append(tile_sums(read, write, shock, matrices, count, add_moments, 6))
-            store(h, tile).start()
-            sums = [packed_sum(list(same)) + answer[2 + i] for i, same in enumerate(zip(*totals))]
+                return tile_sums(read, write, shock, matrices, count, add_moments, 6)
+
+            sums = packed_sums(sums_of, depth)
+            store(k, tile).start()
+            sums = [s + answer[2 + i] for i, s in enumerate(sums)]
             for i, value in enumerate(stress_rows(sums, 1.0 / ALL_FIELDS)):
                 flat[pl.ds(i * depth * tiles + tile, depth, stride=tiles), :] = value
 
     for x in range(depth):
         result(x).start()
-    for k, entry in enumerate(order):
+    for k, (_, tile) in enumerate(order):
 
         @pl.when(k < places)
-        def _(entry=entry):
-            store(entry // tiles, entry % tiles).wait()
+        def _(k=k, tile=tile):
+            store(k, tile).wait()
 
     for x in range(depth):
         result(x).wait()
 
 
-def call_heavy(bits, helper_tile, base_fields, base_noise, grad, near, far, ready, new_base):
+def call_heavy(helper_tile, base_fields, base_noise, grad, near, far, ready, new_base):
     _, _, tiles, _, count, cells = base_fields.shape
     depth = cells // LANES
-    slots = helper_tile.shape[1]
-    return pl.pallas_call(
-        functools.partial(heavy, bits),
+    return pl.pallas_call(
+        heavy,
         out_shape=(
             jax.ShapeDtypeStruct(new_base.shape, f32),
             jax.ShapeDtypeStruct((1, 1, 6, tiles, cells), f32),
@@ -691,10 +696,10 @@
         out_specs=(hbm, hbm),
         input_output_aliases={7: 0},
         scratch_shapes=[
-            pltpu.VMEM((slots, 3, count, cells), f32),
+            pltpu.VMEM((HEAVY_MOST, 3, count, cells), f32),
             pltpu.VMEM((6, depth, tiles, LANES), f32),
             pltpu.VMEM(near.shape[1:], f32),
-            pltpu.SemaphoreType.DMA((slots + depth,)),
+            pltpu.SemaphoreType.DMA((HEAVY_MOST + depth,)),
         ],
         compiler_params=pltpu.CompilerParams(vmem_limit_bytes=SMALL),
         cost_estimate=small(8 << 20, 4 << 20),
@@ -706,12 +711,12 @@
     velocity, wall_cells, tile_counts, helper_tile, base_fields, extra_fields, base_noise, extra_noise
 ):
     tiles = tile_counts.shape[2]
-    bits = lax.axis_size("gy").bit_length() - 1
+    pairs = lax.axis_size("gy") // 2
     helper_tile, x_one, x_two, y_one, y_two = call_edges(helper_tile, velocity)
     halos = two_swaps(x_one, x_two, "gx") + two_swaps(y_one, y_two, "gy")
     moments = call_heavy_moments(helper_tile, base_fields, base_noise)
     grad, keep, send = call_gradients(tiles, helper_tile, velocity, halos, wall_cells, moments)
-    gaps = 2 * bits - 2
+    gaps = 3
     new_base, block, pieces, done = None, None, [], 0
 
     def fill(before, extra_near=None):
@@ -724,26 +729,19 @@
         done += here
         return piece, extra_far
 
-    for bit in range(bits):
-        received = swapped(send, bit)
-        if bit == 1:
-            before = extra_sums = call_extra_moments(send, extra_fields, extra_noise)
-        else:
-            before, _ = fill(send)
-        if bit < bits - 1:
-            keep, send = call_merge(bit, before, keep, received)
-    extra_near, reply = call_extra(before, extra_fields, extra_noise, extra_sums, keep, received)
-    near = reply[None]
-    for bit in range(bits - 1, 0, -1):
-        received = swapped(near, bit)
-        if bit == bits - 1:
-            before, new_extra = fill(near, extra_near)
-        else:
-            before, _ = fill(near)
-        near = call_join(before, near, received)
-    far = swapped(near, 0)
+    received = swapped(send, 1)
+    before, _ = fill(send)
+    keep, *sends = call_merge(before, keep, received)
+    parts = [keep] + [swapped(send, 2 * flip) for flip, send in enumerate(sends, 1)]
+    before, _ = fill(sends[0])
+    extra_sums = call_extra_moments(before, extra_fields, extra_noise)
+    extra_near, reply = call_extra(before, extra_fields, extra_noise, extra_sums, parts)
+    replies = [reply] + [swapped(reply, 2 * flip) for flip in range(1, pairs)]
+    before, new_extra = fill(reply, extra_near)
+    near = call_join(before, replies)
+    far = swapped(near, 1)
     new_base, ready = call_finish(near, block, pieces, new_base)
-    new_base, stress = call_heavy(bits, helper_tile, base_fields, base_noise, grad, near, far, ready, new_base)
+    new_base, stress = call_heavy(helper_tile, base_fields, base_noise, grad, near, far, ready, new_base)
     return new_base, new_extra, jnp.swapaxes(stress, 2, 3)
 
 

time: 36.4 us -> 33.5 us (0.920)
  waiting for transfers between devices: 6.81 us -> 1.52 us
  local copies, waits for them, and re-layouts: 0.79 us -> 2.36 us
  starting transfers between devices: 14.1 us -> 15.4 us
  Pallas kernels: 13.8 us -> 13.2 us
    ppermute x6 -> x8, waiting for transfers between devices: 6.8 us -> 1.51 us  [swapped(): return lax.ppermute(block, 'gy', [(i, i ^ flip) for i in range(size)])]
    unnamed x12, local copies, waits for them, and re-layouts: 0.79 us -> 2.36 us
    ppermute x6 -> x8, starting transfers between devices: 5.93 us -> 7.25 us  [swapped(): return lax.ppermute(block, 'gy', [(i, i ^ flip) for i in range(size)])]
    pallas_call x4 -> x3, Pallas kernels: 4.35 us -> 3.88 us  [call_ordinary(): pl.pallas_call(functools.partial(ordinary, first, has_block, has_base, ha...]
    pallas_call x5 -> x3, Pallas kernels: 1.43 us -> 1.39 us  [the longest x1 1.36 us: call_heavy(): pl.pallas_call(heavy, out_shape=(jax.ShapeDtypeStruct(new_base.shape, f32...]
  transfers between devices with their start and end apart: 10 -> 12, of which waited for: 6 -> 3; matrix products, arithmetic and copies ran while one was open for 0% -> 0% of each run, Pallas kernels for 23% -> 24%
where the time goes in v4:
time: 33.5 us; the launch traced here: 33.3 us
  starting transfers between devices  15.4 us (46%)
  Pallas kernels  13.2 us (39%)
  local copies, waits for them, and re-layouts  2.36 us (7%)
  waiting for transfers between devices  1.52 us (5%)
  between operations  0.81 us (2%)
    ppermute x4, starting transfers between devices, two_swaps(): return (lax.ppermute(one, axis, within), lax.ppermute(two, axis, across))  8.13 us
    ppermute x8, starting transfers between devices, swapped(): return lax.ppermute(block, 'gy', [(i, i ^ flip) for i in range(size)])  7.25 us
    pallas_call x3, Pallas kernels, call_ordinary(): pl.pallas_call(functools.partial(ordinary, first, has_block, has_base, ha...  3.88 us
    unnamed x12, local copies, waits for them, and re-layouts  2.36 us
    pallas_call x1, Pallas kernels, call_extra(): pl.pallas_call(functools.partial(extra, 7), out_shape=(pltpu.VMEM(extra_f...  2.25 us
    pallas_call x1, Pallas kernels, call_heavy_moments(): pl.pallas_call(heavy_moments, out_shape=jax.ShapeDtypeStruct((slots, 16,...  1.65 us
    ppermute x8, waiting for transfers between devices, swapped(): return lax.ppermute(block, 'gy', [(i, i ^ flip) for i in range(size)])  1.51 us
    pallas_call x1, Pallas kernels, call_extra_moments(): pl.pallas_call(functools.partial(extra_moments, 7), out_shape=jax.ShapeDt...  1.4 us
  transfers between devices with their start and end apart: 12, of which 3 were waited for; matrix products, arithmetic and copies ran while one was open for 0% of the time, Pallas kernels for 24%

profile of v4, /device:TPU:0, one launch (start us, length us, event | category | flops | bytes accessed | tf_op | source)
XLA Modules:
  0.0 33.3 jit_solution(11474214358424345027)
XLA Ops:
  0.6 0.9 %edges.1 = (s32[1,8]{1,0:T(1,128)S(1)}, f32[3,8,128]{2,1,0:T(8,128)S(1)}, f32[3,8,128]{2,1,0:T(8,128)S(1)}, f32[3,8,128]{2,1,0:T(8,128)S(1)}, f32[3,8,128]{2,1,0:T(8,128)S(1)}) custom-call(s32[1,8]{1,0:T(1,128)} %helper.1, f32[3,8,8,128]{3,2,1,0:T(8,128)} %velocity.3), custom_call_target="tpu_custom_call" | custom-call | flops 1024 | bytes 131072 | tf_op jit(solution)/shard_map/edges/pallas_call | solution.py:170
  1.6 3.1 %collective-permute-start = (f32[3,8,128]{2,1,0:T(8,128)S(1)}, f32[3,8,128]{2,1,0:T(8,128)S(1)}, u32[]{:S(2)}, u32[]{:S(2)}) collective-permute-start(f32[3,8,128]{2,1,0:T(8,128)S(1)} %get-tuple-element.31), channel_id=1, source_target_pairs={{0,8},{8,0},{16,24},{24,16},{1,9},{9,1},{17,25},{25,17},{2,10},{10... | collective-permute-start | bytes 36872 | tf_op jit(solution)/shard_map/ppermute | solution.py:185
  4.7 2.5 %collective-permute-start.1 = (f32[3,8,128]{2,1,0:T(8,128)S(1)}, f32[3,8,128]{2,1,0:T(8,128)S(1)}, u32[]{:S(2)}, u32[]{:S(2)}) collective-permute-start(f32[3,8,128]{2,1,0:T(8,128)S(1)} %get-tuple-element.32), channel_id=1, source_target_pairs={{0,24},{8,16},{16,8},{24,0},{1,25},{9,17},{17,9},{25,1},{2,26},{10... | collective-permute-start | bytes 36872 | tf_op jit(solution)/shard_map/ppermute | solution.py:185
  7.1 2.6 %collective-permute-start.3 = (f32[3,8,128]{2,1,0:T(8,128)S(1)}, f32[3,8,128]{2,1,0:T(8,128)S(1)}, u32[]{:S(2)}, u32[]{:S(2)}) collective-permute-start(f32[3,8,128]{2,1,0:T(8,128)S(1)} %get-tuple-element.34), channel_id=1, source_target_pairs={{0,7},{1,2},{2,1},{3,4},{4,3},{5,6},{6,5},{7,0},{8,15},{9,10},{10,... | collective-permute-start | bytes 36872 | tf_op jit(solution)/shard_map/ppermute | solution.py:185
  9.7 1.6 %heavy_moments.1.moments = f32[8,16,8,128]{3,2,1,0:T(8,128)S(1)} custom-call(s32[1,8]{1,0:T(1,128)S(1)} %get-tuple-element.30.helper, f32[1,1,8,3,32,1024]{5,4,3,2,1,0:T(8,128)} %base.7, bf16[1,1,8,2,3,32,1024]{6,5,4,3,2,1,0:T(8,128)(2,1)} %noise.7), custom_call_target="tpu_custom_call" | custom-call | flops 8388608 | bytes 3145728 | tf_op jit(solution)/shard_map/heavy_moments/pallas_call | solution.py:238
  11.4 0.0 collective-permute-done.x_one
  11.4 0.0 collective-permute-done.2.y_one
  11.4 0.0 collective-permute-done.3.y_two
  11.4 0.7 %gradients.1 = (f32[576,128]{1,0:T(8,128)S(1)}, f32[4,12,8,128]{3,2,1,0:T(8,128)S(1)}, f32[4,12,8,128]{3,2,1,0:T(8,128)S(1)}) custom-call(s32[1,8]{1,0:T(1,128)S(1)} %get-tuple-element.30.helper, f32[3,8,8,128]{3,2,1,0:T(8,128)S(1)} %copy-done.4, f32[3,8,128]{2,1,0:T(8,128)S(1)} %collective-permute-done.x_one, ...), custom_call_target="tpu_custom_call" | custom-call | flops 4194304 | bytes 1048576 | tf_op jit(solution)/shard_map/gradients/pallas_call | solution.py:340
  12.1 0.1 collective-permute-start.4
  12.2 0.6 %copy-done.1 = bf16[1,1,8,2,3,32,1024]{6,5,4,3,2,1,0:T(8,128)(2,1)S(1)} copy-done((bf16[1,1,8,2,3,32,1024]{6,5,4,3,2,1,0:T(8,128)(2,1)S(1)}, bf16[1,1,8,2,3,32,1024]{6,5,4,3,2,1,0:T(8,128)(2,1)}, u32[]{:S(2)}) %copy-start.1) | copy-done | bytes 3145752
  12.8 0.8 %ordinary_tiles.3 = (f32[2,3,32,1024]{3,2,1,0:T(8,128)S(1)}, f32[6,2,8,128]{3,2,1,0:T(8,128)S(1)}) custom-call(f32[4,12,8,128]{3,2,1,0:T(8,128)S(1)} %get-tuple-element.36.refs_0_, f32[1,1,8,3,32,1024]{5,4,3,2,1,0:T(8,128)S(1)} %copy-done, bf16[1,1,8,2,3,32,1024]{6,5,4,3,2,1,0:T(8,128)(2,1)S(1)} %copy-done.1, f32[576,128]{1,0:T(8,128)S(1)} %get-tuple-element.35.refs_3_.grad), custom_call_target="tpu_custom_call" | custom-call | flops 8388608 | bytes 3145728 | tf_op jit(solution)/shard_map/ordinary_tiles/pallas_call | solution.py:519
  13.6 0.0 collective-permute-done.4.received
  13.7 1.5 %collective-permute-start.5 = (f32[12,8,128]{2,1,0:T(8,128)S(1)}, f32[12,8,128]{2,1,0:T(8,128)S(1)}, u32[]{:S(2)}, u32[]{:S(2)}) collective-permute-start(f32[12,8,128]{2,1,0:T(8,128)S(1)} %get-tuple-element.39.refs_0_), channel_id=1, source_target_pairs={{0,2},{1,3},{2,0},{3,1},{4,6},{5,7},{6,4},{7,5},{8,10},{9,11},{10,... | collective-permute-start | bytes 147464 | tf_op jit(solution)/shard_map/ppermute | solution.py:353
  15.2 1.4 %collective-permute-start.6 = (f32[12,8,128]{2,1,0:T(8,128)S(1)}, f32[12,8,128]{2,1,0:T(8,128)S(1)}, u32[]{:S(2)}, u32[]{:S(2)}) collective-permute-start(f32[12,8,128]{2,1,0:T(8,128)S(1)} %get-tuple-element.43), channel_id=1, source_target_pairs={{0,4},{1,5},{2,6},{3,7},{4,0},{5,1},{6,2},{7,3},{8,12},{9,13},{10,... | collective-permute-start | bytes 147464 | tf_op jit(solution)/shard_map/ppermute | solution.py:353
  16.6 0.6 %collective-permute-start.7 = (f32[12,8,128]{2,1,0:T(8,128)S(1)}, f32[12,8,128]{2,1,0:T(8,128)S(1)}, u32[]{:S(2)}, u32[]{:S(2)}) collective-permute-start(f32[12,8,128]{2,1,0:T(8,128)S(1)} %get-tuple-element.44), channel_id=1, source_target_pairs={{0,6},{1,7},{2,4},{3,5},{4,2},{5,3},{6,0},{7,1},{8,14},{9,15},{10,... | collective-permute-start | bytes 147464 | tf_op jit(solution)/shard_map/ppermute | solution.py:353
  17.2 1.1 %ordinary_tiles.4 = (f32[1,1,8,3,32,1024]{5,4,3,2,1,0:T(8,128)}, f32[3,3,32,1024]{3,2,1,0:T(8,128)S(1)}, f32[6,3,8,128]{3,2,1,0:T(8,128)S(1)}) custom-call(f32[12,8,128]{2,1,0:T(8,128)S(1)} %get-tuple-element.39.refs_0_, f32[1,1,8,3,32,1024]{5,4,3,2,1,0:T(8,128)S(1)} %copy-done, bf16[1,1,8,2,3,32,1024]{6,5,4,3,2,1,0:T(8,128)(2,1)S(1)} %copy-done.1, ...), custom_call_target="tpu_custom_call" | custom-call | flops 8388608 | bytes 3145728 | tf_op jit(solution)/shard_map/ordinary_tiles/pallas_call | solution.py:519
  18.4 0.9 %copy-done.2 = f32[1,1,3,224,1024]{4,3,2,1,0:T(8,128)S(1)} copy-done((f32[1,1,3,224,1024]{4,3,2,1,0:T(8,128)S(1)}, f32[1,1,3,224,1024]{4,3,2,1,0:T(8,128)}, u32[]{:S(2)}) %copy-start.2) | copy-done | bytes 2752536
  19.3 0.8 %copy-done.3 = bf16[1,1,2,3,224,1024]{5,4,3,2,1,0:T(8,128)(2,1)S(1)} copy-done((bf16[1,1,2,3,224,1024]{5,4,3,2,1,0:T(8,128)(2,1)S(1)}, bf16[1,1,2,3,224,1024]{5,4,3,2,1,0:T(8,128)(2,1)}, u32[]{:S(2)}) %copy-start.3) | copy-done | bytes 2752536
  20.1 1.4 %extra_moments.1.moments = f32[16,8,128]{2,1,0:T(8,128)S(1)} custom-call(f32[6,3,8,128]{3,2,1,0:T(8,128)S(1)} %get-tuple-element.41.before.refs_1_, f32[1,1,3,224,1024]{4,3,2,1,0:T(8,128)S(1)} %copy-done.2, bf16[1,1,2,3,224,1024]{5,4,3,2,1,0:T(8,128)(2,1)S(1)} %copy-done.3), custom_call_target="tpu_custom_call" | custom-call | flops 8388608 | bytes 5242880 | tf_op jit(solution)/shard_map/extra_moments/pallas_call | solution.py:276
  21.5 0.0 collective-permute-done.7.refs_3_
  21.6 2.2 %extra_fields.1 = (f32[1,1,3,224,1024]{4,3,2,1,0:T(8,128)S(1)}, f32[8,8,128]{2,1,0:T(8,128)S(1)}) custom-call(f32[6,3,8,128]{3,2,1,0:T(8,128)S(1)} %get-tuple-element.41.before.refs_1_, f32[1,1,3,224,1024]{4,3,2,1,0:T(8,128)S(1)} %copy-done.2, bf16[1,1,2,3,224,1024]{5,4,3,2,1,0:T(8,128)(2,1)S(1)} %copy-done.3, f32[16,8,128]{2,1,0:T(8,128)S(1)} %extra_moments.1.moments, ...), custom_call_target="tpu_custom_call" | custom-call | flops 33554432 | bytes 9437184 | tf_op jit(solution)/shard_map/extra_fields/pallas_call | solution.py:577
  23.8 2.3 %collective-permute-start.10 = (f32[8,8,128]{2,1,0:T(8,128)S(1)}, f32[8,8,128]{2,1,0:T(8,128)S(1)}, u32[]{:S(2)}, u32[]{:S(2)}) collective-permute-start(f32[8,8,128]{2,1,0:T(8,128)S(1)} %get-tuple-element.45.refs_0_), channel_id=1, source_target_pairs={{0,6},{1,7},{2,4},{3,5},{4,2},{5,3},{6,0},{7,1},{8,14},{9,15},{10,... | collective-permute-start | bytes 98312 | tf_op jit(solution)/shard_map/ppermute | solution.py:353
  26.2 0.4 %collective-permute-start.8 = (f32[8,8,128]{2,1,0:T(8,128)S(1)}, f32[8,8,128]{2,1,0:T(8,128)S(1)}, u32[]{:S(2)}, u32[]{:S(2)}) collective-permute-start(f32[8,8,128]{2,1,0:T(8,128)S(1)} %get-tuple-element.45.refs_0_), channel_id=1, source_target_pairs={{0,2},{1,3},{2,0},{3,1},{4,6},{5,7},{6,4},{7,5},{8,10},{9,11},{10,... | collective-permute-start | bytes 98312 | tf_op jit(solution)/shard_map/ppermute | solution.py:353
  26.6 0.8 %collective-permute-start.9 = (f32[8,8,128]{2,1,0:T(8,128)S(1)}, f32[8,8,128]{2,1,0:T(8,128)S(1)}, u32[]{:S(2)}, u32[]{:S(2)}) collective-permute-start(f32[8,8,128]{2,1,0:T(8,128)S(1)} %get-tuple-element.45.refs_0_), channel_id=1, source_target_pairs={{0,4},{1,5},{2,6},{3,7},{4,0},{5,1},{6,2},{7,3},{8,12},{9,13},{10,... | collective-permute-start | bytes 98312 | tf_op jit(solution)/shard_map/ppermute | solution.py:353
  27.4 2.0 %ordinary_tiles.5 = (f32[1,1,8,3,32,1024]{5,4,3,2,1,0:T(8,128)}, f32[1,1,3,224,1024]{4,3,2,1,0:T(8,128)}, f32[3,3,32,1024]{3,2,1,0:T(8,128)S(1)}, f32[6,3,8,128]{3,2,1,0:T(8,128)S(1)}) custom-call(f32[8,8,128]{2,1,0:T(8,128)S(1)} %get-tuple-element.45.refs_0_, f32[1,1,8,3,32,1024]{5,4,3,2,1,0:T(8,128)S(1)} %copy-done, ...), custom_call_target="tpu_custom_call", output_to_operand_aliasing={{0}: (5, {})} | custom-call | flops 8388608 | bytes 3145728 | tf_op jit(solution)/shard_map/ordinary_tiles/pallas_call | solution.py:519
  29.4 0.7 %collective-permute-done.8.refs_1_ = f32[8,8,128]{2,1,0:T(8,128)S(1)} collective-permute-done((f32[8,8,128]{2,1,0:T(8,128)S(1)}, f32[8,8,128]{2,1,0:T(8,128)S(1)}, u32[]{:S(2)}, u32[]{:S(2)}) %collective-permute-start.8) | collective-permute-done | bytes 32800 | tf_op jit(solution)/shard_map/ppermute | solution.py:353
  30.1 0.4 %collective-permute-done.9.refs_2_ = f32[8,8,128]{2,1,0:T(8,128)S(1)} collective-permute-done((f32[8,8,128]{2,1,0:T(8,128)S(1)}, f32[8,8,128]{2,1,0:T(8,128)S(1)}, u32[]{:S(2)}, u32[]{:S(2)}) %collective-permute-start.9) | collective-permute-done | bytes 32800 | tf_op jit(solution)/shard_map/ppermute | solution.py:353
  30.5 0.1 collective-permute-start.11
  30.6 1.0 %finish.1 = (f32[1,1,8,3,32,1024]{5,4,3,2,1,0:T(8,128)}, f32[6,8,8,128]{3,2,1,0:T(8,128)S(1)}) custom-call(f32[4,8,8,128]{3,2,1,0:T(8,128)S(1)} %join.1.before.near, f32[3,3,32,1024]{3,2,1,0:T(8,128)S(1)} %get-tuple-element.50.block, f32[6,2,8,128]{3,2,1,0:T(8,128)S(1)} %get-tuple-element.37.before.refs_0_, ...), custom_call_target="tpu_custom_call", output_to_operand_aliasing={{0}: (5, {})} | custom-call | flops 1024 | bytes 1048576 | tf_op jit(solution)/shard_map/finish/pallas_call | solution.py:612
  31.6 0.3 collective-permute-done.11.far
  31.9 1.4 %heavy_tiles.1 = (f32[1,1,8,3,32,1024]{5,4,3,2,1,0:T(8,128)}, f32[1,1,6,8,1024]{4,3,2,1,0:T(8,128)}) custom-call(s32[1,8]{1,0:T(1,128)S(1)} %get-tuple-element.30.helper, f32[1,1,8,3,32,1024]{5,4,3,2,1,0:T(8,128)S(1)} %copy-done, bf16[1,1,8,2,3,32,1024]{6,5,4,3,2,1,0:T(8,128)(2,1)S(1)} %copy-done.1, ...), custom_call_target="tpu_custom_call", output_to_operand_aliasing={{0}: (7, {})} | custom-call | flops 8388608 | bytes 4194304 | tf_op jit(solution)/shard_map/heavy_tiles/pallas_call | solution.py:689
  (16 shorter events, 0.1 us)
Async XLA Ops:
  1.6 9.8 %collective-permute-start = (f32[3,8,128]{2,1,0:T(8,128)S(1)}, f32[3,8,128]{2,1,0:T(8,128)S(1)}, u32[]{:S(2)}, u32[]{:S(2)}) collective-permute-start(f32[3,8,128]{2,1,0:T(8,128)S(1)} %get-tuple-element.31), channel_id=1, source_target_pairs={{0,8},{8,0},{16,24},{24,16},{1,9},{9,1},{17,25},{25,17},{2,10},{10... | collective-permute-start | bytes 36872 | tf_op jit(solution)/shard_map/ppermute | solution.py:185
  4.7 6.7 %collective-permute-start.1 = (f32[3,8,128]{2,1,0:T(8,128)S(1)}, f32[3,8,128]{2,1,0:T(8,128)S(1)}, u32[]{:S(2)}, u32[]{:S(2)}) collective-permute-start(f32[3,8,128]{2,1,0:T(8,128)S(1)} %get-tuple-element.32), channel_id=1, source_target_pairs={{0,24},{8,16},{16,8},{24,0},{1,25},{9,17},{17,9},{25,1},{2,26},{10... | collective-permute-start | bytes 36872 | tf_op jit(solution)/shard_map/ppermute | solution.py:185
  7.1 4.3 %collective-permute-start.2 = (f32[3,8,128]{2,1,0:T(8,128)S(1)}, f32[3,8,128]{2,1,0:T(8,128)S(1)}, u32[]{:S(2)}, u32[]{:S(2)}) collective-permute-start(f32[3,8,128]{2,1,0:T(8,128)S(1)} %get-tuple-element.33), channel_id=1, source_target_pairs={{0,1},{1,0},{2,3},{3,2},{4,5},{5,4},{6,7},{7,6},{8,9},{9,8},{10,11... | collective-permute-start | bytes 36872 | tf_op jit(solution)/shard_map/ppermute | solution.py:185
  7.1 4.3 %collective-permute-start.3 = (f32[3,8,128]{2,1,0:T(8,128)S(1)}, f32[3,8,128]{2,1,0:T(8,128)S(1)}, u32[]{:S(2)}, u32[]{:S(2)}) collective-permute-start(f32[3,8,128]{2,1,0:T(8,128)S(1)} %get-tuple-element.34), channel_id=1, source_target_pairs={{0,7},{1,2},{2,1},{3,4},{4,3},{5,6},{6,5},{7,0},{8,15},{9,10},{10,... | collective-permute-start | bytes 36872 | tf_op jit(solution)/shard_map/ppermute | solution.py:185
  9.7 1.7 %copy-start.4 = (f32[3,8,8,128]{3,2,1,0:T(8,128)S(1)}, f32[3,8,8,128]{3,2,1,0:T(8,128)}, u32[]{:S(2)}) copy-start(f32[3,8,8,128]{3,2,1,0:T(8,128)} %velocity.3) | copy-start | bytes 294916
  9.7 1.7 %copy-start.5 = (s32[8,8,128]{2,1,0:T(8,128)S(1)}, s32[8,8,128]{2,1,0:T(8,128)}, u32[]{:S(2)}) copy-start(s32[8,8,128]{2,1,0:T(8,128)} %wall.1) | copy-start | bytes 98308
  9.7 2.5 %copy-start = (f32[1,1,8,3,32,1024]{5,4,3,2,1,0:T(8,128)S(1)}, f32[1,1,8,3,32,1024]{5,4,3,2,1,0:T(8,128)}, u32[]{:S(2)}) copy-start(f32[1,1,8,3,32,1024]{5,4,3,2,1,0:T(8,128)} %base.7) | copy-start | bytes 9437188
  9.7 3.1 %copy-start.1 = (bf16[1,1,8,2,3,32,1024]{6,5,4,3,2,1,0:T(8,128)(2,1)S(1)}, bf16[1,1,8,2,3,32,1024]{6,5,4,3,2,1,0:T(8,128)(2,1)}, u32[]{:S(2)}) copy-start(bf16[1,1,8,2,3,32,1024]{6,5,4,3,2,1,0:T(8,128)(2,1)} %noise.7) | copy-start | bytes 9437188
  12.1 1.5 %collective-permute-start.4 = (f32[4,12,8,128]{3,2,1,0:T(8,128)S(1)}, f32[4,12,8,128]{3,2,1,0:T(8,128)S(1)}, u32[]{:S(2)}, u32[]{:S(2)}) collective-permute-start(f32[4,12,8,128]{3,2,1,0:T(8,128)S(1)} %get-tuple-element.36.refs_0_), channel_id=1, source_target_pairs={{0,1},{1,0},{2,3},{3,2},{4,5},{5,4},{6,7},{7,6},{8,9},{9,8},{10,11... | collective-permute-start | bytes 589832 | tf_op jit(solution)/shard_map/ppermute | solution.py:353
  13.7 7.9 %collective-permute-start.5 = (f32[12,8,128]{2,1,0:T(8,128)S(1)}, f32[12,8,128]{2,1,0:T(8,128)S(1)}, u32[]{:S(2)}, u32[]{:S(2)}) collective-permute-start(f32[12,8,128]{2,1,0:T(8,128)S(1)} %get-tuple-element.39.refs_0_), channel_id=1, source_target_pairs={{0,2},{1,3},{2,0},{3,1},{4,6},{5,7},{6,4},{7,5},{8,10},{9,11},{10,... | collective-permute-start | bytes 147464 | tf_op jit(solution)/shard_map/ppermute | solution.py:353
  15.2 6.4 %collective-permute-start.6 = (f32[12,8,128]{2,1,0:T(8,128)S(1)}, f32[12,8,128]{2,1,0:T(8,128)S(1)}, u32[]{:S(2)}, u32[]{:S(2)}) collective-permute-start(f32[12,8,128]{2,1,0:T(8,128)S(1)} %get-tuple-element.43), channel_id=1, source_target_pairs={{0,4},{1,5},{2,6},{3,7},{4,0},{5,1},{6,2},{7,3},{8,12},{9,13},{10,... | collective-permute-start | bytes 147464 | tf_op jit(solution)/shard_map/ppermute | solution.py:353
  16.6 5.0 %collective-permute-start.7 = (f32[12,8,128]{2,1,0:T(8,128)S(1)}, f32[12,8,128]{2,1,0:T(8,128)S(1)}, u32[]{:S(2)}, u32[]{:S(2)}) collective-permute-start(f32[12,8,128]{2,1,0:T(8,128)S(1)} %get-tuple-element.44), channel_id=1, source_target_pairs={{0,6},{1,7},{2,4},{3,5},{4,2},{5,3},{6,0},{7,1},{8,14},{9,15},{10,... | collective-permute-start | bytes 147464 | tf_op jit(solution)/shard_map/ppermute | solution.py:353
  17.2 2.1 %copy-start.2 = (f32[1,1,3,224,1024]{4,3,2,1,0:T(8,128)S(1)}, f32[1,1,3,224,1024]{4,3,2,1,0:T(8,128)}, u32[]{:S(2)}) copy-start(f32[1,1,3,224,1024]{4,3,2,1,0:T(8,128)} %base.6) | copy-start | bytes 8257540
  17.2 2.9 %copy-start.3 = (bf16[1,1,2,3,224,1024]{5,4,3,2,1,0:T(8,128)(2,1)S(1)}, bf16[1,1,2,3,224,1024]{5,4,3,2,1,0:T(8,128)(2,1)}, u32[]{:S(2)}) copy-start(bf16[1,1,2,3,224,1024]{5,4,3,2,1,0:T(8,128)(2,1)} %noise.6) | copy-start | bytes 8257540
  23.8 5.5 %collective-permute-start.10 = (f32[8,8,128]{2,1,0:T(8,128)S(1)}, f32[8,8,128]{2,1,0:T(8,128)S(1)}, u32[]{:S(2)}, u32[]{:S(2)}) collective-permute-start(f32[8,8,128]{2,1,0:T(8,128)S(1)} %get-tuple-element.45.refs_0_), channel_id=1, source_target_pairs={{0,6},{1,7},{2,4},{3,5},{4,2},{5,3},{6,0},{7,1},{8,14},{9,15},{10,... | collective-permute-start | bytes 98312 | tf_op jit(solution)/shard_map/ppermute | solution.py:353
  26.2 3.9 %collective-permute-start.8 = (f32[8,8,128]{2,1,0:T(8,128)S(1)}, f32[8,8,128]{2,1,0:T(8,128)S(1)}, u32[]{:S(2)}, u32[]{:S(2)}) collective-permute-start(f32[8,8,128]{2,1,0:T(8,128)S(1)} %get-tuple-element.45.refs_0_), channel_id=1, source_target_pairs={{0,2},{1,3},{2,0},{3,1},{4,6},{5,7},{6,4},{7,5},{8,10},{9,11},{10,... | collective-permute-start | bytes 98312 | tf_op jit(solution)/shard_map/ppermute | solution.py:353
  26.6 3.9 %collective-permute-start.9 = (f32[8,8,128]{2,1,0:T(8,128)S(1)}, f32[8,8,128]{2,1,0:T(8,128)S(1)}, u32[]{:S(2)}, u32[]{:S(2)}) collective-permute-start(f32[8,8,128]{2,1,0:T(8,128)S(1)} %get-tuple-element.45.refs_0_), channel_id=1, source_target_pairs={{0,4},{1,5},{2,6},{3,7},{4,0},{5,1},{6,2},{7,3},{8,12},{9,13},{10,... | collective-permute-start | bytes 98312 | tf_op jit(solution)/shard_map/ppermute | solution.py:353
  30.5 1.4 %collective-permute-start.11 = (f32[4,8,8,128]{3,2,1,0:T(8,128)S(1)}, f32[4,8,8,128]{3,2,1,0:T(8,128)S(1)}, u32[]{:S(2)}, u32[]{:S(2)}) collective-permute-start(f32[4,8,8,128]{3,2,1,0:T(8,128)S(1)} %join.1.before.near), channel_id=1, source_target_pairs={{0,1},{1,0},{2,3},{3,2},{4,5},{5,4},{6,7},{7,6},{8,9},{9,8},{10,11... | collective-permute-start | bytes 393224 | tf_op jit(solution)/shard_map/ppermute | solution.py:353

commit v5 on v4

--- a/solution.py
+++ b/solution.py
@@ -733,8 +733,8 @@
     before, _ = fill(send)
     keep, *sends = call_merge(before, keep, received)
     parts = [keep] + [swapped(send, 2 * flip) for flip, send in enumerate(sends, 1)]
-    before, _ = fill(sends[0])
-    extra_sums = call_extra_moments(before, extra_fields, extra_noise)
+    extra_sums = call_extra_moments(sends[0], extra_fields, extra_noise)
+    before, _ = fill(extra_sums)
     extra_near, reply = call_extra(before, extra_fields, extra_noise, extra_sums, parts)
     replies = [reply] + [swapped(reply, 2 * flip) for flip in range(1, pairs)]
     before, new_extra = fill(reply, extra_near)

time: 33.5 us -> 32.6 us (0.973)
  waiting for transfers between devices: 1.52 us -> 3.88 us
  Pallas kernels: 13.2 us -> 11.4 us
  local copies, waits for them, and re-layouts: 2.36 us -> 0.7 us
    unnamed x12, local copies, waits for them, and re-layouts: 2.36 us -> 0.7 us
    pallas_call x1, Pallas kernels: 1.65 us -> 0.26 us  [call_heavy_moments(): pl.pallas_call(heavy_moments, out_shape=jax.ShapeDtypeStruct((slots, 16,...]
    ppermute x8, waiting for transfers between devices: 1.51 us -> 2.71 us  [swapped(): return lax.ppermute(block, 'gy', [(i, i ^ flip) for i in range(size)])]
    ppermute x4, waiting for transfers between devices: 0.01 us -> 1.17 us  [two_swaps(): return (lax.ppermute(one, axis, within), lax.ppermute(two, axis, across))]
    pallas_call x1, Pallas kernels: 1.36 us -> 0.96 us  [call_heavy(): pl.pallas_call(heavy, out_shape=(jax.ShapeDtypeStruct(new_base.shape, f32...]
  transfers between devices with their start and end apart: 12 -> 12, of which waited for: 3 -> 5; matrix products, arithmetic and copies ran while one was open for 0% -> 0% of each run, Pallas kernels for 24% -> 20%
where the time goes in v5:
time: 32.6 us; the launch traced here: 32.2 us
  starting transfers between devices  15.4 us (47%)
  Pallas kernels  11.4 us (35%)
  waiting for transfers between devices  3.88 us (12%)
  between operations  0.8 us (2%)
  local copies, waits for them, and re-layouts  0.7 us (2%)
    ppermute x4, starting transfers between devices, two_swaps(): return (lax.ppermute(one, axis, within), lax.ppermute(two, axis, across))  8.13 us
    ppermute x8, starting transfers between devices, swapped(): return lax.ppermute(block, 'gy', [(i, i ^ flip) for i in range(size)])  7.25 us
    pallas_call x3, Pallas kernels, call_ordinary(): pl.pallas_call(functools.partial(ordinary, first, has_block, has_base, ha...  3.86 us
    ppermute x8, waiting for transfers between devices, swapped(): return lax.ppermute(block, 'gy', [(i, i ^ flip) for i in range(size)])  2.71 us
    pallas_call x1, Pallas kernels, call_extra(): pl.pallas_call(functools.partial(extra, 7), out_shape=(pltpu.VMEM(extra_f...  2.25 us
    pallas_call x1, Pallas kernels, call_extra_moments(): pl.pallas_call(functools.partial(extra_moments, 7), out_shape=jax.ShapeDt...  1.41 us
    ppermute x4, waiting for transfers between devices, two_swaps(): return (lax.ppermute(one, axis, within), lax.ppermute(two, axis, across))  1.17 us
    pallas_call x1, Pallas kernels, call_finish(): pl.pallas_call(functools.partial(finish, len(pieces)), out_shape=(jax.Sha...  1.04 us
  transfers between devices with their start and end apart: 12, of which 5 were waited for; matrix products, arithmetic and copies ran while one was open for 0% of the time, Pallas kernels for 20%

profile of v5, /device:TPU:0, one launch (start us, length us, event | category | flops | bytes accessed | tf_op | source)
XLA Modules:
  0.0 32.2 jit_solution(6657862251036481043)
XLA Ops:
  0.6 0.9 %edges.1 = (s32[1,8]{1,0:T(1,128)S(1)}, f32[3,8,128]{2,1,0:T(8,128)S(1)}, f32[3,8,128]{2,1,0:T(8,128)S(1)}, f32[3,8,128]{2,1,0:T(8,128)S(1)}, f32[3,8,128]{2,1,0:T(8,128)S(1)}) custom-call(s32[1,8]{1,0:T(1,128)} %helper.1, f32[3,8,8,128]{3,2,1,0:T(8,128)} %velocity.3), custom_call_target="tpu_custom_call" | custom-call | flops 1024 | bytes 131072 | tf_op jit(solution)/shard_map/edges/pallas_call | solution.py:170
  1.6 3.1 %collective-permute-start = (f32[3,8,128]{2,1,0:T(8,128)S(1)}, f32[3,8,128]{2,1,0:T(8,128)S(1)}, u32[]{:S(2)}, u32[]{:S(2)}) collective-permute-start(f32[3,8,128]{2,1,0:T(8,128)S(1)} %get-tuple-element.31), channel_id=1, source_target_pairs={{0,8},{8,0},{16,24},{24,16},{1,9},{9,1},{17,25},{25,17},{2,10},{10... | collective-permute-start | bytes 36872 | tf_op jit(solution)/shard_map/ppermute | solution.py:185
  4.7 2.5 %collective-permute-start.1 = (f32[3,8,128]{2,1,0:T(8,128)S(1)}, f32[3,8,128]{2,1,0:T(8,128)S(1)}, u32[]{:S(2)}, u32[]{:S(2)}) collective-permute-start(f32[3,8,128]{2,1,0:T(8,128)S(1)} %get-tuple-element.32), channel_id=1, source_target_pairs={{0,24},{8,16},{16,8},{24,0},{1,25},{9,17},{17,9},{25,1},{2,26},{10... | collective-permute-start | bytes 36872 | tf_op jit(solution)/shard_map/ppermute | solution.py:185
  7.1 0.0 collective-permute-start.2
  7.1 2.6 %collective-permute-start.3 = (f32[3,8,128]{2,1,0:T(8,128)S(1)}, f32[3,8,128]{2,1,0:T(8,128)S(1)}, u32[]{:S(2)}, u32[]{:S(2)}) collective-permute-start(f32[3,8,128]{2,1,0:T(8,128)S(1)} %get-tuple-element.34), channel_id=1, source_target_pairs={{0,7},{1,2},{2,1},{3,4},{4,3},{5,6},{6,5},{7,0},{8,15},{9,10},{10,... | collective-permute-start | bytes 36872 | tf_op jit(solution)/shard_map/ppermute | solution.py:185
  9.7 0.3 heavy_moments.1.moments
  10.0 0.0 collective-permute-done.x_one
  10.0 0.2 collective-permute-done.1.x_two
  10.2 0.0 collective-permute-done.2.y_one
  10.2 1.0 %collective-permute-done.3.y_two = f32[3,8,128]{2,1,0:T(8,128)S(1)} collective-permute-done((f32[3,8,128]{2,1,0:T(8,128)S(1)}, f32[3,8,128]{2,1,0:T(8,128)S(1)}, u32[]{:S(2)}, u32[]{:S(2)}) %collective-permute-start.3) | collective-permute-done | bytes 12320 | tf_op jit(solution)/shard_map/ppermute | solution.py:185
  11.2 0.7 %gradients.1 = (f32[576,128]{1,0:T(8,128)S(1)}, f32[4,12,8,128]{3,2,1,0:T(8,128)S(1)}, f32[4,12,8,128]{3,2,1,0:T(8,128)S(1)}) custom-call(s32[1,8]{1,0:T(1,128)S(1)} %get-tuple-element.30.helper, f32[3,8,8,128]{3,2,1,0:T(8,128)S(1)} %copy-done.4, f32[3,8,128]{2,1,0:T(8,128)S(1)} %collective-permute-done.x_one, ...), custom_call_target="tpu_custom_call" | custom-call | flops 4194304 | bytes 1048576 | tf_op jit(solution)/shard_map/gradients/pallas_call | solution.py:340
  11.8 0.1 collective-permute-start.4
  11.9 0.7 %copy-done.1 = bf16[1,1,8,2,3,32,1024]{6,5,4,3,2,1,0:T(8,128)(2,1)S(1)} copy-done((bf16[1,1,8,2,3,32,1024]{6,5,4,3,2,1,0:T(8,128)(2,1)S(1)}, bf16[1,1,8,2,3,32,1024]{6,5,4,3,2,1,0:T(8,128)(2,1)}, u32[]{:S(2)}) %copy-start.1) | copy-done | bytes 3145752
  12.6 0.8 %ordinary_tiles.3 = (f32[2,3,32,1024]{3,2,1,0:T(8,128)S(1)}, f32[6,2,8,128]{3,2,1,0:T(8,128)S(1)}) custom-call(f32[4,12,8,128]{3,2,1,0:T(8,128)S(1)} %get-tuple-element.36.refs_0_, f32[1,1,8,3,32,1024]{5,4,3,2,1,0:T(8,128)S(1)} %copy-done, bf16[1,1,8,2,3,32,1024]{6,5,4,3,2,1,0:T(8,128)(2,1)S(1)} %copy-done.1, f32[576,128]{1,0:T(8,128)S(1)} %get-tuple-element.35.refs_3_.grad), custom_call_target="tpu_custom_call" | custom-call | flops 8388608 | bytes 3145728 | tf_op jit(solution)/shard_map/ordinary_tiles/pallas_call | solution.py:519
  13.4 1.6 %collective-permute-start.5 = (f32[12,8,128]{2,1,0:T(8,128)S(1)}, f32[12,8,128]{2,1,0:T(8,128)S(1)}, u32[]{:S(2)}, u32[]{:S(2)}) collective-permute-start(f32[12,8,128]{2,1,0:T(8,128)S(1)} %get-tuple-element.39.before), channel_id=1, source_target_pairs={{0,2},{1,3},{2,0},{3,1},{4,6},{5,7},{6,4},{7,5},{8,10},{9,11},{10,... | collective-permute-start | bytes 147464 | tf_op jit(solution)/shard_map/ppermute | solution.py:353
  15.1 1.5 %collective-permute-start.6 = (f32[12,8,128]{2,1,0:T(8,128)S(1)}, f32[12,8,128]{2,1,0:T(8,128)S(1)}, u32[]{:S(2)}, u32[]{:S(2)}) collective-permute-start(f32[12,8,128]{2,1,0:T(8,128)S(1)} %get-tuple-element.43), channel_id=1, source_target_pairs={{0,4},{1,5},{2,6},{3,7},{4,0},{5,1},{6,2},{7,3},{8,12},{9,13},{10,... | collective-permute-start | bytes 147464 | tf_op jit(solution)/shard_map/ppermute | solution.py:353
  16.6 0.4 %collective-permute-start.7 = (f32[12,8,128]{2,1,0:T(8,128)S(1)}, f32[12,8,128]{2,1,0:T(8,128)S(1)}, u32[]{:S(2)}, u32[]{:S(2)}) collective-permute-start(f32[12,8,128]{2,1,0:T(8,128)S(1)} %get-tuple-element.44), channel_id=1, source_target_pairs={{0,6},{1,7},{2,4},{3,5},{4,2},{5,3},{6,0},{7,1},{8,14},{9,15},{10,... | collective-permute-start | bytes 147464 | tf_op jit(solution)/shard_map/ppermute | solution.py:353
  17.0 1.4 %extra_moments.1.refs_0_.moments = f32[16,8,128]{2,1,0:T(8,128)S(1)} custom-call(f32[12,8,128]{2,1,0:T(8,128)S(1)} %get-tuple-element.39.before, f32[1,1,3,224,1024]{4,3,2,1,0:T(8,128)S(1)} %copy-done.2, bf16[1,1,2,3,224,1024]{5,4,3,2,1,0:T(8,128)(2,1)S(1)} %copy-done.3), custom_call_target="tpu_custom_call" | custom-call | flops 8388608 | bytes 5242880 | tf_op jit(solution)/shard_map/extra_moments/pallas_call | solution.py:276
  18.4 1.1 %ordinary_tiles.4 = (f32[1,1,8,3,32,1024]{5,4,3,2,1,0:T(8,128)}, f32[3,3,32,1024]{3,2,1,0:T(8,128)S(1)}, f32[6,3,8,128]{3,2,1,0:T(8,128)S(1)}) custom-call(f32[16,8,128]{2,1,0:T(8,128)S(1)} %extra_moments.1.refs_0_.moments, f32[1,1,8,3,32,1024]{5,4,3,2,1,0:T(8,128)S(1)} %copy-done, bf16[1,1,8,2,3,32,1024]{6,5,4,3,2,1,0:T(8,128)(2,1)S(1)} %copy-done.1, ...), custom_call_target="tpu_custom_call" | custom-call | flops 8388608 | bytes 3145728 | tf_op jit(solution)/shard_map/ordinary_tiles/pallas_call | solution.py:519
  19.6 0.0 collective-permute-done.6.refs_2_
  19.6 2.0 %collective-permute-done.7.refs_3_ = f32[12,8,128]{2,1,0:T(8,128)S(1)} collective-permute-done((f32[12,8,128]{2,1,0:T(8,128)S(1)}, f32[12,8,128]{2,1,0:T(8,128)S(1)}, u32[]{:S(2)}, u32[]{:S(2)}) %collective-permute-start.7) | collective-permute-done | bytes 49184 | tf_op jit(solution)/shard_map/ppermute | solution.py:353
  21.6 2.2 %extra_fields.1 = (f32[1,1,3,224,1024]{4,3,2,1,0:T(8,128)S(1)}, f32[8,8,128]{2,1,0:T(8,128)S(1)}) custom-call(f32[6,3,8,128]{3,2,1,0:T(8,128)S(1)} %get-tuple-element.41.before.refs_1_, f32[1,1,3,224,1024]{4,3,2,1,0:T(8,128)S(1)} %copy-done.2, bf16[1,1,2,3,224,1024]{5,4,3,2,1,0:T(8,128)(2,1)S(1)} %copy-done.3, ...), custom_call_target="tpu_custom_call" | custom-call | flops 33554432 | bytes 9437184 | tf_op jit(solution)/shard_map/extra_fields/pallas_call | solution.py:577
  23.9 0.6 %collective-permute-start.10 = (f32[8,8,128]{2,1,0:T(8,128)S(1)}, f32[8,8,128]{2,1,0:T(8,128)S(1)}, u32[]{:S(2)}, u32[]{:S(2)}) collective-permute-start(f32[8,8,128]{2,1,0:T(8,128)S(1)} %get-tuple-element.45.refs_0_), channel_id=1, source_target_pairs={{0,6},{1,7},{2,4},{3,5},{4,2},{5,3},{6,0},{7,1},{8,14},{9,15},{10,... | collective-permute-start | bytes 98312 | tf_op jit(solution)/shard_map/ppermute | solution.py:353
  24.5 1.4 %collective-permute-start.8 = (f32[8,8,128]{2,1,0:T(8,128)S(1)}, f32[8,8,128]{2,1,0:T(8,128)S(1)}, u32[]{:S(2)}, u32[]{:S(2)}) collective-permute-start(f32[8,8,128]{2,1,0:T(8,128)S(1)} %get-tuple-element.45.refs_0_), channel_id=1, source_target_pairs={{0,2},{1,3},{2,0},{3,1},{4,6},{5,7},{6,4},{7,5},{8,10},{9,11},{10,... | collective-permute-start | bytes 98312 | tf_op jit(solution)/shard_map/ppermute | solution.py:353
  25.9 1.5 %collective-permute-start.9 = (f32[8,8,128]{2,1,0:T(8,128)S(1)}, f32[8,8,128]{2,1,0:T(8,128)S(1)}, u32[]{:S(2)}, u32[]{:S(2)}) collective-permute-start(f32[8,8,128]{2,1,0:T(8,128)S(1)} %get-tuple-element.45.refs_0_), channel_id=1, source_target_pairs={{0,4},{1,5},{2,6},{3,7},{4,0},{5,1},{6,2},{7,3},{8,12},{9,13},{10,... | collective-permute-start | bytes 98312 | tf_op jit(solution)/shard_map/ppermute | solution.py:353
  27.4 2.0 %ordinary_tiles.5 = (f32[1,1,8,3,32,1024]{5,4,3,2,1,0:T(8,128)}, f32[1,1,3,224,1024]{4,3,2,1,0:T(8,128)}, f32[3,3,32,1024]{3,2,1,0:T(8,128)S(1)}, f32[6,3,8,128]{3,2,1,0:T(8,128)S(1)}) custom-call(f32[8,8,128]{2,1,0:T(8,128)S(1)} %get-tuple-element.45.refs_0_, f32[1,1,8,3,32,1024]{5,4,3,2,1,0:T(8,128)S(1)} %copy-done, ...), custom_call_target="tpu_custom_call", output_to_operand_aliasing={{0}: (5, {})} | custom-call | flops 8388608 | bytes 3145728 | tf_op jit(solution)/shard_map/ordinary_tiles/pallas_call | solution.py:519
  29.4 0.0 collective-permute-done.8.refs_1_
  29.4 0.4 %collective-permute-done.9.refs_2_ = f32[8,8,128]{2,1,0:T(8,128)S(1)} collective-permute-done((f32[8,8,128]{2,1,0:T(8,128)S(1)}, f32[8,8,128]{2,1,0:T(8,128)S(1)}, u32[]{:S(2)}, u32[]{:S(2)}) %collective-permute-start.9) | collective-permute-done | bytes 32800 | tf_op jit(solution)/shard_map/ppermute | solution.py:353
  29.8 0.1 collective-permute-start.11
  29.9 1.0 %finish.1 = (f32[1,1,8,3,32,1024]{5,4,3,2,1,0:T(8,128)}, f32[6,8,8,128]{3,2,1,0:T(8,128)S(1)}) custom-call(f32[4,8,8,128]{3,2,1,0:T(8,128)S(1)} %join.1.before.near, f32[3,3,32,1024]{3,2,1,0:T(8,128)S(1)} %get-tuple-element.50.block, f32[6,2,8,128]{3,2,1,0:T(8,128)S(1)} %get-tuple-element.37.before.refs_0_, ...), custom_call_target="tpu_custom_call", output_to_operand_aliasing={{0}: (5, {})} | custom-call | flops 1024 | bytes 1048576 | tf_op jit(solution)/shard_map/finish/pallas_call | solution.py:612
  30.9 0.3 collective-permute-done.11.far
  31.2 1.0 %heavy_tiles.1 = (f32[1,1,8,3,32,1024]{5,4,3,2,1,0:T(8,128)}, f32[1,1,6,8,1024]{4,3,2,1,0:T(8,128)}) custom-call(s32[1,8]{1,0:T(1,128)S(1)} %get-tuple-element.30.helper, f32[1,1,8,3,32,1024]{5,4,3,2,1,0:T(8,128)S(1)} %copy-done, bf16[1,1,8,2,3,32,1024]{6,5,4,3,2,1,0:T(8,128)(2,1)S(1)} %copy-done.1, ...), custom_call_target="tpu_custom_call", output_to_operand_aliasing={{0}: (7, {})} | custom-call | flops 8388608 | bytes 4194304 | tf_op jit(solution)/shard_map/heavy_tiles/pallas_call | solution.py:689
  (16 shorter events, 0.1 us)
Async XLA Ops:
  1.6 8.4 %collective-permute-start = (f32[3,8,128]{2,1,0:T(8,128)S(1)}, f32[3,8,128]{2,1,0:T(8,128)S(1)}, u32[]{:S(2)}, u32[]{:S(2)}) collective-permute-start(f32[3,8,128]{2,1,0:T(8,128)S(1)} %get-tuple-element.31), channel_id=1, source_target_pairs={{0,8},{8,0},{16,24},{24,16},{1,9},{9,1},{17,25},{25,17},{2,10},{10... | collective-permute-start | bytes 36872 | tf_op jit(solution)/shard_map/ppermute | solution.py:185
  4.7 5.5 %collective-permute-start.1 = (f32[3,8,128]{2,1,0:T(8,128)S(1)}, f32[3,8,128]{2,1,0:T(8,128)S(1)}, u32[]{:S(2)}, u32[]{:S(2)}) collective-permute-start(f32[3,8,128]{2,1,0:T(8,128)S(1)} %get-tuple-element.32), channel_id=1, source_target_pairs={{0,24},{8,16},{16,8},{24,0},{1,25},{9,17},{17,9},{25,1},{2,26},{10... | collective-permute-start | bytes 36872 | tf_op jit(solution)/shard_map/ppermute | solution.py:185
  7.1 3.0 %collective-permute-start.2 = (f32[3,8,128]{2,1,0:T(8,128)S(1)}, f32[3,8,128]{2,1,0:T(8,128)S(1)}, u32[]{:S(2)}, u32[]{:S(2)}) collective-permute-start(f32[3,8,128]{2,1,0:T(8,128)S(1)} %get-tuple-element.33), channel_id=1, source_target_pairs={{0,1},{1,0},{2,3},{3,2},{4,5},{5,4},{6,7},{7,6},{8,9},{9,8},{10,11... | collective-permute-start | bytes 36872 | tf_op jit(solution)/shard_map/ppermute | solution.py:185
  7.1 4.0 %collective-permute-start.3 = (f32[3,8,128]{2,1,0:T(8,128)S(1)}, f32[3,8,128]{2,1,0:T(8,128)S(1)}, u32[]{:S(2)}, u32[]{:S(2)}) collective-permute-start(f32[3,8,128]{2,1,0:T(8,128)S(1)} %get-tuple-element.34), channel_id=1, source_target_pairs={{0,7},{1,2},{2,1},{3,4},{4,3},{5,6},{6,5},{7,0},{8,15},{9,10},{10,... | collective-permute-start | bytes 36872 | tf_op jit(solution)/shard_map/ppermute | solution.py:185
  9.7 1.5 %copy-start.4 = (f32[3,8,8,128]{3,2,1,0:T(8,128)S(1)}, f32[3,8,8,128]{3,2,1,0:T(8,128)}, u32[]{:S(2)}) copy-start(f32[3,8,8,128]{3,2,1,0:T(8,128)} %velocity.3) | copy-start | bytes 294916
  9.7 1.5 %copy-start.5 = (s32[8,8,128]{2,1,0:T(8,128)S(1)}, s32[8,8,128]{2,1,0:T(8,128)}, u32[]{:S(2)}) copy-start(s32[8,8,128]{2,1,0:T(8,128)} %wall.1) | copy-start | bytes 98308
  9.7 2.2 %copy-start = (f32[1,1,8,3,32,1024]{5,4,3,2,1,0:T(8,128)S(1)}, f32[1,1,8,3,32,1024]{5,4,3,2,1,0:T(8,128)}, u32[]{:S(2)}) copy-start(f32[1,1,8,3,32,1024]{5,4,3,2,1,0:T(8,128)} %base.7) | copy-start | bytes 9437188
  9.7 2.9 %copy-start.1 = (bf16[1,1,8,2,3,32,1024]{6,5,4,3,2,1,0:T(8,128)(2,1)S(1)}, bf16[1,1,8,2,3,32,1024]{6,5,4,3,2,1,0:T(8,128)(2,1)}, u32[]{:S(2)}) copy-start(bf16[1,1,8,2,3,32,1024]{6,5,4,3,2,1,0:T(8,128)(2,1)} %noise.7) | copy-start | bytes 9437188
  11.8 1.5 %collective-permute-start.4 = (f32[4,12,8,128]{3,2,1,0:T(8,128)S(1)}, f32[4,12,8,128]{3,2,1,0:T(8,128)S(1)}, u32[]{:S(2)}, u32[]{:S(2)}) collective-permute-start(f32[4,12,8,128]{3,2,1,0:T(8,128)S(1)} %get-tuple-element.36.refs_0_), channel_id=1, source_target_pairs={{0,1},{1,0},{2,3},{3,2},{4,5},{5,4},{6,7},{7,6},{8,9},{9,8},{10,11... | collective-permute-start | bytes 589832 | tf_op jit(solution)/shard_map/ppermute | solution.py:353
  12.6 4.4 %copy-start.2 = (f32[1,1,3,224,1024]{4,3,2,1,0:T(8,128)S(1)}, f32[1,1,3,224,1024]{4,3,2,1,0:T(8,128)}, u32[]{:S(2)}) copy-start(f32[1,1,3,224,1024]{4,3,2,1,0:T(8,128)} %base.6) | copy-start | bytes 8257540
  12.6 4.4 %copy-start.3 = (bf16[1,1,2,3,224,1024]{5,4,3,2,1,0:T(8,128)(2,1)S(1)}, bf16[1,1,2,3,224,1024]{5,4,3,2,1,0:T(8,128)(2,1)}, u32[]{:S(2)}) copy-start(bf16[1,1,2,3,224,1024]{5,4,3,2,1,0:T(8,128)(2,1)} %noise.6) | copy-start | bytes 8257540
  13.4 6.1 %collective-permute-start.5 = (f32[12,8,128]{2,1,0:T(8,128)S(1)}, f32[12,8,128]{2,1,0:T(8,128)S(1)}, u32[]{:S(2)}, u32[]{:S(2)}) collective-permute-start(f32[12,8,128]{2,1,0:T(8,128)S(1)} %get-tuple-element.39.before), channel_id=1, source_target_pairs={{0,2},{1,3},{2,0},{3,1},{4,6},{5,7},{6,4},{7,5},{8,10},{9,11},{10,... | collective-permute-start | bytes 147464 | tf_op jit(solution)/shard_map/ppermute | solution.py:353
  15.1 4.5 %collective-permute-start.6 = (f32[12,8,128]{2,1,0:T(8,128)S(1)}, f32[12,8,128]{2,1,0:T(8,128)S(1)}, u32[]{:S(2)}, u32[]{:S(2)}) collective-permute-start(f32[12,8,128]{2,1,0:T(8,128)S(1)} %get-tuple-element.43), channel_id=1, source_target_pairs={{0,4},{1,5},{2,6},{3,7},{4,0},{5,1},{6,2},{7,3},{8,12},{9,13},{10,... | collective-permute-start | bytes 147464 | tf_op jit(solution)/shard_map/ppermute | solution.py:353
  16.6 5.0 %collective-permute-start.7 = (f32[12,8,128]{2,1,0:T(8,128)S(1)}, f32[12,8,128]{2,1,0:T(8,128)S(1)}, u32[]{:S(2)}, u32[]{:S(2)}) collective-permute-start(f32[12,8,128]{2,1,0:T(8,128)S(1)} %get-tuple-element.44), channel_id=1, source_target_pairs={{0,6},{1,7},{2,4},{3,5},{4,2},{5,3},{6,0},{7,1},{8,14},{9,15},{10,... | collective-permute-start | bytes 147464 | tf_op jit(solution)/shard_map/ppermute | solution.py:353
  23.9 5.5 %collective-permute-start.10 = (f32[8,8,128]{2,1,0:T(8,128)S(1)}, f32[8,8,128]{2,1,0:T(8,128)S(1)}, u32[]{:S(2)}, u32[]{:S(2)}) collective-permute-start(f32[8,8,128]{2,1,0:T(8,128)S(1)} %get-tuple-element.45.refs_0_), channel_id=1, source_target_pairs={{0,6},{1,7},{2,4},{3,5},{4,2},{5,3},{6,0},{7,1},{8,14},{9,15},{10,... | collective-permute-start | bytes 98312 | tf_op jit(solution)/shard_map/ppermute | solution.py:353
  24.5 4.9 %collective-permute-start.8 = (f32[8,8,128]{2,1,0:T(8,128)S(1)}, f32[8,8,128]{2,1,0:T(8,128)S(1)}, u32[]{:S(2)}, u32[]{:S(2)}) collective-permute-start(f32[8,8,128]{2,1,0:T(8,128)S(1)} %get-tuple-element.45.refs_0_), channel_id=1, source_target_pairs={{0,2},{1,3},{2,0},{3,1},{4,6},{5,7},{6,4},{7,5},{8,10},{9,11},{10,... | collective-permute-start | bytes 98312 | tf_op jit(solution)/shard_map/ppermute | solution.py:353
  25.9 3.9 %collective-permute-start.9 = (f32[8,8,128]{2,1,0:T(8,128)S(1)}, f32[8,8,128]{2,1,0:T(8,128)S(1)}, u32[]{:S(2)}, u32[]{:S(2)}) collective-permute-start(f32[8,8,128]{2,1,0:T(8,128)S(1)} %get-tuple-element.45.refs_0_), channel_id=1, source_target_pairs={{0,4},{1,5},{2,6},{3,7},{4,0},{5,1},{6,2},{7,3},{8,12},{9,13},{10,... | collective-permute-start | bytes 98312 | tf_op jit(solution)/shard_map/ppermute | solution.py:353
  29.8 1.4 %collective-permute-start.11 = (f32[4,8,8,128]{3,2,1,0:T(8,128)S(1)}, f32[4,8,8,128]{3,2,1,0:T(8,128)S(1)}, u32[]{:S(2)}, u32[]{:S(2)}) collective-permute-start(f32[4,8,8,128]{3,2,1,0:T(8,128)S(1)} %join.1.before.near), channel_id=1, source_target_pairs={{0,1},{1,0},{2,3},{3,2},{4,5},{5,4},{6,7},{7,6},{8,9},{9,8},{10,11... | collective-permute-start | bytes 393224 | tf_op jit(solution)/shard_map/ppermute | solution.py:353

commit v6 on v5

--- a/solution.py
+++ b/solution.py
@@ -348,45 +348,60 @@
     )(helper_tile, velocity, *halos, wall_cells, moments)
 
 
-def swapped(block, flip):
+def swapped_within(block):
     size = lax.axis_size("gy")
-    return lax.ppermute(block, "gy", [(i, i ^ flip) for i in range(size)])
-
-
-def merge(before, kept, received, keep, *sends):
-    pair = lax.axis_index("gy") >> 1
-    for flip, out in enumerate((keep,) + sends):
-        out[...] = kept[pair ^ flip] + received[pair ^ flip]
-
-
-def call_merge(before, kept, received):
-    one = jax.ShapeDtypeStruct(kept.shape[1:], f32)
-    return pl.pallas_call(
-        merge,
-        out_shape=(one,) * kept.shape[0],
+    return lax.ppermute(block, "gy", [(i, i ^ 1) for i in range(size)])
+
+
+def swapped_across(block, stage):
+    size = lax.axis_size("gy")
+    bits = (size // 2).bit_length() - 1
+    return lax.ppermute(block, "gy", [(i, i ^ (2 << (bits - 1 - stage if i & 1 else stage))) for i in range(size)])
+
+
+def by_stage(flip, pairs, odd):
+    bits = pairs.bit_length() - 1
+    turned_over = sum(((flip >> (bits - 1 - i)) & 1) << i for i in range(bits))
+    return jnp.where(odd, turned_over, flip)
+
+
+def halve(first, before, kept, received, keep, send):
+    me = lax.axis_index("gy")
+    for k in range(kept.shape[0]):
+        slot = (me >> 1) ^ by_stage(k, kept.shape[0], (me & 1) == 1) if first else k
+        out = send if k & 1 else keep
+        out[k >> 1] = kept[slot] + received[slot]
+
+
+def call_halve(first, before, kept, received):
+    half = jax.ShapeDtypeStruct((kept.shape[0] // 2,) + kept.shape[1:], f32)
+    return pl.pallas_call(
+        functools.partial(halve, first),
+        out_shape=(half, half),
         in_specs=[anywhere, vmem, vmem],
-        out_specs=(vmem,) * kept.shape[0],
+        out_specs=(vmem, vmem),
         compiler_params=pltpu.CompilerParams(vmem_limit_bytes=4 << 20),
         cost_estimate=small(1 << 10, 1 << 18),
-        name="merge",
+        name="halve",
     )(before, kept, received)
 
 
-def join(before, *refs):
-    for i, ref in enumerate(refs[:-1]):
-        refs[-1][i] = ref[...]
-
-
-def call_join(before, blocks):
+def join(before, first, second, out):
+    count = first.shape[0]
+    out[:count] = first[...]
+    out[count:] = second[...]
+
+
+def call_join(before, first, second):
     return pl.pallas_call(
         join,
-        out_shape=jax.ShapeDtypeStruct((len(blocks),) + blocks[0].shape, f32),
-        in_specs=[anywhere] + [vmem] * len(blocks),
+        out_shape=jax.ShapeDtypeStruct((2 * first.shape[0],) + first.shape[1:], f32),
+        in_specs=[anywhere, vmem, vmem],
         out_specs=vmem,
         compiler_params=pltpu.CompilerParams(vmem_limit_bytes=4 << 20),
         cost_estimate=small(1 << 10, 1 << 18),
         name="join",
-    )(before, *blocks)
+    )(before, first, second)
 
 
 def stress_rows(sums, inverse):
@@ -418,16 +433,18 @@
     return [sums[0] + (q[0] * q[0] + q[1] * q[1] + q[2] * q[2])]
 
 
-def ordinary(first, has_block, has_base, has_extra, *refs):
+def ordinary(first, has_block, has_base, leaving, has_old, *refs):
     refs = list(refs)
     before, base, noise, grad = refs[:4]
     del refs[:4]
     block = refs.pop(0) if has_block else None
     if has_base:
         refs.pop(0)
-    extra_near = refs.pop(0) if has_extra else None
+    extra_near = refs.pop(0) if leaving else None
+    if has_old:
+        refs.pop(0)
     new_base = refs.pop(0) if has_block else None
-    new_extra = refs.pop(0) if has_extra else None
+    new_extra = refs.pop(0) if leaving else None
     fields, stress, halfway, relaxes, sems = refs
     here, _, count, cells = fields.shape
     depth = cells // LANES
@@ -438,11 +455,10 @@
         copies += [
             pltpu.make_async_copy(block.at[i], new_base.at[0, 0, first - last + i], sems.at[i]) for i in range(last)
         ]
-    if has_extra:
-        copies += [
-            pltpu.make_async_copy(extra_near.at[0, 0, a], new_extra.at[0, 0, a], sems.at[len(copies) + a])
-            for a in range(3)
-        ]
+    copies += [
+        pltpu.make_async_copy(extra_near.at[0, 0, a], new_extra.at[0, 0, a], sems.at[len(copies) + i])
+        for i, a in enumerate(leaving)
+    ]
     for copy in copies:
         copy.start()
     for place in range(here):
@@ -487,10 +503,10 @@
         copy.wait()
 
 
-def call_ordinary(first, here, before, base_fields, base_noise, grad, block, new_base, new_extra):
+def call_ordinary(first, here, before, base_fields, base_noise, grad, block, new_base, extra_near, leaving, new_extra):
     count, cells = base_fields.shape[-2:]
     depth = cells // LANES
-    has_block, has_base, has_extra = block is not None, new_base is not None, new_extra is not None
+    has_block, has_base, has_old = block is not None, new_base is not None, bool(leaving) and new_extra is not None
     operands = [before, *near_memory(base_fields, base_noise), grad]
     specs = [anywhere, vmem, vmem, vmem]
     shapes, out_specs, aliases = [], [], {}
@@ -505,19 +521,23 @@
         aliases[len(operands)] = 0
         operands.append(new_base)
         specs.append(hbm)
-    if has_extra:
-        operands += near_memory(new_extra)
+    if leaving:
+        operands += near_memory(extra_near)
         specs.append(vmem)
-        shapes.append(jax.ShapeDtypeStruct(new_extra.shape, f32))
+        if has_old:
+            aliases[len(operands)] = len(shapes)
+            operands.append(new_extra)
+            specs.append(hbm)
+        shapes.append(jax.ShapeDtypeStruct(extra_near.shape, f32))
         out_specs.append(hbm)
-        copies += 3
+        copies += len(leaving)
     shapes += [
         pltpu.VMEM((here, 3, count, cells), f32),
         jax.ShapeDtypeStruct((6, here, depth, LANES), f32),
     ]
     out_specs += [vmem, vmem]
     results = pl.pallas_call(
-        functools.partial(ordinary, first, has_block, has_base, has_extra),
+        functools.partial(ordinary, first, has_block, has_base, leaving, has_old),
         out_shape=tuple(shapes),
         in_specs=specs,
         out_specs=tuple(out_specs),
@@ -534,7 +554,7 @@
     results = list(results)
     piece, block = results.pop(), results.pop()
     new_base = results.pop(0) if has_block else None
-    return new_base, block, piece, (results[0] if has_extra else None)
+    return new_base, block, piece, (results[0] if leaving else None)
 
 
 def extra(unroll, before, base, noise, moments, *refs):
@@ -542,7 +562,7 @@
     _, _, _, count, cells = base.shape
     inverse = 1.0 / float(ALL_FIELDS)
     zero = jnp.zeros((SUB, LANES), f32)
-    message[...] = sum(part[...] for part in parts)
+    message[...] = sum(part[0] for part in parts)
     own = coefficients([message[i] for i in range(9)], [moments[i] for i in range(16)])
     both = [message[9 + i] + own[i] for i in range(3)]
     first = relax_of(both[2], inverse)
@@ -582,7 +602,7 @@
         ),
         in_specs=[anywhere, vmem, vmem, vmem] + [vmem] * len(parts),
         out_specs=(vmem, vmem),
-        scratch_shapes=[pltpu.VMEM(parts[0].shape, f32)],
+        scratch_shapes=[pltpu.VMEM(parts[0].shape[1:], f32)],
         compiler_params=pltpu.CompilerParams(vmem_limit_bytes=SMALL),
         cost_estimate=small(32 << 20, 9 << 20),
         name="extra_fields",
@@ -645,9 +665,10 @@
         @pl.when(k < places)
         def _(k=k, h=h, tile=tile):
             flip = (me ^ h) >> 1
-            is_far = ((me ^ h) & 1) == 1
+            is_far, odd = ((me ^ h) & 1) == 1, (h & 1) == 1
+            place = by_stage(flip, near.shape[0], odd)
             for i in range(near.shape[1]):
-                answer[i] = jnp.where(is_far, far[flip, i], near[flip, i])
+                answer[i] = jnp.where(is_far, far[place, i], near[place, i])
 
             def sums_of(x):
                 lanes = pl.ds(x * LANES, LANES)
@@ -711,35 +732,41 @@
     velocity, wall_cells, tile_counts, helper_tile, base_fields, extra_fields, base_noise, extra_noise
 ):
     tiles = tile_counts.shape[2]
-    pairs = lax.axis_size("gy") // 2
+    stages = (lax.axis_size("gy") // 2).bit_length() - 1
     helper_tile, x_one, x_two, y_one, y_two = call_edges(helper_tile, velocity)
     halos = two_swaps(x_one, x_two, "gx") + two_swaps(y_one, y_two, "gy")
     moments = call_heavy_moments(helper_tile, base_fields, base_noise)
     grad, keep, send = call_gradients(tiles, helper_tile, velocity, halos, wall_cells, moments)
-    gaps = 3
-    new_base, block, pieces, done = None, None, [], 0
-
-    def fill(before, extra_near=None):
-        nonlocal new_base, block, done
+    gaps = 2 * stages
+    new_base, block, pieces, done, new_extra = None, None, [], 0, None
+
+    def fill(before, extra_near=None, leaving=()):
+        nonlocal new_base, block, done, new_extra
         here = (tiles - done) // (gaps - len(pieces))
         new_base, block, piece, extra_far = call_ordinary(
-            done, here, before, base_fields, base_noise, grad, block, new_base, extra_near
+            done, here, before, base_fields, base_noise, grad, block, new_base, extra_near, leaving, new_extra
         )
+        new_extra = extra_far if leaving else new_extra
         pieces.append(piece)
         done += here
-        return piece, extra_far
-
-    received = swapped(send, 1)
-    before, _ = fill(send)
-    keep, *sends = call_merge(before, keep, received)
-    parts = [keep] + [swapped(send, 2 * flip) for flip, send in enumerate(sends, 1)]
-    extra_sums = call_extra_moments(sends[0], extra_fields, extra_noise)
-    before, _ = fill(extra_sums)
-    extra_near, reply = call_extra(before, extra_fields, extra_noise, extra_sums, parts)
-    replies = [reply] + [swapped(reply, 2 * flip) for flip in range(1, pairs)]
-    before, new_extra = fill(reply, extra_near)
-    near = call_join(before, replies)
-    far = swapped(near, 1)
+        return piece
+
+    received = swapped_within(send)
+    before = fill(send)
+    for stage in range(stages):
+        keep, send = call_halve(stage == 0, before, keep, received)
+        received = swapped_across(send, stage)
+        if stage == 0:
+            before = extra_sums = call_extra_moments(send, extra_fields, extra_noise)
+        else:
+            before = fill(send)
+    extra_near, reply = call_extra(before, extra_fields, extra_noise, extra_sums, [keep, received])
+    near = reply[None]
+    for stage in range(stages):
+        received = swapped_across(near, stage)
+        before = fill(near, extra_near, ((0,), (1, 2))[stage] if stage < 2 else ())
+        near = call_join(before, near, received)
+    far = swapped_within(near)
     new_base, ready = call_finish(near, block, pieces, new_base)
     new_base, stress = call_heavy(helper_tile, base_fields, base_noise, grad, near, far, ready, new_base)
     return new_base, new_extra, jnp.swapaxes(stress, 2, 3)

time: 32.6 us -> 36.3 us (1.11)
  waiting for transfers between devices: 3.88 us -> 7.26 us
  Pallas kernels: 11.4 us -> 13.6 us
  starting transfers between devices: 15.4 us -> 13.5 us
    ppermute x8 -> x6, waiting for transfers between devices: 2.71 us -> 7.25 us  [the longest x4 6.76 us: swapped_across(): lax.ppermute(block, 'gy', [(i, i ^ 2 << (bits - 1 - stage if i & 1 else s...]
    ppermute x8 -> x6, starting transfers between devices: 7.25 us -> 5.39 us  [the longest x4 5.25 us: swapped_across(): lax.ppermute(block, 'gy', [(i, i ^ 2 << (bits - 1 - stage if i & 1 else s...]
    pallas_call x1, Pallas kernels: 0.26 us -> 1.65 us  [call_heavy_moments(): pl.pallas_call(heavy_moments, out_shape=jax.ShapeDtypeStruct((slots, 16,...]
    ppermute x4, waiting for transfers between devices: 1.17 us -> 0.01 us  [two_swaps(): return (lax.ppermute(one, axis, within), lax.ppermute(two, axis, across))]
    pallas_call x5 -> x8, Pallas kernels: 3.91 us -> 4.41 us  [the longest x4 4.36 us: call_ordinary(): pl.pallas_call(functools.partial(ordinary, first, has_block, has_base, le...]
    pallas_call x1, Pallas kernels: 0.96 us -> 1.36 us  [call_heavy(): pl.pallas_call(heavy, out_shape=(jax.ShapeDtypeStruct(new_base.shape, f32...]
  transfers between devices with their start and end apart: 12 -> 10, of which waited for: 5 -> 6; matrix products, arithmetic and copies ran while one was open for 0% -> 0% of each run, Pallas kernels for 20% -> 23%
where the time goes in v6:
time: 36.3 us; the launch traced here: 36.2 us
  Pallas kernels  13.6 us (37%)
  starting transfers between devices  13.5 us (37%)
  waiting for transfers between devices  7.26 us (20%)
  local copies, waits for them, and re-layouts  0.99 us (3%)
  between operations  0.8 us (2%)
    ppermute x4, starting transfers between devices, two_swaps(): return (lax.ppermute(one, axis, within), lax.ppermute(two, axis, across))  8.13 us
    ppermute x4, waiting for transfers between devices, swapped_across(): lax.ppermute(block, 'gy', [(i, i ^ 2 << (bits - 1 - stage if i & 1 else s...  6.76 us
    ppermute x4, starting transfers between devices, swapped_across(): lax.ppermute(block, 'gy', [(i, i ^ 2 << (bits - 1 - stage if i & 1 else s...  5.25 us
    pallas_call x4, Pallas kernels, call_ordinary(): pl.pallas_call(functools.partial(ordinary, first, has_block, has_base, le...  4.36 us
    pallas_call x1, Pallas kernels, call_extra(): pl.pallas_call(functools.partial(extra, 7), out_shape=(pltpu.VMEM(extra_f...  2.25 us
    pallas_call x1, Pallas kernels, call_heavy_moments(): pl.pallas_call(heavy_moments, out_shape=jax.ShapeDtypeStruct((slots, 16,...  1.65 us
    pallas_call x1, Pallas kernels, call_extra_moments(): pl.pallas_call(functools.partial(extra_moments, 7), out_shape=jax.ShapeDt...  1.4 us
    pallas_call x1, Pallas kernels, call_heavy(): pl.pallas_call(heavy, out_shape=(jax.ShapeDtypeStruct(new_base.shape, f32...  1.36 us
  transfers between devices with their start and end apart: 10, of which 6 were waited for; matrix products, arithmetic and copies ran while one was open for 0% of the time, Pallas kernels for 23%

profile of v6, /device:TPU:0, one launch (start us, length us, event | category | flops | bytes accessed | tf_op | source)
XLA Modules:
  0.0 36.2 jit_solution(16581933054416260996)
XLA Ops:
  0.6 0.9 %edges.1 = (s32[1,8]{1,0:T(1,128)S(1)}, f32[3,8,128]{2,1,0:T(8,128)S(1)}, f32[3,8,128]{2,1,0:T(8,128)S(1)}, f32[3,8,128]{2,1,0:T(8,128)S(1)}, f32[3,8,128]{2,1,0:T(8,128)S(1)}) custom-call(s32[1,8]{1,0:T(1,128)} %helper.1, f32[3,8,8,128]{3,2,1,0:T(8,128)} %velocity.3), custom_call_target="tpu_custom_call" | custom-call | flops 1024 | bytes 131072 | tf_op jit(solution)/shard_map/edges/pallas_call | solution.py:170
  1.6 3.1 %collective-permute-start = (f32[3,8,128]{2,1,0:T(8,128)S(1)}, f32[3,8,128]{2,1,0:T(8,128)S(1)}, u32[]{:S(2)}, u32[]{:S(2)}) collective-permute-start(f32[3,8,128]{2,1,0:T(8,128)S(1)} %get-tuple-element.35), channel_id=1, source_target_pairs={{0,8},{8,0},{16,24},{24,16},{1,9},{9,1},{17,25},{25,17},{2,10},{10... | collective-permute-start | bytes 36872 | tf_op jit(solution)/shard_map/ppermute | solution.py:185
  4.7 2.5 %collective-permute-start.1 = (f32[3,8,128]{2,1,0:T(8,128)S(1)}, f32[3,8,128]{2,1,0:T(8,128)S(1)}, u32[]{:S(2)}, u32[]{:S(2)}) collective-permute-start(f32[3,8,128]{2,1,0:T(8,128)S(1)} %get-tuple-element.36), channel_id=1, source_target_pairs={{0,24},{8,16},{16,8},{24,0},{1,25},{9,17},{17,9},{25,1},{2,26},{10... | collective-permute-start | bytes 36872 | tf_op jit(solution)/shard_map/ppermute | solution.py:185
  7.1 0.0 collective-permute-start.2
  7.1 2.6 %collective-permute-start.3 = (f32[3,8,128]{2,1,0:T(8,128)S(1)}, f32[3,8,128]{2,1,0:T(8,128)S(1)}, u32[]{:S(2)}, u32[]{:S(2)}) collective-permute-start(f32[3,8,128]{2,1,0:T(8,128)S(1)} %get-tuple-element.38), channel_id=1, source_target_pairs={{0,7},{1,2},{2,1},{3,4},{4,3},{5,6},{6,5},{7,0},{8,15},{9,10},{10,... | collective-permute-start | bytes 36872 | tf_op jit(solution)/shard_map/ppermute | solution.py:185
  9.7 1.6 %heavy_moments.1.moments = f32[8,16,8,128]{3,2,1,0:T(8,128)S(1)} custom-call(s32[1,8]{1,0:T(1,128)S(1)} %get-tuple-element.34.helper, f32[1,1,8,3,32,1024]{5,4,3,2,1,0:T(8,128)} %base.7, bf16[1,1,8,2,3,32,1024]{6,5,4,3,2,1,0:T(8,128)(2,1)} %noise.7), custom_call_target="tpu_custom_call" | custom-call | flops 8388608 | bytes 3145728 | tf_op jit(solution)/shard_map/heavy_moments/pallas_call | solution.py:238
  11.4 0.0 collective-permute-done.x_one
  11.4 0.0 collective-permute-done.1.x_two
  11.4 0.0 collective-permute-done.2.y_one
  11.4 0.7 %gradients.1 = (f32[576,128]{1,0:T(8,128)S(1)}, f32[4,12,8,128]{3,2,1,0:T(8,128)S(1)}, f32[4,12,8,128]{3,2,1,0:T(8,128)S(1)}) custom-call(s32[1,8]{1,0:T(1,128)S(1)} %get-tuple-element.34.helper, f32[3,8,8,128]{3,2,1,0:T(8,128)S(1)} %copy-done.4, f32[3,8,128]{2,1,0:T(8,128)S(1)} %collective-permute-done.x_one, ...), custom_call_target="tpu_custom_call" | custom-call | flops 4194304 | bytes 1048576 | tf_op jit(solution)/shard_map/gradients/pallas_call | solution.py:340
  12.1 0.1 collective-permute-start.4
  12.2 0.6 %copy-done.1 = bf16[1,1,8,2,3,32,1024]{6,5,4,3,2,1,0:T(8,128)(2,1)S(1)} copy-done((bf16[1,1,8,2,3,32,1024]{6,5,4,3,2,1,0:T(8,128)(2,1)S(1)}, bf16[1,1,8,2,3,32,1024]{6,5,4,3,2,1,0:T(8,128)(2,1)}, u32[]{:S(2)}) %copy-start.1) | copy-done | bytes 3145752
  12.8 0.7 %ordinary_tiles.4 = (f32[2,3,32,1024]{3,2,1,0:T(8,128)S(1)}, f32[6,2,8,128]{3,2,1,0:T(8,128)S(1)}) custom-call(f32[4,12,8,128]{3,2,1,0:T(8,128)S(1)} %get-tuple-element.40.refs_0_, f32[1,1,8,3,32,1024]{5,4,3,2,1,0:T(8,128)S(1)} %copy-done, bf16[1,1,8,2,3,32,1024]{6,5,4,3,2,1,0:T(8,128)(2,1)S(1)} %copy-done.1, f32[576,128]{1,0:T(8,128)S(1)} %get-tuple-element.39.refs_3_.grad), custom_call_target="tpu_custom_call" | custom-call | flops 8388608 | bytes 3145728 | tf_op jit(solution)/shard_map/ordinary_tiles/pallas_call | solution.py:539
  13.6 0.1 collective-permute-done.4.received
  13.7 1.4 %collective-permute-start.5 = (f32[2,12,8,128]{3,2,1,0:T(8,128)S(1)}, f32[2,12,8,128]{3,2,1,0:T(8,128)S(1)}, u32[]{:S(2)}, u32[]{:S(2)}) collective-permute-start(f32[2,12,8,128]{3,2,1,0:T(8,128)S(1)} %get-tuple-element.43.before), channel_id=1, source_target_pairs={{0,2},{1,5},{2,0},{3,7},{4,6},{5,1},{6,4},{7,3},{8,10},{9,13},{10,... | collective-permute-start | bytes 294920 | tf_op jit(solution)/shard_map/ppermute | solution.py:359
  15.1 0.4 %copy-done.3 = bf16[1,1,2,3,224,1024]{5,4,3,2,1,0:T(8,128)(2,1)S(1)} copy-done((bf16[1,1,2,3,224,1024]{5,4,3,2,1,0:T(8,128)(2,1)S(1)}, bf16[1,1,2,3,224,1024]{5,4,3,2,1,0:T(8,128)(2,1)}, u32[]{:S(2)}) %copy-start.3) | copy-done | bytes 2752536
  15.4 1.4 %extra_moments.1.before.moments = f32[16,8,128]{2,1,0:T(8,128)S(1)} custom-call(f32[2,12,8,128]{3,2,1,0:T(8,128)S(1)} %get-tuple-element.43.before, f32[1,1,3,224,1024]{4,3,2,1,0:T(8,128)S(1)} %copy-done.2, bf16[1,1,2,3,224,1024]{5,4,3,2,1,0:T(8,128)(2,1)S(1)} %copy-done.3), custom_call_target="tpu_custom_call" | custom-call | flops 8388608 | bytes 5242880 | tf_op jit(solution)/shard_map/extra_moments/pallas_call | solution.py:276
  16.8 1.5 %collective-permute-done.5.received = f32[2,12,8,128]{3,2,1,0:T(8,128)S(1)} collective-permute-done((f32[2,12,8,128]{3,2,1,0:T(8,128)S(1)}, f32[2,12,8,128]{3,2,1,0:T(8,128)S(1)}, u32[]{:S(2)}, u32[]{:S(2)}) %collective-permute-start.5) | collective-permute-done | bytes 98336 | tf_op jit(solution)/shard_map/ppermute | solution.py:359
  18.4 1.3 %collective-permute-start.6 = (f32[1,12,8,128]{3,2,1,0:T(8,128)S(1)}, f32[1,12,8,128]{3,2,1,0:T(8,128)S(1)}, u32[]{:S(2)}, u32[]{:S(2)}) collective-permute-start(f32[1,12,8,128]{3,2,1,0:T(8,128)S(1)} %get-tuple-element.45.refs_0_), channel_id=1, source_target_pairs={{0,4},{1,3},{2,6},{3,1},{4,0},{5,7},{6,2},{7,5},{8,12},{9,11},{10,... | collective-permute-start | bytes 147464 | tf_op jit(solution)/shard_map/ppermute | solution.py:359
  19.7 0.9 %ordinary_tiles.5 = (f32[1,1,8,3,32,1024]{5,4,3,2,1,0:T(8,128)}, f32[2,3,32,1024]{3,2,1,0:T(8,128)S(1)}, f32[6,2,8,128]{3,2,1,0:T(8,128)S(1)}) custom-call(f32[1,12,8,128]{3,2,1,0:T(8,128)S(1)} %get-tuple-element.45.refs_0_, f32[1,1,8,3,32,1024]{5,4,3,2,1,0:T(8,128)S(1)} %copy-done, bf16[1,1,8,2,3,32,1024]{6,5,4,3,2,1,0:T(8,128)(2,1)S(1)} %copy-done.1, ...), custom_call_target="tpu_custom_call" | custom-call | flops 8388608 | bytes 3145728 | tf_op jit(solution)/shard_map/ordinary_tiles/pallas_call | solution.py:539
  20.6 2.0 %collective-permute-done.6.refs_1_ = f32[1,12,8,128]{3,2,1,0:T(8,128)S(1)} collective-permute-done((f32[1,12,8,128]{3,2,1,0:T(8,128)S(1)}, f32[1,12,8,128]{3,2,1,0:T(8,128)S(1)}, u32[]{:S(2)}, u32[]{:S(2)}) %collective-permute-start.6) | collective-permute-done | bytes 49184 | tf_op jit(solution)/shard_map/ppermute | solution.py:359
  22.5 2.3 %extra_fields.1 = (f32[1,1,3,224,1024]{4,3,2,1,0:T(8,128)S(1)}, f32[8,8,128]{2,1,0:T(8,128)S(1)}) custom-call(f32[6,2,8,128]{3,2,1,0:T(8,128)S(1)} %get-tuple-element.47.before.refs_1_, f32[1,1,3,224,1024]{4,3,2,1,0:T(8,128)S(1)} %copy-done.2, bf16[1,1,2,3,224,1024]{5,4,3,2,1,0:T(8,128)(2,1)S(1)} %copy-done.3, ...), custom_call_target="tpu_custom_call" | custom-call | flops 33554432 | bytes 9437184 | tf_op jit(solution)/shard_map/extra_fields/pallas_call | solution.py:597
  24.8 1.4 %collective-permute-start.7 = (f32[1,8,8,128]{3,2,1,0:T(8,128)S(1)}, f32[1,8,8,128]{3,2,1,0:T(8,128)S(1)}, u32[]{:S(2)}, u32[]{:S(2)}) collective-permute-start(f32[1,8,8,128]{3,2,1,0:T(8,128)S(1)} %bitcast.2), channel_id=1, source_target_pairs={{0,2},{1,5},{2,0},{3,7},{4,6},{5,1},{6,4},{7,3},{8,10},{9,13},{10,... | collective-permute-start | bytes 98312 | tf_op jit(solution)/shard_map/ppermute | solution.py:359
  26.2 1.2 %ordinary_tiles.6 = (f32[1,1,8,3,32,1024]{5,4,3,2,1,0:T(8,128)}, f32[1,1,3,224,1024]{4,3,2,1,0:T(8,128)}, f32[2,3,32,1024]{3,2,1,0:T(8,128)S(1)}, f32[6,2,8,128]{3,2,1,0:T(8,128)S(1)}) custom-call(f32[1,8,8,128]{3,2,1,0:T(8,128)S(1)} %bitcast.3, f32[1,1,8,3,32,1024]{5,4,3,2,1,0:T(8,128)S(1)} %copy-done, ...), custom_call_target="tpu_custom_call", output_to_operand_aliasing={{0}: (5, {})} | custom-call | flops 8388608 | bytes 3145728 | tf_op jit(solution)/shard_map/ordinary_tiles/pallas_call | solution.py:539
  27.4 1.7 %collective-permute-done.7.second = f32[1,8,8,128]{3,2,1,0:T(8,128)S(1)} collective-permute-done((f32[1,8,8,128]{3,2,1,0:T(8,128)S(1)}, f32[1,8,8,128]{3,2,1,0:T(8,128)S(1)}, u32[]{:S(2)}, u32[]{:S(2)}) %collective-permute-start.7) | collective-permute-done | bytes 32800 | tf_op jit(solution)/shard_map/ppermute | solution.py:359
  29.1 1.2 %collective-permute-start.8 = (f32[2,8,8,128]{3,2,1,0:T(8,128)S(1)}, f32[2,8,8,128]{3,2,1,0:T(8,128)S(1)}, u32[]{:S(2)}, u32[]{:S(2)}) collective-permute-start(f32[2,8,8,128]{3,2,1,0:T(8,128)S(1)} %join.2.refs_0_.first), channel_id=1, source_target_pairs={{0,4},{1,3},{2,6},{3,1},{4,0},{5,7},{6,2},{7,5},{8,12},{9,11},{10,... | collective-permute-start | bytes 196616 | tf_op jit(solution)/shard_map/ppermute | solution.py:359
  30.3 1.5 %ordinary_tiles.7 = (f32[1,1,8,3,32,1024]{5,4,3,2,1,0:T(8,128)}, f32[1,1,3,224,1024]{4,3,2,1,0:T(8,128)}, f32[2,3,32,1024]{3,2,1,0:T(8,128)S(1)}, f32[6,2,8,128]{3,2,1,0:T(8,128)S(1)}) custom-call(f32[2,8,8,128]{3,2,1,0:T(8,128)S(1)} %join.2.refs_0_.first, f32[1,1,8,3,32,1024]{5,4,3,2,1,0:T(8,128)S(1)} %copy-done, ...), custom_call_target="tpu_custom_call", output_to_operand_aliasing={{0}: (5, {}), {1}: (7, {})} | custom-call | flops 8388608 | bytes 3145728 | tf_op jit(solution)/shard_map/ordinary_tiles/pallas_call | solution.py:539
  31.8 1.6 %collective-permute-done.8.second = f32[2,8,8,128]{3,2,1,0:T(8,128)S(1)} collective-permute-done((f32[2,8,8,128]{3,2,1,0:T(8,128)S(1)}, f32[2,8,8,128]{3,2,1,0:T(8,128)S(1)}, u32[]{:S(2)}, u32[]{:S(2)}) %collective-permute-start.8) | collective-permute-done | bytes 65568 | tf_op jit(solution)/shard_map/ppermute | solution.py:359
  33.4 0.1 collective-permute-start.9
  33.5 0.9 %finish.1 = (f32[1,1,8,3,32,1024]{5,4,3,2,1,0:T(8,128)}, f32[6,8,8,128]{3,2,1,0:T(8,128)S(1)}) custom-call(f32[4,8,8,128]{3,2,1,0:T(8,128)S(1)} %join.3.before.near, f32[2,3,32,1024]{3,2,1,0:T(8,128)S(1)} %get-tuple-element.58.block, f32[6,2,8,128]{3,2,1,0:T(8,128)S(1)} %get-tuple-element.41.before.refs_0_, ...), custom_call_target="tpu_custom_call", output_to_operand_aliasing={{0}: (6, {})} | custom-call | flops 1024 | bytes 1048576 | tf_op jit(solution)/shard_map/finish/pallas_call | solution.py:632
  34.4 0.4 %collective-permute-done.9.far = f32[4,8,8,128]{3,2,1,0:T(8,128)S(1)} collective-permute-done((f32[4,8,8,128]{3,2,1,0:T(8,128)S(1)}, f32[4,8,8,128]{3,2,1,0:T(8,128)S(1)}, u32[]{:S(2)}, u32[]{:S(2)}) %collective-permute-start.9) | collective-permute-done | bytes 131104 | tf_op jit(solution)/shard_map/ppermute | solution.py:353
  34.8 1.4 %heavy_tiles.1 = (f32[1,1,8,3,32,1024]{5,4,3,2,1,0:T(8,128)}, f32[1,1,6,8,1024]{4,3,2,1,0:T(8,128)}) custom-call(s32[1,8]{1,0:T(1,128)S(1)} %get-tuple-element.34.helper, f32[1,1,8,3,32,1024]{5,4,3,2,1,0:T(8,128)S(1)} %copy-done, bf16[1,1,8,2,3,32,1024]{6,5,4,3,2,1,0:T(8,128)(2,1)S(1)} %copy-done.1, ...), custom_call_target="tpu_custom_call", output_to_operand_aliasing={{0}: (7, {})} | custom-call | flops 8388608 | bytes 4194304 | tf_op jit(solution)/shard_map/heavy_tiles/pallas_call | solution.py:710
  (15 shorter events, 0.1 us)
Async XLA Ops:
  1.6 9.8 %collective-permute-start = (f32[3,8,128]{2,1,0:T(8,128)S(1)}, f32[3,8,128]{2,1,0:T(8,128)S(1)}, u32[]{:S(2)}, u32[]{:S(2)}) collective-permute-start(f32[3,8,128]{2,1,0:T(8,128)S(1)} %get-tuple-element.35), channel_id=1, source_target_pairs={{0,8},{8,0},{16,24},{24,16},{1,9},{9,1},{17,25},{25,17},{2,10},{10... | collective-permute-start | bytes 36872 | tf_op jit(solution)/shard_map/ppermute | solution.py:185
  4.7 6.7 %collective-permute-start.1 = (f32[3,8,128]{2,1,0:T(8,128)S(1)}, f32[3,8,128]{2,1,0:T(8,128)S(1)}, u32[]{:S(2)}, u32[]{:S(2)}) collective-permute-start(f32[3,8,128]{2,1,0:T(8,128)S(1)} %get-tuple-element.36), channel_id=1, source_target_pairs={{0,24},{8,16},{16,8},{24,0},{1,25},{9,17},{17,9},{25,1},{2,26},{10... | collective-permute-start | bytes 36872 | tf_op jit(solution)/shard_map/ppermute | solution.py:185
  7.1 4.3 %collective-permute-start.2 = (f32[3,8,128]{2,1,0:T(8,128)S(1)}, f32[3,8,128]{2,1,0:T(8,128)S(1)}, u32[]{:S(2)}, u32[]{:S(2)}) collective-permute-start(f32[3,8,128]{2,1,0:T(8,128)S(1)} %get-tuple-element.37), channel_id=1, source_target_pairs={{0,1},{1,0},{2,3},{3,2},{4,5},{5,4},{6,7},{7,6},{8,9},{9,8},{10,11... | collective-permute-start | bytes 36872 | tf_op jit(solution)/shard_map/ppermute | solution.py:185
  7.1 4.3 %collective-permute-start.3 = (f32[3,8,128]{2,1,0:T(8,128)S(1)}, f32[3,8,128]{2,1,0:T(8,128)S(1)}, u32[]{:S(2)}, u32[]{:S(2)}) collective-permute-start(f32[3,8,128]{2,1,0:T(8,128)S(1)} %get-tuple-element.38), channel_id=1, source_target_pairs={{0,7},{1,2},{2,1},{3,4},{4,3},{5,6},{6,5},{7,0},{8,15},{9,10},{10,... | collective-permute-start | bytes 36872 | tf_op jit(solution)/shard_map/ppermute | solution.py:185
  9.7 1.7 %copy-start.4 = (f32[3,8,8,128]{3,2,1,0:T(8,128)S(1)}, f32[3,8,8,128]{3,2,1,0:T(8,128)}, u32[]{:S(2)}) copy-start(f32[3,8,8,128]{3,2,1,0:T(8,128)} %velocity.3) | copy-start | bytes 294916
  9.7 1.7 %copy-start.5 = (s32[8,8,128]{2,1,0:T(8,128)S(1)}, s32[8,8,128]{2,1,0:T(8,128)}, u32[]{:S(2)}) copy-start(s32[8,8,128]{2,1,0:T(8,128)} %wall.1) | copy-start | bytes 98308
  9.7 2.5 %copy-start = (f32[1,1,8,3,32,1024]{5,4,3,2,1,0:T(8,128)S(1)}, f32[1,1,8,3,32,1024]{5,4,3,2,1,0:T(8,128)}, u32[]{:S(2)}) copy-start(f32[1,1,8,3,32,1024]{5,4,3,2,1,0:T(8,128)} %base.7) | copy-start | bytes 9437188
  9.7 3.1 %copy-start.1 = (bf16[1,1,8,2,3,32,1024]{6,5,4,3,2,1,0:T(8,128)(2,1)S(1)}, bf16[1,1,8,2,3,32,1024]{6,5,4,3,2,1,0:T(8,128)(2,1)}, u32[]{:S(2)}) copy-start(bf16[1,1,8,2,3,32,1024]{6,5,4,3,2,1,0:T(8,128)(2,1)} %noise.7) | copy-start | bytes 9437188
  12.1 1.5 %collective-permute-start.4 = (f32[4,12,8,128]{3,2,1,0:T(8,128)S(1)}, f32[4,12,8,128]{3,2,1,0:T(8,128)S(1)}, u32[]{:S(2)}, u32[]{:S(2)}) collective-permute-start(f32[4,12,8,128]{3,2,1,0:T(8,128)S(1)} %get-tuple-element.40.refs_0_), channel_id=1, source_target_pairs={{0,1},{1,0},{2,3},{3,2},{4,5},{5,4},{6,7},{7,6},{8,9},{9,8},{10,11... | collective-permute-start | bytes 589832 | tf_op jit(solution)/shard_map/ppermute | solution.py:353
  12.8 2.2 %copy-start.2 = (f32[1,1,3,224,1024]{4,3,2,1,0:T(8,128)S(1)}, f32[1,1,3,224,1024]{4,3,2,1,0:T(8,128)}, u32[]{:S(2)}) copy-start(f32[1,1,3,224,1024]{4,3,2,1,0:T(8,128)} %base.6) | copy-start | bytes 8257540
  12.8 2.6 %copy-start.3 = (bf16[1,1,2,3,224,1024]{5,4,3,2,1,0:T(8,128)(2,1)S(1)}, bf16[1,1,2,3,224,1024]{5,4,3,2,1,0:T(8,128)(2,1)}, u32[]{:S(2)}) copy-start(bf16[1,1,2,3,224,1024]{5,4,3,2,1,0:T(8,128)(2,1)} %noise.6) | copy-start | bytes 8257540
  13.7 4.7 %collective-permute-start.5 = (f32[2,12,8,128]{3,2,1,0:T(8,128)S(1)}, f32[2,12,8,128]{3,2,1,0:T(8,128)S(1)}, u32[]{:S(2)}, u32[]{:S(2)}) collective-permute-start(f32[2,12,8,128]{3,2,1,0:T(8,128)S(1)} %get-tuple-element.43.before), channel_id=1, source_target_pairs={{0,2},{1,5},{2,0},{3,7},{4,6},{5,1},{6,4},{7,3},{8,10},{9,13},{10,... | collective-permute-start | bytes 294920 | tf_op jit(solution)/shard_map/ppermute | solution.py:359
  18.4 4.2 %collective-permute-start.6 = (f32[1,12,8,128]{3,2,1,0:T(8,128)S(1)}, f32[1,12,8,128]{3,2,1,0:T(8,128)S(1)}, u32[]{:S(2)}, u32[]{:S(2)}) collective-permute-start(f32[1,12,8,128]{3,2,1,0:T(8,128)S(1)} %get-tuple-element.45.refs_0_), channel_id=1, source_target_pairs={{0,4},{1,3},{2,6},{3,1},{4,0},{5,7},{6,2},{7,5},{8,12},{9,11},{10,... | collective-permute-start | bytes 147464 | tf_op jit(solution)/shard_map/ppermute | solution.py:359
  24.8 4.3 %collective-permute-start.7 = (f32[1,8,8,128]{3,2,1,0:T(8,128)S(1)}, f32[1,8,8,128]{3,2,1,0:T(8,128)S(1)}, u32[]{:S(2)}, u32[]{:S(2)}) collective-permute-start(f32[1,8,8,128]{3,2,1,0:T(8,128)S(1)} %bitcast.2), channel_id=1, source_target_pairs={{0,2},{1,5},{2,0},{3,7},{4,6},{5,1},{6,4},{7,3},{8,10},{9,13},{10,... | collective-permute-start | bytes 98312 | tf_op jit(solution)/shard_map/ppermute | solution.py:359
  29.1 4.3 %collective-permute-start.8 = (f32[2,8,8,128]{3,2,1,0:T(8,128)S(1)}, f32[2,8,8,128]{3,2,1,0:T(8,128)S(1)}, u32[]{:S(2)}, u32[]{:S(2)}) collective-permute-start(f32[2,8,8,128]{3,2,1,0:T(8,128)S(1)} %join.2.refs_0_.first), channel_id=1, source_target_pairs={{0,4},{1,3},{2,6},{3,1},{4,0},{5,7},{6,2},{7,5},{8,12},{9,11},{10,... | collective-permute-start | bytes 196616 | tf_op jit(solution)/shard_map/ppermute | solution.py:359
  33.4 1.4 %collective-permute-start.9 = (f32[4,8,8,128]{3,2,1,0:T(8,128)S(1)}, f32[4,8,8,128]{3,2,1,0:T(8,128)S(1)}, u32[]{:S(2)}, u32[]{:S(2)}) collective-permute-start(f32[4,8,8,128]{3,2,1,0:T(8,128)S(1)} %join.3.before.near), channel_id=1, source_target_pairs={{0,1},{1,0},{2,3},{3,2},{4,5},{5,4},{6,7},{7,6},{8,9},{9,8},{10,11... | collective-permute-start | bytes 393224 | tf_op jit(solution)/shard_map/ppermute | solution.py:353

commit v7 on v5

--- a/solution.py
+++ b/solution.py
@@ -178,11 +178,13 @@
     )(*far_memory(helper_tile, velocity))
 
 
-def two_swaps(one, two, axis):
+def swap_within(block, axis):
+    return lax.ppermute(block, axis, [(i, i ^ 1) for i in range(lax.axis_size(axis))])
+
+
+def swap_across(block, axis):
     size = lax.axis_size(axis)
-    within = [(i, i ^ 1) for i in range(size)]
-    across = [(i, (i - 1 + 2 * (i & 1)) % size) for i in range(size)]
-    return lax.ppermute(one, axis, within), lax.ppermute(two, axis, across)
+    return lax.ppermute(block, axis, [(i, (i - 1 + 2 * (i & 1)) % size) for i in range(size)])
 
 
 def low_and_high(axis, one, two, a):
@@ -284,7 +286,7 @@
     )(before, *near_memory(extra_fields, extra_noise))
 
 
-def gradients(tiles, helper, velocity, x_one, x_two, y_one, y_two, wall, moments, grad, keep, send):
+def gradients(tiles, helper, velocity, y_two, x_two, x_one, y_one, wall, moments, grad, keep, send):
     me = lax.axis_index("gy")
     depth = velocity.shape[1]
     cell_z = velocity.shape[3] // tiles
@@ -713,7 +715,11 @@
     tiles = tile_counts.shape[2]
     pairs = lax.axis_size("gy") // 2
     helper_tile, x_one, x_two, y_one, y_two = call_edges(helper_tile, velocity)
-    halos = two_swaps(x_one, x_two, "gx") + two_swaps(y_one, y_two, "gy")
+    y_two = swap_across(y_two, "gy")
+    x_two = swap_across(x_two, "gx")
+    x_one = swap_within(x_one, "gx")
+    y_one = swap_within(y_one, "gy")
+    halos = (y_two, x_two, x_one, y_one)
     moments = call_heavy_moments(helper_tile, base_fields, base_noise)
     grad, keep, send = call_gradients(tiles, helper_tile, velocity, halos, wall_cells, moments)
     gaps = 3
@@ -732,13 +738,14 @@
     received = swapped(send, 1)
     before, _ = fill(send)
     keep, *sends = call_merge(before, keep, received)
-    parts = [keep] + [swapped(send, 2 * flip) for flip, send in enumerate(sends, 1)]
+    farthest_first = sorted(range(1, pairs), key=lambda flip: -flip.bit_count())
+    parts = [keep] + [swapped(sends[flip - 1], 2 * flip) for flip in farthest_first]
     extra_sums = call_extra_moments(sends[0], extra_fields, extra_noise)
     before, _ = fill(extra_sums)
     extra_near, reply = call_extra(before, extra_fields, extra_noise, extra_sums, parts)
-    replies = [reply] + [swapped(reply, 2 * flip) for flip in range(1, pairs)]
+    replies = {flip: swapped(reply, 2 * flip) for flip in farthest_first}
     before, new_extra = fill(reply, extra_near)
-    near = call_join(before, replies)
+    near = call_join(before, [reply] + [replies[flip] for flip in range(1, pairs)])
     far = swapped(near, 1)
     new_base, ready = call_finish(near, block, pieces, new_base)
     new_base, stress = call_heavy(helper_tile, base_fields, base_noise, grad, near, far, ready, new_base)

time: 32.6 us -> 33.3 us (1.021); the launches traced: 32.2 us -> 33.7 us
  Pallas kernels: 11.4 us -> 14.9 us
  starting transfers between devices: 15.4 us -> 14.3 us
  local copies, waits for them, and re-layouts: 0.7 us -> 0.04 us
    pallas_call x1, Pallas kernels: 0.26 us -> 2.31 us  [call_heavy_moments(): pl.pallas_call(heavy_moments, out_shape=jax.ShapeDtypeStruct((slots, 16,...]
    pallas_call x1, Pallas kernels: 0.96 us -> 2.31 us  [call_heavy(): pl.pallas_call(heavy, out_shape=(jax.ShapeDtypeStruct(new_base.shape, f32...]
    ppermute x4, starting transfers between devices: 8.13 us -> 7.01 us  [the longest x2 7 us: swap_across(): lax.ppermute(block, axis, [(i, (i - 1 + 2 * (i & 1)) % size) for i in ran...]
    unnamed x12, local copies, waits for them, and re-layouts: 0.7 us -> 0.04 us
    ppermute x8, waiting for transfers between devices: 2.71 us -> 2.3 us  [swapped(): return lax.ppermute(block, 'gy', [(i, i ^ flip) for i in range(size)])]
  transfers between devices with their start and end apart: 12 -> 12, of which waited for: 5 -> 4; matrix products, arithmetic and copies ran while one was open for 0% -> 0% of each run, Pallas kernels for 20% -> 26%
where the time goes in v7:
time: 33.3 us; the launch traced here: 33.7 us
  Pallas kernels  14.9 us (45%)
  starting transfers between devices  14.3 us (43%)
  waiting for transfers between devices  3.61 us (11%)
  between operations  0.85 us (3%)
    ppermute x8, starting transfers between devices, swapped(): return lax.ppermute(block, 'gy', [(i, i ^ flip) for i in range(size)])  7.25 us
    ppermute x2, starting transfers between devices, swap_across(): lax.ppermute(block, axis, [(i, (i - 1 + 2 * (i & 1)) % size) for i in ran...  7 us
    pallas_call x3, Pallas kernels, call_ordinary(): pl.pallas_call(functools.partial(ordinary, first, has_block, has_base, ha...  3.87 us
    pallas_call x1, Pallas kernels, call_heavy_moments(): pl.pallas_call(heavy_moments, out_shape=jax.ShapeDtypeStruct((slots, 16,...  2.31 us
    pallas_call x1, Pallas kernels, call_heavy(): pl.pallas_call(heavy, out_shape=(jax.ShapeDtypeStruct(new_base.shape, f32...  2.31 us
    ppermute x8, waiting for transfers between devices, swapped(): return lax.ppermute(block, 'gy', [(i, i ^ flip) for i in range(size)])  2.3 us
    pallas_call x1, Pallas kernels, call_extra(): pl.pallas_call(functools.partial(extra, 7), out_shape=(pltpu.VMEM(extra_f...  2.25 us
    pallas_call x1, Pallas kernels, call_extra_moments(): pl.pallas_call(functools.partial(extra_moments, 7), out_shape=jax.ShapeDt...  1.41 us
  transfers between devices with their start and end apart: 12, of which 4 were waited for; matrix products, arithmetic and copies ran while one was open for 0% of the time, Pallas kernels for 26%

profile of v7, /device:TPU:0, one launch (start us, length us, event | category | flops | bytes accessed | tf_op | source)
XLA Modules:
  0.0 33.7 jit_solution(7942686231112617223)
XLA Ops:
  0.6 0.9 %edges.1 = (s32[1,8]{1,0:T(1,128)S(1)}, f32[3,8,128]{2,1,0:T(8,128)S(1)}, f32[3,8,128]{2,1,0:T(8,128)S(1)}, f32[3,8,128]{2,1,0:T(8,128)S(1)}, f32[3,8,128]{2,1,0:T(8,128)S(1)}) custom-call(s32[1,8]{1,0:T(1,128)} %helper.1, f32[3,8,8,128]{3,2,1,0:T(8,128)} %velocity.3), custom_call_target="tpu_custom_call" | custom-call | flops 1024 | bytes 131072 | tf_op jit(solution)/shard_map/edges/pallas_call | solution.py:170
  1.6 3.4 %collective-permute-start = (f32[3,8,128]{2,1,0:T(8,128)S(1)}, f32[3,8,128]{2,1,0:T(8,128)S(1)}, u32[]{:S(2)}, u32[]{:S(2)}) collective-permute-start(f32[3,8,128]{2,1,0:T(8,128)S(1)} %get-tuple-element.31), channel_id=1, source_target_pairs={{0,7},{1,2},{2,1},{3,4},{4,3},{5,6},{6,5},{7,0},{8,15},{9,10},{10,... | collective-permute-start | bytes 36872 | tf_op jit(solution)/shard_map/ppermute | solution.py:187
  5.0 3.6 %collective-permute-start.1 = (f32[3,8,128]{2,1,0:T(8,128)S(1)}, f32[3,8,128]{2,1,0:T(8,128)S(1)}, u32[]{:S(2)}, u32[]{:S(2)}) collective-permute-start(f32[3,8,128]{2,1,0:T(8,128)S(1)} %get-tuple-element.32), channel_id=1, source_target_pairs={{0,24},{8,16},{16,8},{24,0},{1,25},{9,17},{17,9},{25,1},{2,26},{10... | collective-permute-start | bytes 36872 | tf_op jit(solution)/shard_map/ppermute | solution.py:187
  8.6 0.0 collective-permute-start.2
  8.6 0.0 collective-permute-start.3
  8.6 0.0 copy-start.5
  8.6 0.0 copy-start
  8.6 0.0 copy-start.1
  8.6 2.3 %heavy_moments.1.moments = f32[8,16,8,128]{3,2,1,0:T(8,128)S(1)} custom-call(s32[1,8]{1,0:T(1,128)S(1)} %get-tuple-element.30.helper, f32[1,1,8,3,32,1024]{5,4,3,2,1,0:T(8,128)} %base.7, bf16[1,1,8,2,3,32,1024]{6,5,4,3,2,1,0:T(8,128)(2,1)} %noise.7), custom_call_target="tpu_custom_call" | custom-call | flops 8388608 | bytes 3145728 | tf_op jit(solution)/shard_map/heavy_moments/pallas_call | solution.py:240
  10.9 0.0 collective-permute-done.1.x_two
  11.0 1.3 %collective-permute-done.2.x_one = f32[3,8,128]{2,1,0:T(8,128)S(1)} collective-permute-done((f32[3,8,128]{2,1,0:T(8,128)S(1)}, f32[3,8,128]{2,1,0:T(8,128)S(1)}, u32[]{:S(2)}, u32[]{:S(2)}) %collective-permute-start.2) | collective-permute-done | bytes 12320 | tf_op jit(solution)/shard_map/ppermute | solution.py:182
  12.3 0.8 %gradients.1 = (f32[576,128]{1,0:T(8,128)S(1)}, f32[4,12,8,128]{3,2,1,0:T(8,128)S(1)}, f32[4,12,8,128]{3,2,1,0:T(8,128)S(1)}) custom-call(s32[1,8]{1,0:T(1,128)S(1)} %get-tuple-element.30.helper, f32[3,8,8,128]{3,2,1,0:T(8,128)S(1)} %copy-done.4, f32[3,8,128]{2,1,0:T(8,128)S(1)} %collective-permute-done.y_two, ...), custom_call_target="tpu_custom_call" | custom-call | flops 4194304 | bytes 1048576 | tf_op jit(solution)/shard_map/gradients/pallas_call | solution.py:342
  13.1 0.1 collective-permute-start.4
  13.2 0.0 copy-start.2
  13.2 0.0 copy-start.3
  13.2 0.8 %ordinary_tiles.3 = (f32[2,3,32,1024]{3,2,1,0:T(8,128)S(1)}, f32[6,2,8,128]{3,2,1,0:T(8,128)S(1)}) custom-call(f32[4,12,8,128]{3,2,1,0:T(8,128)S(1)} %get-tuple-element.36.refs_0_, f32[1,1,8,3,32,1024]{5,4,3,2,1,0:T(8,128)S(1)} %copy-done, bf16[1,1,8,2,3,32,1024]{6,5,4,3,2,1,0:T(8,128)(2,1)S(1)} %copy-done.1, f32[576,128]{1,0:T(8,128)S(1)} %get-tuple-element.35.refs_3_.grad), custom_call_target="tpu_custom_call" | custom-call | flops 8388608 | bytes 3145728 | tf_op jit(solution)/shard_map/ordinary_tiles/pallas_call | solution.py:521
  13.9 0.6 %collective-permute-done.4.received = f32[4,12,8,128]{3,2,1,0:T(8,128)S(1)} collective-permute-done((f32[4,12,8,128]{3,2,1,0:T(8,128)S(1)}, f32[4,12,8,128]{3,2,1,0:T(8,128)S(1)}, u32[]{:S(2)}, u32[]{:S(2)}) %collective-permute-start.4) | collective-permute-done | bytes 196640 | tf_op jit(solution)/shard_map/ppermute | solution.py:355
  14.6 0.6 %collective-permute-start.5 = (f32[12,8,128]{2,1,0:T(8,128)S(1)}, f32[12,8,128]{2,1,0:T(8,128)S(1)}, u32[]{:S(2)}, u32[]{:S(2)}) collective-permute-start(f32[12,8,128]{2,1,0:T(8,128)S(1)} %get-tuple-element.43), channel_id=1, source_target_pairs={{0,6},{1,7},{2,4},{3,5},{4,2},{5,3},{6,0},{7,1},{8,14},{9,15},{10,... | collective-permute-start | bytes 147464 | tf_op jit(solution)/shard_map/ppermute | solution.py:355
  15.2 1.4 %collective-permute-start.6 = (f32[12,8,128]{2,1,0:T(8,128)S(1)}, f32[12,8,128]{2,1,0:T(8,128)S(1)}, u32[]{:S(2)}, u32[]{:S(2)}) collective-permute-start(f32[12,8,128]{2,1,0:T(8,128)S(1)} %get-tuple-element.39.before), channel_id=1, source_target_pairs={{0,2},{1,3},{2,0},{3,1},{4,6},{5,7},{6,4},{7,5},{8,10},{9,11},{10,... | collective-permute-start | bytes 147464 | tf_op jit(solution)/shard_map/ppermute | solution.py:355
  16.5 1.6 %collective-permute-start.7 = (f32[12,8,128]{2,1,0:T(8,128)S(1)}, f32[12,8,128]{2,1,0:T(8,128)S(1)}, u32[]{:S(2)}, u32[]{:S(2)}) collective-permute-start(f32[12,8,128]{2,1,0:T(8,128)S(1)} %get-tuple-element.44), channel_id=1, source_target_pairs={{0,4},{1,5},{2,6},{3,7},{4,0},{5,1},{6,2},{7,3},{8,12},{9,13},{10,... | collective-permute-start | bytes 147464 | tf_op jit(solution)/shard_map/ppermute | solution.py:355
  18.1 1.4 %extra_moments.1.refs_0_.moments = f32[16,8,128]{2,1,0:T(8,128)S(1)} custom-call(f32[12,8,128]{2,1,0:T(8,128)S(1)} %get-tuple-element.39.before, f32[1,1,3,224,1024]{4,3,2,1,0:T(8,128)S(1)} %copy-done.2, bf16[1,1,2,3,224,1024]{5,4,3,2,1,0:T(8,128)(2,1)S(1)} %copy-done.3), custom_call_target="tpu_custom_call" | custom-call | flops 8388608 | bytes 5242880 | tf_op jit(solution)/shard_map/extra_moments/pallas_call | solution.py:278
  19.6 1.1 %ordinary_tiles.4 = (f32[1,1,8,3,32,1024]{5,4,3,2,1,0:T(8,128)}, f32[3,3,32,1024]{3,2,1,0:T(8,128)S(1)}, f32[6,3,8,128]{3,2,1,0:T(8,128)S(1)}) custom-call(f32[16,8,128]{2,1,0:T(8,128)S(1)} %extra_moments.1.refs_0_.moments, f32[1,1,8,3,32,1024]{5,4,3,2,1,0:T(8,128)S(1)} %copy-done, bf16[1,1,8,2,3,32,1024]{6,5,4,3,2,1,0:T(8,128)(2,1)S(1)} %copy-done.1, ...), custom_call_target="tpu_custom_call" | custom-call | flops 8388608 | bytes 3145728 | tf_op jit(solution)/shard_map/ordinary_tiles/pallas_call | solution.py:521
  20.7 2.3 %extra_fields.1 = (f32[1,1,3,224,1024]{4,3,2,1,0:T(8,128)S(1)}, f32[8,8,128]{2,1,0:T(8,128)S(1)}) custom-call(f32[6,3,8,128]{3,2,1,0:T(8,128)S(1)} %get-tuple-element.41.before.refs_1_, f32[1,1,3,224,1024]{4,3,2,1,0:T(8,128)S(1)} %copy-done.2, bf16[1,1,2,3,224,1024]{5,4,3,2,1,0:T(8,128)(2,1)S(1)} %copy-done.3, ...), custom_call_target="tpu_custom_call" | custom-call | flops 33554432 | bytes 9437184 | tf_op jit(solution)/shard_map/extra_fields/pallas_call | solution.py:579
  23.0 1.0 %collective-permute-start.10 = (f32[8,8,128]{2,1,0:T(8,128)S(1)}, f32[8,8,128]{2,1,0:T(8,128)S(1)}, u32[]{:S(2)}, u32[]{:S(2)}) collective-permute-start(f32[8,8,128]{2,1,0:T(8,128)S(1)} %get-tuple-element.45.refs_0_), channel_id=1, source_target_pairs={{0,6},{1,7},{2,4},{3,5},{4,2},{5,3},{6,0},{7,1},{8,14},{9,15},{10,... | collective-permute-start | bytes 98312 | tf_op jit(solution)/shard_map/ppermute | solution.py:355
  24.0 2.0 %collective-permute-start.8 = (f32[8,8,128]{2,1,0:T(8,128)S(1)}, f32[8,8,128]{2,1,0:T(8,128)S(1)}, u32[]{:S(2)}, u32[]{:S(2)}) collective-permute-start(f32[8,8,128]{2,1,0:T(8,128)S(1)} %get-tuple-element.45.refs_0_), channel_id=1, source_target_pairs={{0,2},{1,3},{2,0},{3,1},{4,6},{5,7},{6,4},{7,5},{8,10},{9,11},{10,... | collective-permute-start | bytes 98312 | tf_op jit(solution)/shard_map/ppermute | solution.py:355
  26.0 0.5 %collective-permute-start.9 = (f32[8,8,128]{2,1,0:T(8,128)S(1)}, f32[8,8,128]{2,1,0:T(8,128)S(1)}, u32[]{:S(2)}, u32[]{:S(2)}) collective-permute-start(f32[8,8,128]{2,1,0:T(8,128)S(1)} %get-tuple-element.45.refs_0_), channel_id=1, source_target_pairs={{0,4},{1,5},{2,6},{3,7},{4,0},{5,1},{6,2},{7,3},{8,12},{9,13},{10,... | collective-permute-start | bytes 98312 | tf_op jit(solution)/shard_map/ppermute | solution.py:355
  26.6 2.0 %ordinary_tiles.5 = (f32[1,1,8,3,32,1024]{5,4,3,2,1,0:T(8,128)}, f32[1,1,3,224,1024]{4,3,2,1,0:T(8,128)}, f32[3,3,32,1024]{3,2,1,0:T(8,128)S(1)}, f32[6,3,8,128]{3,2,1,0:T(8,128)S(1)}) custom-call(f32[8,8,128]{2,1,0:T(8,128)S(1)} %get-tuple-element.45.refs_0_, f32[1,1,8,3,32,1024]{5,4,3,2,1,0:T(8,128)S(1)} %copy-done, ...), custom_call_target="tpu_custom_call", output_to_operand_aliasing={{0}: (5, {})} | custom-call | flops 8388608 | bytes 3145728 | tf_op jit(solution)/shard_map/ordinary_tiles/pallas_call | solution.py:521
  28.5 1.4 %collective-permute-done.9.refs_2_ = f32[8,8,128]{2,1,0:T(8,128)S(1)} collective-permute-done((f32[8,8,128]{2,1,0:T(8,128)S(1)}, f32[8,8,128]{2,1,0:T(8,128)S(1)}, u32[]{:S(2)}, u32[]{:S(2)}) %collective-permute-start.9) | collective-permute-done | bytes 32800 | tf_op jit(solution)/shard_map/ppermute | solution.py:355
  29.9 0.1 collective-permute-start.11
  30.0 1.0 %finish.1 = (f32[1,1,8,3,32,1024]{5,4,3,2,1,0:T(8,128)}, f32[6,8,8,128]{3,2,1,0:T(8,128)S(1)}) custom-call(f32[4,8,8,128]{3,2,1,0:T(8,128)S(1)} %join.1.before.near, f32[3,3,32,1024]{3,2,1,0:T(8,128)S(1)} %get-tuple-element.50.block, f32[6,2,8,128]{3,2,1,0:T(8,128)S(1)} %get-tuple-element.37.before.refs_0_, ...), custom_call_target="tpu_custom_call", output_to_operand_aliasing={{0}: (5, {})} | custom-call | flops 1024 | bytes 1048576 | tf_op jit(solution)/shard_map/finish/pallas_call | solution.py:614
  31.1 0.3 collective-permute-done.11.far
  31.4 2.3 %heavy_tiles.1 = (f32[1,1,8,3,32,1024]{5,4,3,2,1,0:T(8,128)}, f32[1,1,6,8,1024]{4,3,2,1,0:T(8,128)}) custom-call(s32[1,8]{1,0:T(1,128)S(1)} %get-tuple-element.30.helper, f32[1,1,8,3,32,1024]{5,4,3,2,1,0:T(8,128)S(1)} %copy-done, bf16[1,1,8,2,3,32,1024]{6,5,4,3,2,1,0:T(8,128)(2,1)S(1)} %copy-done.1, ...), custom_call_target="tpu_custom_call", output_to_operand_aliasing={{0}: (7, {})} | custom-call | flops 8388608 | bytes 4194304 | tf_op jit(solution)/shard_map/heavy_tiles/pallas_call | solution.py:691
  (16 shorter events, 0.1 us)
Async XLA Ops:
  1.6 9.4 %collective-permute-start = (f32[3,8,128]{2,1,0:T(8,128)S(1)}, f32[3,8,128]{2,1,0:T(8,128)S(1)}, u32[]{:S(2)}, u32[]{:S(2)}) collective-permute-start(f32[3,8,128]{2,1,0:T(8,128)S(1)} %get-tuple-element.31), channel_id=1, source_target_pairs={{0,7},{1,2},{2,1},{3,4},{4,3},{5,6},{6,5},{7,0},{8,15},{9,10},{10,... | collective-permute-start | bytes 36872 | tf_op jit(solution)/shard_map/ppermute | solution.py:187
  5.0 6.0 %collective-permute-start.1 = (f32[3,8,128]{2,1,0:T(8,128)S(1)}, f32[3,8,128]{2,1,0:T(8,128)S(1)}, u32[]{:S(2)}, u32[]{:S(2)}) collective-permute-start(f32[3,8,128]{2,1,0:T(8,128)S(1)} %get-tuple-element.32), channel_id=1, source_target_pairs={{0,24},{8,16},{16,8},{24,0},{1,25},{9,17},{17,9},{25,1},{2,26},{10... | collective-permute-start | bytes 36872 | tf_op jit(solution)/shard_map/ppermute | solution.py:187
  8.6 3.7 %collective-permute-start.2 = (f32[3,8,128]{2,1,0:T(8,128)S(1)}, f32[3,8,128]{2,1,0:T(8,128)S(1)}, u32[]{:S(2)}, u32[]{:S(2)}) collective-permute-start(f32[3,8,128]{2,1,0:T(8,128)S(1)} %get-tuple-element.33), channel_id=1, source_target_pairs={{0,8},{8,0},{16,24},{24,16},{1,9},{9,1},{17,25},{25,17},{2,10},{10... | collective-permute-start | bytes 36872 | tf_op jit(solution)/shard_map/ppermute | solution.py:182
  8.6 3.7 %collective-permute-start.3 = (f32[3,8,128]{2,1,0:T(8,128)S(1)}, f32[3,8,128]{2,1,0:T(8,128)S(1)}, u32[]{:S(2)}, u32[]{:S(2)}) collective-permute-start(f32[3,8,128]{2,1,0:T(8,128)S(1)} %get-tuple-element.34), channel_id=1, source_target_pairs={{0,1},{1,0},{2,3},{3,2},{4,5},{5,4},{6,7},{7,6},{8,9},{9,8},{10,11... | collective-permute-start | bytes 36872 | tf_op jit(solution)/shard_map/ppermute | solution.py:182
  8.6 3.7 %copy-start.4 = (f32[3,8,8,128]{3,2,1,0:T(8,128)S(1)}, f32[3,8,8,128]{3,2,1,0:T(8,128)}, u32[]{:S(2)}) copy-start(f32[3,8,8,128]{3,2,1,0:T(8,128)} %velocity.3) | copy-start | bytes 294916
  8.6 3.7 %copy-start.5 = (s32[8,8,128]{2,1,0:T(8,128)S(1)}, s32[8,8,128]{2,1,0:T(8,128)}, u32[]{:S(2)}) copy-start(s32[8,8,128]{2,1,0:T(8,128)} %wall.1) | copy-start | bytes 98308
  8.6 4.5 %copy-start = (f32[1,1,8,3,32,1024]{5,4,3,2,1,0:T(8,128)S(1)}, f32[1,1,8,3,32,1024]{5,4,3,2,1,0:T(8,128)}, u32[]{:S(2)}) copy-start(f32[1,1,8,3,32,1024]{5,4,3,2,1,0:T(8,128)} %base.7) | copy-start | bytes 9437188
  8.6 4.5 %copy-start.1 = (bf16[1,1,8,2,3,32,1024]{6,5,4,3,2,1,0:T(8,128)(2,1)S(1)}, bf16[1,1,8,2,3,32,1024]{6,5,4,3,2,1,0:T(8,128)(2,1)}, u32[]{:S(2)}) copy-start(bf16[1,1,8,2,3,32,1024]{6,5,4,3,2,1,0:T(8,128)(2,1)} %noise.7) | copy-start | bytes 9437188
  13.1 1.5 %collective-permute-start.4 = (f32[4,12,8,128]{3,2,1,0:T(8,128)S(1)}, f32[4,12,8,128]{3,2,1,0:T(8,128)S(1)}, u32[]{:S(2)}, u32[]{:S(2)}) collective-permute-start(f32[4,12,8,128]{3,2,1,0:T(8,128)S(1)} %get-tuple-element.36.refs_0_), channel_id=1, source_target_pairs={{0,1},{1,0},{2,3},{3,2},{4,5},{5,4},{6,7},{7,6},{8,9},{9,8},{10,11... | collective-permute-start | bytes 589832 | tf_op jit(solution)/shard_map/ppermute | solution.py:355
  13.2 5.0 %copy-start.2 = (f32[1,1,3,224,1024]{4,3,2,1,0:T(8,128)S(1)}, f32[1,1,3,224,1024]{4,3,2,1,0:T(8,128)}, u32[]{:S(2)}) copy-start(f32[1,1,3,224,1024]{4,3,2,1,0:T(8,128)} %base.6) | copy-start | bytes 8257540
  13.2 5.0 %copy-start.3 = (bf16[1,1,2,3,224,1024]{5,4,3,2,1,0:T(8,128)(2,1)S(1)}, bf16[1,1,2,3,224,1024]{5,4,3,2,1,0:T(8,128)(2,1)}, u32[]{:S(2)}) copy-start(bf16[1,1,2,3,224,1024]{5,4,3,2,1,0:T(8,128)(2,1)} %noise.6) | copy-start | bytes 8257540
  14.6 6.1 %collective-permute-start.5 = (f32[12,8,128]{2,1,0:T(8,128)S(1)}, f32[12,8,128]{2,1,0:T(8,128)S(1)}, u32[]{:S(2)}, u32[]{:S(2)}) collective-permute-start(f32[12,8,128]{2,1,0:T(8,128)S(1)} %get-tuple-element.43), channel_id=1, source_target_pairs={{0,6},{1,7},{2,4},{3,5},{4,2},{5,3},{6,0},{7,1},{8,14},{9,15},{10,... | collective-permute-start | bytes 147464 | tf_op jit(solution)/shard_map/ppermute | solution.py:355
  15.2 5.5 %collective-permute-start.6 = (f32[12,8,128]{2,1,0:T(8,128)S(1)}, f32[12,8,128]{2,1,0:T(8,128)S(1)}, u32[]{:S(2)}, u32[]{:S(2)}) collective-permute-start(f32[12,8,128]{2,1,0:T(8,128)S(1)} %get-tuple-element.39.before), channel_id=1, source_target_pairs={{0,2},{1,3},{2,0},{3,1},{4,6},{5,7},{6,4},{7,5},{8,10},{9,11},{10,... | collective-permute-start | bytes 147464 | tf_op jit(solution)/shard_map/ppermute | solution.py:355
  16.5 4.2 %collective-permute-start.7 = (f32[12,8,128]{2,1,0:T(8,128)S(1)}, f32[12,8,128]{2,1,0:T(8,128)S(1)}, u32[]{:S(2)}, u32[]{:S(2)}) collective-permute-start(f32[12,8,128]{2,1,0:T(8,128)S(1)} %get-tuple-element.44), channel_id=1, source_target_pairs={{0,4},{1,5},{2,6},{3,7},{4,0},{5,1},{6,2},{7,3},{8,12},{9,13},{10,... | collective-permute-start | bytes 147464 | tf_op jit(solution)/shard_map/ppermute | solution.py:355
  23.0 5.5 %collective-permute-start.10 = (f32[8,8,128]{2,1,0:T(8,128)S(1)}, f32[8,8,128]{2,1,0:T(8,128)S(1)}, u32[]{:S(2)}, u32[]{:S(2)}) collective-permute-start(f32[8,8,128]{2,1,0:T(8,128)S(1)} %get-tuple-element.45.refs_0_), channel_id=1, source_target_pairs={{0,6},{1,7},{2,4},{3,5},{4,2},{5,3},{6,0},{7,1},{8,14},{9,15},{10,... | collective-permute-start | bytes 98312 | tf_op jit(solution)/shard_map/ppermute | solution.py:355
  24.0 4.5 %collective-permute-start.8 = (f32[8,8,128]{2,1,0:T(8,128)S(1)}, f32[8,8,128]{2,1,0:T(8,128)S(1)}, u32[]{:S(2)}, u32[]{:S(2)}) collective-permute-start(f32[8,8,128]{2,1,0:T(8,128)S(1)} %get-tuple-element.45.refs_0_), channel_id=1, source_target_pairs={{0,2},{1,3},{2,0},{3,1},{4,6},{5,7},{6,4},{7,5},{8,10},{9,11},{10,... | collective-permute-start | bytes 98312 | tf_op jit(solution)/shard_map/ppermute | solution.py:355
  26.0 3.9 %collective-permute-start.9 = (f32[8,8,128]{2,1,0:T(8,128)S(1)}, f32[8,8,128]{2,1,0:T(8,128)S(1)}, u32[]{:S(2)}, u32[]{:S(2)}) collective-permute-start(f32[8,8,128]{2,1,0:T(8,128)S(1)} %get-tuple-element.45.refs_0_), channel_id=1, source_target_pairs={{0,4},{1,5},{2,6},{3,7},{4,0},{5,1},{6,2},{7,3},{8,12},{9,13},{10,... | collective-permute-start | bytes 98312 | tf_op jit(solution)/shard_map/ppermute | solution.py:355
  29.9 1.4 %collective-permute-start.11 = (f32[4,8,8,128]{3,2,1,0:T(8,128)S(1)}, f32[4,8,8,128]{3,2,1,0:T(8,128)S(1)}, u32[]{:S(2)}, u32[]{:S(2)}) collective-permute-start(f32[4,8,8,128]{3,2,1,0:T(8,128)S(1)} %join.1.before.near), channel_id=1, source_target_pairs={{0,1},{1,0},{2,3},{3,2},{4,5},{5,4},{6,7},{7,6},{8,9},{9,8},{10,11... | collective-permute-start | bytes 393224 | tf_op jit(solution)/shard_map/ppermute | solution.py:355

commit v8 on v7

--- a/solution.py
+++ b/solution.py
@@ -182,9 +182,21 @@
     return lax.ppermute(block, axis, [(i, i ^ 1) for i in range(lax.axis_size(axis))])
 
 
-def swap_across(block, axis):
-    size = lax.axis_size(axis)
-    return lax.ppermute(block, axis, [(i, (i - 1 + 2 * (i & 1)) % size) for i in range(size)])
+def swap_across(block, along_rows):
+    rows, columns = lax.axis_size("gx"), lax.axis_size("gy")
+    size = rows if along_rows else columns
+
+    def partner(row, column):
+        place = row if along_rows else column
+        if place in (0, size - 1):
+            row, column = (row, column ^ 1) if along_rows else (row ^ 1, column)
+        else:
+            place += 1 if place & 1 else -1
+            row, column = (place, column) if along_rows else (row, place)
+        return row * columns + column
+
+    places = [(row, column) for row in range(rows) for column in range(columns)]
+    return lax.ppermute(block, ("gx", "gy"), [(i, partner(*place)) for i, place in enumerate(places)])
 
 
 def low_and_high(axis, one, two, a):
@@ -420,7 +432,7 @@
     return [sums[0] + (q[0] * q[0] + q[1] * q[1] + q[2] * q[2])]
 
 
-def ordinary(first, has_block, has_base, has_extra, *refs):
+def ordinary(first, direct, has_block, has_base, has_extra, *refs):
     refs = list(refs)
     before, base, noise, grad = refs[:4]
     del refs[:4]
@@ -428,10 +440,11 @@
     if has_base:
         refs.pop(0)
     extra_near = refs.pop(0) if has_extra else None
-    new_base = refs.pop(0) if has_block else None
+    new_base = refs.pop(0) if has_block or direct else None
     new_extra = refs.pop(0) if has_extra else None
-    fields, stress, halfway, relaxes, sems = refs
-    here, _, count, cells = fields.shape
+    fields, stress, early, halfway, relaxes, sems = refs
+    _, _, count, cells = fields.shape
+    here = direct + fields.shape[0]
     depth = cells // LANES
     inverse = 1.0 / count
     copies = []
@@ -472,8 +485,10 @@
                 def write(a, rows, value):
                     if step == 0:
                         halfway[place, a, rows, lanes] = value
+                    elif place < direct:
+                        early[place, a, rows, lanes] = value
                     else:
-                        fields[place, a, rows, lanes] = value
+                        fields[place - direct, a, rows, lanes] = value
 
                 def shock(_, a, rows):
                     return noise[0, 0, tile, step, a, rows, lanes]
@@ -483,13 +498,16 @@
                 return tile_sums(read, write, shock, [matrix], count, add_moments, 6)
 
             sums = packed_sums(sums_of, depth)
+        if place < direct:
+            copies.append(pltpu.make_async_copy(early.at[place], new_base.at[0, 0, tile], sems.at[len(copies)]))
+            copies[-1].start()
         for i, row in enumerate(stress_rows(sums, inverse)):
             stress[i, place] = row
     for copy in copies:
         copy.wait()
 
 
-def call_ordinary(first, here, before, base_fields, base_noise, grad, block, new_base, new_extra):
+def call_ordinary(first, here, direct, before, base_fields, base_noise, grad, block, new_base, new_extra):
     count, cells = base_fields.shape[-2:]
     depth = cells // LANES
     has_block, has_base, has_extra = block is not None, new_base is not None, new_extra is not None
@@ -500,9 +518,11 @@
     if has_block:
         operands += near_memory(block)
         specs.append(vmem)
+        copies += block.shape[0]
+    if has_block or direct:
+        copies += direct
         shapes.append(jax.ShapeDtypeStruct(base_fields.shape, f32))
         out_specs.append(hbm)
-        copies += block.shape[0]
     if has_base:
         aliases[len(operands)] = 0
         operands.append(new_base)
@@ -514,17 +534,18 @@
         out_specs.append(hbm)
         copies += 3
     shapes += [
-        pltpu.VMEM((here, 3, count, cells), f32),
+        pltpu.VMEM((here - direct, 3, count, cells), f32),
         jax.ShapeDtypeStruct((6, here, depth, LANES), f32),
     ]
     out_specs += [vmem, vmem]
     results = pl.pallas_call(
-        functools.partial(ordinary, first, has_block, has_base, has_extra),
+        functools.partial(ordinary, first, direct, has_block, has_base, has_extra),
         out_shape=tuple(shapes),
         in_specs=specs,
         out_specs=tuple(out_specs),
         input_output_aliases=aliases,
         scratch_shapes=[
+            pltpu.VMEM((max(direct, 1), 3, count, cells), f32),
             pltpu.VMEM((here, 3, count, cells), f32),
             pltpu.VMEM((here, 2, depth, LANES), f32),
             pltpu.SemaphoreType.DMA((max(copies, 1),)),
@@ -535,7 +556,7 @@
     )(*operands)
     results = list(results)
     piece, block = results.pop(), results.pop()
-    new_base = results.pop(0) if has_block else None
+    new_base = results.pop(0) if has_block or direct else None
     return new_base, block, piece, (results[0] if has_extra else None)
 
 
@@ -715,39 +736,30 @@
     tiles = tile_counts.shape[2]
     pairs = lax.axis_size("gy") // 2
     helper_tile, x_one, x_two, y_one, y_two = call_edges(helper_tile, velocity)
-    y_two = swap_across(y_two, "gy")
-    x_two = swap_across(x_two, "gx")
+    y_two = swap_across(y_two, False)
+    x_two = swap_across(x_two, True)
     x_one = swap_within(x_one, "gx")
     y_one = swap_within(y_one, "gy")
     halos = (y_two, x_two, x_one, y_one)
     moments = call_heavy_moments(helper_tile, base_fields, base_noise)
     grad, keep, send = call_gradients(tiles, helper_tile, velocity, halos, wall_cells, moments)
-    gaps = 3
-    new_base, block, pieces, done = None, None, [], 0
-
-    def fill(before, extra_near=None):
-        nonlocal new_base, block, done
-        here = (tiles - done) // (gaps - len(pieces))
-        new_base, block, piece, extra_far = call_ordinary(
-            done, here, before, base_fields, base_noise, grad, block, new_base, extra_near
-        )
-        pieces.append(piece)
-        done += here
-        return piece, extra_far
-
+    some = tiles // 4
+    ordinary_fields = (base_fields, base_noise, grad)
     received = swapped(send, 1)
-    before, _ = fill(send)
+    _, block, begun, _ = call_ordinary(0, some, 0, send, *ordinary_fields, None, None, None)
+    before = begun
     keep, *sends = call_merge(before, keep, received)
     farthest_first = sorted(range(1, pairs), key=lambda flip: -flip.bit_count())
     parts = [keep] + [swapped(sends[flip - 1], 2 * flip) for flip in farthest_first]
     extra_sums = call_extra_moments(sends[0], extra_fields, extra_noise)
-    before, _ = fill(extra_sums)
-    extra_near, reply = call_extra(before, extra_fields, extra_noise, extra_sums, parts)
+    extra_near, reply = call_extra(extra_sums, extra_fields, extra_noise, extra_sums, parts)
     replies = {flip: swapped(reply, 2 * flip) for flip in farthest_first}
-    before, new_extra = fill(reply, extra_near)
-    near = call_join(before, [reply] + [replies[flip] for flip in range(1, pairs)])
+    new_base, block, ended, new_extra = call_ordinary(
+        some, tiles - some, tiles - 2 * some, reply, *ordinary_fields, block, None, extra_near
+    )
+    near = call_join(ended, [reply] + [replies[flip] for flip in range(1, pairs)])
     far = swapped(near, 1)
-    new_base, ready = call_finish(near, block, pieces, new_base)
+    new_base, ready = call_finish(near, block, (begun, ended), new_base)
     new_base, stress = call_heavy(helper_tile, base_fields, base_noise, grad, near, far, ready, new_base)
     return new_base, new_extra, jnp.swapaxes(stress, 2, 3)
 

time: 33.3 us -> 30.2 us (0.907); the launches traced: 33.7 us -> 29.9 us
  Pallas kernels: 14.9 us -> 12.3 us
  waiting for transfers between devices: 3.61 us -> 2.68 us
  starting transfers between devices: 14.3 us -> 13.5 us
  local copies, waits for them, and re-layouts: 0.04 us -> 0.62 us
    ppermute x2, starting transfers between devices: 7 us -> 3.12 us  [swap_across(): lax.ppermute(block, ('gx', 'gy'), [(i, partner(*place)) for i, place in e...]
    ppermute x2, starting transfers between devices: 0.01 us -> 3.13 us  [swap_within(): lax.ppermute(block, axis, [(i, i ^ 1) for i in range(lax.axis_size(axis))])]
    ppermute x2, waiting for transfers between devices: 1.31 us -> 0.01 us  [swap_within(): lax.ppermute(block, axis, [(i, i ^ 1) for i in range(lax.axis_size(axis))])]
    pallas_call x1, Pallas kernels: 2.31 us -> 1.36 us  [call_heavy(): pl.pallas_call(heavy, out_shape=(jax.ShapeDtypeStruct(new_base.shape, f32...]
    pallas_call x3 -> x2, Pallas kernels: 3.87 us -> 3.1 us  [call_ordinary(): pl.pallas_call(functools.partial(ordinary, first, direct, has_block, has_...]
    pallas_call x1, Pallas kernels: 2.31 us -> 1.65 us  [call_heavy_moments(): pl.pallas_call(heavy_moments, out_shape=jax.ShapeDtypeStruct((slots, 16,...]
    unnamed x12, local copies, waits for them, and re-layouts: 0.04 us -> 0.62 us
    ppermute x8, waiting for transfers between devices: 2.3 us -> 2.67 us  [swapped(): return lax.ppermute(block, 'gy', [(i, i ^ flip) for i in range(size)])]
  transfers between devices with their start and end apart: 12 -> 12, of which waited for: 4 -> 6; matrix products, arithmetic and copies ran while one was open for 0% -> 0% of each run, Pallas kernels for 26% -> 24%
where the time goes in v8:
time: 30.2 us; the launch traced here: 29.9 us
  starting transfers between devices  13.5 us (45%)
  Pallas kernels  12.3 us (41%)
  waiting for transfers between devices  2.68 us (9%)
  between operations  0.81 us (3%)
  local copies, waits for them, and re-layouts  0.62 us (2%)
    ppermute x8, starting transfers between devices, swapped(): return lax.ppermute(block, 'gy', [(i, i ^ flip) for i in range(size)])  7.25 us
    ppermute x2, starting transfers between devices, swap_within(): lax.ppermute(block, axis, [(i, i ^ 1) for i in range(lax.axis_size(axis))])  3.13 us
    ppermute x2, starting transfers between devices, swap_across(): lax.ppermute(block, ('gx', 'gy'), [(i, partner(*place)) for i, place in e...  3.12 us
    pallas_call x2, Pallas kernels, call_ordinary(): pl.pallas_call(functools.partial(ordinary, first, direct, has_block, has_...  3.1 us
    ppermute x8, waiting for transfers between devices, swapped(): return lax.ppermute(block, 'gy', [(i, i ^ flip) for i in range(size)])  2.67 us
    pallas_call x1, Pallas kernels, call_extra(): pl.pallas_call(functools.partial(extra, 7), out_shape=(pltpu.VMEM(extra_f...  2.25 us
    pallas_call x1, Pallas kernels, call_heavy_moments(): pl.pallas_call(heavy_moments, out_shape=jax.ShapeDtypeStruct((slots, 16,...  1.65 us
    pallas_call x1, Pallas kernels, call_extra_moments(): pl.pallas_call(functools.partial(extra_moments, 7), out_shape=jax.ShapeDt...  1.41 us
  transfers between devices with their start and end apart: 12, of which 6 were waited for; matrix products, arithmetic and copies ran while one was open for 0% of the time, Pallas kernels for 24%

profile of v8, /device:TPU:0, one launch (start us, length us, event | category | flops | bytes accessed | tf_op | source)
XLA Modules:
  0.0 29.9 jit_solution(10200166238905169586)
XLA Ops:
  0.6 0.9 %edges.1 = (s32[1,8]{1,0:T(1,128)S(1)}, f32[3,8,128]{2,1,0:T(8,128)S(1)}, f32[3,8,128]{2,1,0:T(8,128)S(1)}, f32[3,8,128]{2,1,0:T(8,128)S(1)}, f32[3,8,128]{2,1,0:T(8,128)S(1)}) custom-call(s32[1,8]{1,0:T(1,128)} %helper.1, f32[3,8,8,128]{3,2,1,0:T(8,128)} %velocity.3), custom_call_target="tpu_custom_call" | custom-call | flops 1024 | bytes 131072 | tf_op jit(solution)/shard_map/edges/pallas_call | solution.py:170
  1.6 3.1 %collective-permute-start = (f32[3,8,128]{2,1,0:T(8,128)S(1)}, f32[3,8,128]{2,1,0:T(8,128)S(1)}, u32[]{:S(2)}, u32[]{:S(2)}) collective-permute-start(f32[3,8,128]{2,1,0:T(8,128)S(1)} %get-tuple-element.28), channel_id=1, source_target_pairs={{0,8},{1,2},{2,1},{3,4},{4,3},{5,6},{6,5},{7,15},{8,0},{9,10},{10,... | collective-permute-start | bytes 36872 | tf_op jit(solution)/shard_map/ppermute | solution.py:199
  4.7 0.0 collective-permute-start.1
  4.7 3.1 %collective-permute-start.2 = (f32[3,8,128]{2,1,0:T(8,128)S(1)}, f32[3,8,128]{2,1,0:T(8,128)S(1)}, u32[]{:S(2)}, u32[]{:S(2)}) collective-permute-start(f32[3,8,128]{2,1,0:T(8,128)S(1)} %get-tuple-element.30), channel_id=1, source_target_pairs={{0,8},{8,0},{16,24},{24,16},{1,9},{9,1},{17,25},{25,17},{2,10},{10... | collective-permute-start | bytes 36872 | tf_op jit(solution)/shard_map/ppermute | solution.py:182
  7.8 0.0 collective-permute-start.3
  7.8 0.0 copy-start.1
  7.8 1.6 %heavy_moments.1.moments = f32[8,16,8,128]{3,2,1,0:T(8,128)S(1)} custom-call(s32[1,8]{1,0:T(1,128)S(1)} %get-tuple-element.27.helper, f32[1,1,8,3,32,1024]{5,4,3,2,1,0:T(8,128)} %base.7, bf16[1,1,8,2,3,32,1024]{6,5,4,3,2,1,0:T(8,128)(2,1)} %noise.7), custom_call_target="tpu_custom_call" | custom-call | flops 8388608 | bytes 3145728 | tf_op jit(solution)/shard_map/heavy_moments/pallas_call | solution.py:252
  9.5 0.0 collective-permute-done.y_two
  9.5 0.0 collective-permute-done.1.x_two
  9.5 0.0 collective-permute-done.2.x_one
  9.6 0.7 %gradients.1 = (f32[576,128]{1,0:T(8,128)S(1)}, f32[4,12,8,128]{3,2,1,0:T(8,128)S(1)}, f32[4,12,8,128]{3,2,1,0:T(8,128)S(1)}) custom-call(s32[1,8]{1,0:T(1,128)S(1)} %get-tuple-element.27.helper, f32[3,8,8,128]{3,2,1,0:T(8,128)S(1)} %copy-done.4, f32[3,8,128]{2,1,0:T(8,128)S(1)} %collective-permute-done.y_two, ...), custom_call_target="tpu_custom_call" | custom-call | flops 4194304 | bytes 1048576 | tf_op jit(solution)/shard_map/gradients/pallas_call | solution.py:354
  10.3 0.1 collective-permute-start.4
  10.3 0.6 %copy-done.1 = bf16[1,1,8,2,3,32,1024]{6,5,4,3,2,1,0:T(8,128)(2,1)S(1)} copy-done((bf16[1,1,8,2,3,32,1024]{6,5,4,3,2,1,0:T(8,128)(2,1)S(1)}, bf16[1,1,8,2,3,32,1024]{6,5,4,3,2,1,0:T(8,128)(2,1)}, u32[]{:S(2)}) %copy-start.1) | copy-done | bytes 3145752
  10.9 0.7 %ordinary_tiles.2 = (f32[2,3,32,1024]{3,2,1,0:T(8,128)S(1)}, f32[6,2,8,128]{3,2,1,0:T(8,128)S(1)}) custom-call(f32[4,12,8,128]{3,2,1,0:T(8,128)S(1)} %get-tuple-element.33.refs_0_, f32[1,1,8,3,32,1024]{5,4,3,2,1,0:T(8,128)S(1)} %copy-done, bf16[1,1,8,2,3,32,1024]{6,5,4,3,2,1,0:T(8,128)(2,1)S(1)} %copy-done.1, f32[576,128]{1,0:T(8,128)S(1)} %get-tuple-element.32.refs_3_.grad), custom_call_target="tpu_custom_call" | custom-call | flops 8388608 | bytes 3145728 | tf_op jit(solution)/shard_map/ordinary_tiles/pallas_call | solution.py:541
  11.7 0.1 collective-permute-done.4.received
  11.8 1.9 %collective-permute-start.5 = (f32[12,8,128]{2,1,0:T(8,128)S(1)}, f32[12,8,128]{2,1,0:T(8,128)S(1)}, u32[]{:S(2)}, u32[]{:S(2)}) collective-permute-start(f32[12,8,128]{2,1,0:T(8,128)S(1)} %get-tuple-element.38), channel_id=1, source_target_pairs={{0,6},{1,7},{2,4},{3,5},{4,2},{5,3},{6,0},{7,1},{8,14},{9,15},{10,... | collective-permute-start | bytes 147464 | tf_op jit(solution)/shard_map/ppermute | solution.py:367
  13.7 0.6 %collective-permute-start.6 = (f32[12,8,128]{2,1,0:T(8,128)S(1)}, f32[12,8,128]{2,1,0:T(8,128)S(1)}, u32[]{:S(2)}, u32[]{:S(2)}) collective-permute-start(f32[12,8,128]{2,1,0:T(8,128)S(1)} %get-tuple-element.36.before), channel_id=1, source_target_pairs={{0,2},{1,3},{2,0},{3,1},{4,6},{5,7},{6,4},{7,5},{8,10},{9,11},{10,... | collective-permute-start | bytes 147464 | tf_op jit(solution)/shard_map/ppermute | solution.py:367
  14.3 1.0 %collective-permute-start.7 = (f32[12,8,128]{2,1,0:T(8,128)S(1)}, f32[12,8,128]{2,1,0:T(8,128)S(1)}, u32[]{:S(2)}, u32[]{:S(2)}) collective-permute-start(f32[12,8,128]{2,1,0:T(8,128)S(1)} %get-tuple-element.39), channel_id=1, source_target_pairs={{0,4},{1,5},{2,6},{3,7},{4,0},{5,1},{6,2},{7,3},{8,12},{9,13},{10,... | collective-permute-start | bytes 147464 | tf_op jit(solution)/shard_map/ppermute | solution.py:367
  15.3 1.4 %extra_moments.1.before.moments = f32[16,8,128]{2,1,0:T(8,128)S(1)} custom-call(f32[12,8,128]{2,1,0:T(8,128)S(1)} %get-tuple-element.36.before, f32[1,1,3,224,1024]{4,3,2,1,0:T(8,128)S(1)} %copy-done.2, bf16[1,1,2,3,224,1024]{5,4,3,2,1,0:T(8,128)(2,1)S(1)} %copy-done.3), custom_call_target="tpu_custom_call" | custom-call | flops 8388608 | bytes 5242880 | tf_op jit(solution)/shard_map/extra_moments/pallas_call | solution.py:290
  16.8 0.5 %collective-permute-done.5.refs_1_ = f32[12,8,128]{2,1,0:T(8,128)S(1)} collective-permute-done((f32[12,8,128]{2,1,0:T(8,128)S(1)}, f32[12,8,128]{2,1,0:T(8,128)S(1)}, u32[]{:S(2)}, u32[]{:S(2)}) %collective-permute-start.5) | collective-permute-done | bytes 49184 | tf_op jit(solution)/shard_map/ppermute | solution.py:367
  17.3 0.5 %collective-permute-done.6.refs_2_ = f32[12,8,128]{2,1,0:T(8,128)S(1)} collective-permute-done((f32[12,8,128]{2,1,0:T(8,128)S(1)}, f32[12,8,128]{2,1,0:T(8,128)S(1)}, u32[]{:S(2)}, u32[]{:S(2)}) %collective-permute-start.6) | collective-permute-done | bytes 49184 | tf_op jit(solution)/shard_map/ppermute | solution.py:367
  17.8 0.6 %collective-permute-done.7.refs_3_ = f32[12,8,128]{2,1,0:T(8,128)S(1)} collective-permute-done((f32[12,8,128]{2,1,0:T(8,128)S(1)}, f32[12,8,128]{2,1,0:T(8,128)S(1)}, u32[]{:S(2)}, u32[]{:S(2)}) %collective-permute-start.7) | collective-permute-done | bytes 49184 | tf_op jit(solution)/shard_map/ppermute | solution.py:367
  18.4 2.2 %extra_fields.1 = (f32[1,1,3,224,1024]{4,3,2,1,0:T(8,128)S(1)}, f32[8,8,128]{2,1,0:T(8,128)S(1)}) custom-call(f32[16,8,128]{2,1,0:T(8,128)S(1)} %extra_moments.1.before.moments, f32[1,1,3,224,1024]{4,3,2,1,0:T(8,128)S(1)} %copy-done.2, bf16[1,1,2,3,224,1024]{5,4,3,2,1,0:T(8,128)(2,1)S(1)} %copy-done.3, f32[16,8,128]{2,1,0:T(8,128)S(1)} %extra_moments.1.before.moments, ...), custom_call_target="tpu_custom_call" | custom-call | flops 33554432 | bytes 9437184 | tf_op jit(solution)/shard_map/extra_fields/pallas_call | solution.py:600
  20.6 1.5 %collective-permute-start.10 = (f32[8,8,128]{2,1,0:T(8,128)S(1)}, f32[8,8,128]{2,1,0:T(8,128)S(1)}, u32[]{:S(2)}, u32[]{:S(2)}) collective-permute-start(f32[8,8,128]{2,1,0:T(8,128)S(1)} %get-tuple-element.40.refs_0_), channel_id=1, source_target_pairs={{0,6},{1,7},{2,4},{3,5},{4,2},{5,3},{6,0},{7,1},{8,14},{9,15},{10,... | collective-permute-start | bytes 98312 | tf_op jit(solution)/shard_map/ppermute | solution.py:367
  22.1 1.1 %collective-permute-start.8 = (f32[8,8,128]{2,1,0:T(8,128)S(1)}, f32[8,8,128]{2,1,0:T(8,128)S(1)}, u32[]{:S(2)}, u32[]{:S(2)}) collective-permute-start(f32[8,8,128]{2,1,0:T(8,128)S(1)} %get-tuple-element.40.refs_0_), channel_id=1, source_target_pairs={{0,2},{1,3},{2,0},{3,1},{4,6},{5,7},{6,4},{7,5},{8,10},{9,11},{10,... | collective-permute-start | bytes 98312 | tf_op jit(solution)/shard_map/ppermute | solution.py:367
  23.2 1.0 %collective-permute-start.9 = (f32[8,8,128]{2,1,0:T(8,128)S(1)}, f32[8,8,128]{2,1,0:T(8,128)S(1)}, u32[]{:S(2)}, u32[]{:S(2)}) collective-permute-start(f32[8,8,128]{2,1,0:T(8,128)S(1)} %get-tuple-element.40.refs_0_), channel_id=1, source_target_pairs={{0,4},{1,5},{2,6},{3,7},{4,0},{5,1},{6,2},{7,3},{8,12},{9,13},{10,... | collective-permute-start | bytes 98312 | tf_op jit(solution)/shard_map/ppermute | solution.py:367
  24.2 2.4 %ordinary_tiles.3 = (f32[1,1,8,3,32,1024]{5,4,3,2,1,0:T(8,128)}, f32[1,1,3,224,1024]{4,3,2,1,0:T(8,128)}, f32[2,3,32,1024]{3,2,1,0:T(8,128)S(1)}, f32[6,6,8,128]{3,2,1,0:T(8,128)S(1)}) custom-call(f32[8,8,128]{2,1,0:T(8,128)S(1)} %get-tuple-element.40.refs_0_, f32[1,1,8,3,32,1024]{5,4,3,2,1,0:T(8,128)S(1)} %copy-done, ...), custom_call_target="tpu_custom_call" | custom-call | flops 8388608 | bytes 3145728 | tf_op jit(solution)/shard_map/ordinary_tiles/pallas_call | solution.py:541
  26.6 0.5 %collective-permute-done.9.refs_2_ = f32[8,8,128]{2,1,0:T(8,128)S(1)} collective-permute-done((f32[8,8,128]{2,1,0:T(8,128)S(1)}, f32[8,8,128]{2,1,0:T(8,128)S(1)}, u32[]{:S(2)}, u32[]{:S(2)}) %collective-permute-start.9) | collective-permute-done | bytes 32800 | tf_op jit(solution)/shard_map/ppermute | solution.py:367
  27.1 0.1 collective-permute-start.11
  27.2 0.9 %finish.1 = (f32[1,1,8,3,32,1024]{5,4,3,2,1,0:T(8,128)}, f32[6,8,8,128]{3,2,1,0:T(8,128)S(1)}) custom-call(f32[4,8,8,128]{3,2,1,0:T(8,128)S(1)} %join.1.before.near, f32[2,3,32,1024]{3,2,1,0:T(8,128)S(1)} %get-tuple-element.44.block, f32[6,2,8,128]{3,2,1,0:T(8,128)S(1)} %get-tuple-element.34.before.refs_0_, ...), custom_call_target="tpu_custom_call", output_to_operand_aliasing={{0}: (4, {})} | custom-call | flops 1024 | bytes 1048576 | tf_op jit(solution)/shard_map/finish/pallas_call | solution.py:635
  28.1 0.4 %collective-permute-done.11.far = f32[4,8,8,128]{3,2,1,0:T(8,128)S(1)} collective-permute-done((f32[4,8,8,128]{3,2,1,0:T(8,128)S(1)}, f32[4,8,8,128]{3,2,1,0:T(8,128)S(1)}, u32[]{:S(2)}, u32[]{:S(2)}) %collective-permute-start.11) | collective-permute-done | bytes 131104 | tf_op jit(solution)/shard_map/ppermute | solution.py:367
  28.6 1.4 %heavy_tiles.1 = (f32[1,1,8,3,32,1024]{5,4,3,2,1,0:T(8,128)}, f32[1,1,6,8,1024]{4,3,2,1,0:T(8,128)}) custom-call(s32[1,8]{1,0:T(1,128)S(1)} %get-tuple-element.27.helper, f32[1,1,8,3,32,1024]{5,4,3,2,1,0:T(8,128)S(1)} %copy-done, bf16[1,1,8,2,3,32,1024]{6,5,4,3,2,1,0:T(8,128)(2,1)S(1)} %copy-done.1, ...), custom_call_target="tpu_custom_call", output_to_operand_aliasing={{0}: (7, {})} | custom-call | flops 8388608 | bytes 4194304 | tf_op jit(solution)/shard_map/heavy_tiles/pallas_call | solution.py:712
  (15 shorter events, 0.1 us)
Async XLA Ops:
  1.6 7.9 %collective-permute-start = (f32[3,8,128]{2,1,0:T(8,128)S(1)}, f32[3,8,128]{2,1,0:T(8,128)S(1)}, u32[]{:S(2)}, u32[]{:S(2)}) collective-permute-start(f32[3,8,128]{2,1,0:T(8,128)S(1)} %get-tuple-element.28), channel_id=1, source_target_pairs={{0,8},{1,2},{2,1},{3,4},{4,3},{5,6},{6,5},{7,15},{8,0},{9,10},{10,... | collective-permute-start | bytes 36872 | tf_op jit(solution)/shard_map/ppermute | solution.py:199
  4.7 4.8 %collective-permute-start.1 = (f32[3,8,128]{2,1,0:T(8,128)S(1)}, f32[3,8,128]{2,1,0:T(8,128)S(1)}, u32[]{:S(2)}, u32[]{:S(2)}) collective-permute-start(f32[3,8,128]{2,1,0:T(8,128)S(1)} %get-tuple-element.29), channel_id=1, source_target_pairs={{0,1},{1,0},{2,3},{3,2},{4,5},{5,4},{6,7},{7,6},{8,16},{9,17},{10,... | collective-permute-start | bytes 36872 | tf_op jit(solution)/shard_map/ppermute | solution.py:199
  4.7 4.8 %collective-permute-start.2 = (f32[3,8,128]{2,1,0:T(8,128)S(1)}, f32[3,8,128]{2,1,0:T(8,128)S(1)}, u32[]{:S(2)}, u32[]{:S(2)}) collective-permute-start(f32[3,8,128]{2,1,0:T(8,128)S(1)} %get-tuple-element.30), channel_id=1, source_target_pairs={{0,8},{8,0},{16,24},{24,16},{1,9},{9,1},{17,25},{25,17},{2,10},{10... | collective-permute-start | bytes 36872 | tf_op jit(solution)/shard_map/ppermute | solution.py:182
  7.8 1.7 %collective-permute-start.3 = (f32[3,8,128]{2,1,0:T(8,128)S(1)}, f32[3,8,128]{2,1,0:T(8,128)S(1)}, u32[]{:S(2)}, u32[]{:S(2)}) collective-permute-start(f32[3,8,128]{2,1,0:T(8,128)S(1)} %get-tuple-element.31), channel_id=1, source_target_pairs={{0,1},{1,0},{2,3},{3,2},{4,5},{5,4},{6,7},{7,6},{8,9},{9,8},{10,11... | collective-permute-start | bytes 36872 | tf_op jit(solution)/shard_map/ppermute | solution.py:182
  7.8 1.7 %copy-start.4 = (f32[3,8,8,128]{3,2,1,0:T(8,128)S(1)}, f32[3,8,8,128]{3,2,1,0:T(8,128)}, u32[]{:S(2)}) copy-start(f32[3,8,8,128]{3,2,1,0:T(8,128)} %velocity.3) | copy-start | bytes 294916
  7.8 1.7 %copy-start.5 = (s32[8,8,128]{2,1,0:T(8,128)S(1)}, s32[8,8,128]{2,1,0:T(8,128)}, u32[]{:S(2)}) copy-start(s32[8,8,128]{2,1,0:T(8,128)} %wall.1) | copy-start | bytes 98308
  7.8 2.5 %copy-start = (f32[1,1,8,3,32,1024]{5,4,3,2,1,0:T(8,128)S(1)}, f32[1,1,8,3,32,1024]{5,4,3,2,1,0:T(8,128)}, u32[]{:S(2)}) copy-start(f32[1,1,8,3,32,1024]{5,4,3,2,1,0:T(8,128)} %base.7) | copy-start | bytes 9437188
  7.8 3.1 %copy-start.1 = (bf16[1,1,8,2,3,32,1024]{6,5,4,3,2,1,0:T(8,128)(2,1)S(1)}, bf16[1,1,8,2,3,32,1024]{6,5,4,3,2,1,0:T(8,128)(2,1)}, u32[]{:S(2)}) copy-start(bf16[1,1,8,2,3,32,1024]{6,5,4,3,2,1,0:T(8,128)(2,1)} %noise.7) | copy-start | bytes 9437188
  10.3 1.5 %collective-permute-start.4 = (f32[4,12,8,128]{3,2,1,0:T(8,128)S(1)}, f32[4,12,8,128]{3,2,1,0:T(8,128)S(1)}, u32[]{:S(2)}, u32[]{:S(2)}) collective-permute-start(f32[4,12,8,128]{3,2,1,0:T(8,128)S(1)} %get-tuple-element.33.refs_0_), channel_id=1, source_target_pairs={{0,1},{1,0},{2,3},{3,2},{4,5},{5,4},{6,7},{7,6},{8,9},{9,8},{10,11... | collective-permute-start | bytes 589832 | tf_op jit(solution)/shard_map/ppermute | solution.py:367
  10.9 4.4 %copy-start.2 = (f32[1,1,3,224,1024]{4,3,2,1,0:T(8,128)S(1)}, f32[1,1,3,224,1024]{4,3,2,1,0:T(8,128)}, u32[]{:S(2)}) copy-start(f32[1,1,3,224,1024]{4,3,2,1,0:T(8,128)} %base.6) | copy-start | bytes 8257540
  10.9 4.4 %copy-start.3 = (bf16[1,1,2,3,224,1024]{5,4,3,2,1,0:T(8,128)(2,1)S(1)}, bf16[1,1,2,3,224,1024]{5,4,3,2,1,0:T(8,128)(2,1)}, u32[]{:S(2)}) copy-start(bf16[1,1,2,3,224,1024]{5,4,3,2,1,0:T(8,128)(2,1)} %noise.6) | copy-start | bytes 8257540
  11.8 5.5 %collective-permute-start.5 = (f32[12,8,128]{2,1,0:T(8,128)S(1)}, f32[12,8,128]{2,1,0:T(8,128)S(1)}, u32[]{:S(2)}, u32[]{:S(2)}) collective-permute-start(f32[12,8,128]{2,1,0:T(8,128)S(1)} %get-tuple-element.38), channel_id=1, source_target_pairs={{0,6},{1,7},{2,4},{3,5},{4,2},{5,3},{6,0},{7,1},{8,14},{9,15},{10,... | collective-permute-start | bytes 147464 | tf_op jit(solution)/shard_map/ppermute | solution.py:367
  13.7 4.1 %collective-permute-start.6 = (f32[12,8,128]{2,1,0:T(8,128)S(1)}, f32[12,8,128]{2,1,0:T(8,128)S(1)}, u32[]{:S(2)}, u32[]{:S(2)}) collective-permute-start(f32[12,8,128]{2,1,0:T(8,128)S(1)} %get-tuple-element.36.before), channel_id=1, source_target_pairs={{0,2},{1,3},{2,0},{3,1},{4,6},{5,7},{6,4},{7,5},{8,10},{9,11},{10,... | collective-permute-start | bytes 147464 | tf_op jit(solution)/shard_map/ppermute | solution.py:367
  14.3 4.1 %collective-permute-start.7 = (f32[12,8,128]{2,1,0:T(8,128)S(1)}, f32[12,8,128]{2,1,0:T(8,128)S(1)}, u32[]{:S(2)}, u32[]{:S(2)}) collective-permute-start(f32[12,8,128]{2,1,0:T(8,128)S(1)} %get-tuple-element.39), channel_id=1, source_target_pairs={{0,4},{1,5},{2,6},{3,7},{4,0},{5,1},{6,2},{7,3},{8,12},{9,13},{10,... | collective-permute-start | bytes 147464 | tf_op jit(solution)/shard_map/ppermute | solution.py:367
  20.6 5.9 %collective-permute-start.10 = (f32[8,8,128]{2,1,0:T(8,128)S(1)}, f32[8,8,128]{2,1,0:T(8,128)S(1)}, u32[]{:S(2)}, u32[]{:S(2)}) collective-permute-start(f32[8,8,128]{2,1,0:T(8,128)S(1)} %get-tuple-element.40.refs_0_), channel_id=1, source_target_pairs={{0,6},{1,7},{2,4},{3,5},{4,2},{5,3},{6,0},{7,1},{8,14},{9,15},{10,... | collective-permute-start | bytes 98312 | tf_op jit(solution)/shard_map/ppermute | solution.py:367
  22.1 4.4 %collective-permute-start.8 = (f32[8,8,128]{2,1,0:T(8,128)S(1)}, f32[8,8,128]{2,1,0:T(8,128)S(1)}, u32[]{:S(2)}, u32[]{:S(2)}) collective-permute-start(f32[8,8,128]{2,1,0:T(8,128)S(1)} %get-tuple-element.40.refs_0_), channel_id=1, source_target_pairs={{0,2},{1,3},{2,0},{3,1},{4,6},{5,7},{6,4},{7,5},{8,10},{9,11},{10,... | collective-permute-start | bytes 98312 | tf_op jit(solution)/shard_map/ppermute | solution.py:367
  23.2 3.9 %collective-permute-start.9 = (f32[8,8,128]{2,1,0:T(8,128)S(1)}, f32[8,8,128]{2,1,0:T(8,128)S(1)}, u32[]{:S(2)}, u32[]{:S(2)}) collective-permute-start(f32[8,8,128]{2,1,0:T(8,128)S(1)} %get-tuple-element.40.refs_0_), channel_id=1, source_target_pairs={{0,4},{1,5},{2,6},{3,7},{4,0},{5,1},{6,2},{7,3},{8,12},{9,13},{10,... | collective-permute-start | bytes 98312 | tf_op jit(solution)/shard_map/ppermute | solution.py:367
  27.1 1.4 %collective-permute-start.11 = (f32[4,8,8,128]{3,2,1,0:T(8,128)S(1)}, f32[4,8,8,128]{3,2,1,0:T(8,128)S(1)}, u32[]{:S(2)}, u32[]{:S(2)}) collective-permute-start(f32[4,8,8,128]{3,2,1,0:T(8,128)S(1)} %join.1.before.near), channel_id=1, source_target_pairs={{0,1},{1,0},{2,3},{3,2},{4,5},{5,4},{6,7},{7,6},{8,9},{9,8},{10,11... | collective-permute-start | bytes 393224 | tf_op jit(solution)/shard_map/ppermute | solution.py:367
